TPU v7x, 32 devices: a whole 2x2x4 slice. The times are simulated.
32 devices in a mesh: section: 2 (over x), ctx: 4 (over z), exp: 4 (over y, core).
Axes of the slice: x: 2, y: 2, z: 4, core: 2. Of those that a mesh axis runs over, the one named last changes fastest.
Arguments:
- queries: bfloat16 [2, 256, 2048], P('section', 'ctx', 'exp'), may hold values from -0.8984375 to 0.8984375
- keys_in: bfloat16 [2, 256, 2048], P('section', 'ctx', 'exp'), may hold values from -0.8984375 to 0.8984375
- values: bfloat16 [2, 256, 2048], P('section', 'ctx', 'exp'), may hold values from -6 to 6
- decay_rate: float32 [2, 16, 256], P('section', 'exp', 'ctx'), may hold values from 0 to 1
- out_weight: bfloat16 [2, 2048, 6144], P('section', 'exp'), may hold values from -0.125 to 0.125
- residual: bfloat16 [2, 256, 6144], P('section', ('ctx', 'exp')), may hold values from -6 to 6
- norm_gain: float32 [2, 6144], P('section'), may hold values from 0.5 to 1.5
- router: bfloat16 [2, 6144, 16], P('section'), may hold values from -0.078125 to 0.078125
- expert_ids: int32 [2, 256, 2], P('section', ('ctx', 'exp')), may hold values from 0 to 15, all different within a row; in each aligned block of 16 rows (0 to 15, 16 to 31, ..., all dimensions but the last counted through in order) at most 4 rows name the same one
Outputs:
- expert_rows: bfloat16 [2, 4, 16, 4, 4, 6144], P('section', 'ctx', 'exp')
- expert_gates: bfloat16 [2, 4, 16, 4, 4], P('section', 'ctx', 'exp')
Inputs may be any that keep to these rules, and one draw needn't show every extreme that they name: `expert_ids`: in each device's 16 rows, every row names two different experts, no expert is named more than 4 times, and in some devices' rows an expert is named exactly 4 times.
All inputs are finite; a program needn't handle non-finite values.
Results may differ from a plain program's by a relative error of at most 0.02.
Values may be sent and summed in bfloat16 or wider, within the bound.
No kernel may reach another device: no remote copies, remote signals or barrier semaphores. Data moves between devices by JAX's collectives and lax.ppermute only.
A program may use at most 64 MiB of HBM per device.

v0:
```python
import jax
import jax.numpy as jnp
from jax import lax
from jax.sharding import PartitionSpec as P

HEAD_DIM = 128
HEAD_DEV = 4
EXPERTS = 16
CAP = 4


precise = lax.Precision.HIGHEST
epsilon = 1e-05


def entering(value, axis, join, neutral):
    place = lax.axis_index(axis)
    gathered = jax.tree.map(
        lambda a, kind: lax.all_gather(a.astype(kind), axis), value, (jnp.bfloat16, jnp.bfloat16)
    )
    state = jax.tree.map(lambda a, e: jnp.zeros_like(a) + jnp.asarray(e, a.dtype), value, neutral)

    def one(lap, state):
        return join(
            state,
            jax.tree.map(
                lambda a, own: lax.dynamic_index_in_dim(a, lap, 0, False).astype(own.dtype),
                gathered,
                value,
            ),
        )

    return lax.fori_loop(0, place, one, state)


def from_behind(block, axis, distance):
    devices = range(lax.axis_size(axis))
    route = [((i - distance) % len(devices), i) for i in devices]
    return lax.ppermute(block, axis, route)


def chain_combine(earlier, later_part):
    return (
        earlier[0] + later_part[0],
        jnp.exp(later_part[0])[:, None, None] * earlier[1] + later_part[1],
    )


def on_device(
    queries, keys_in, values, decay_rate, out_weight, residual, norm_gain, router, expert_ids
):
    seq_len = queries.shape[1]
    query_heads = queries[0].reshape(seq_len, HEAD_DEV, HEAD_DIM)
    key_heads = keys_in[0].reshape(seq_len, HEAD_DEV, HEAD_DIM)
    value_heads = values[0].reshape(seq_len, HEAD_DEV, HEAD_DIM)
    cum_log = jnp.cumsum(-decay_rate[0], axis=-1)
    attention_logits = jnp.einsum(
        "bsx,osx->sbo", query_heads, key_heads, preferred_element_type=jnp.float32
    )
    log_gap = cum_log[:, :, None] - cum_log[:, None, :]
    causal = lax.broadcasted_iota(jnp.int32, (seq_len, seq_len), 0) >= lax.broadcasted_iota(
        jnp.int32, (seq_len, seq_len), 1
    )
    weight_matrix = jnp.where(
        causal, attention_logits * jnp.exp(jnp.minimum(log_gap, 0.0)), 0.0
    ).astype(jnp.bfloat16)
    inner_part = jnp.einsum(
        "nsj,jng->sng", weight_matrix, value_heads, preferred_element_type=jnp.float32
    )
    tail_decay = jnp.exp(cum_log[:, -1:] - cum_log)
    keyed_rows = key_heads.astype(jnp.float32) * jnp.transpose(tail_decay)[:, :, None]
    local_state = jnp.einsum(
        "lha,lhb->hab", keyed_rows, value_heads.astype(jnp.float32), precision=precise
    )
    total_log = cum_log[:, -1]
    prefix = entering(
        (total_log, local_state),
        "ctx",
        chain_combine,
        (jnp.zeros_like(total_log), jnp.zeros_like(local_state)),
    )
    carried = prefix[1]
    outside = jnp.exp(jnp.transpose(cum_log))[:, :, None] * jnp.einsum(
        "lhd,hde->lhe", query_heads.astype(jnp.float32), carried, precision=precise
    )
    attended = (inner_part + outside).astype(jnp.bfloat16).reshape(seq_len, HEAD_DEV * HEAD_DIM)
    projection = out_weight[0]
    my_share = lax.psum_scatter(
        jnp.dot(attended, projection, preferred_element_type=jnp.float32).astype(jnp.bfloat16),
        "exp",
        scatter_dimension=0,
        tiled=True,
    ).astype(jnp.float32)
    hidden = (residual[0].astype(jnp.float32) + my_share).astype(jnp.bfloat16)
    received = from_behind(hidden, "section", 1)
    wide = received.astype(jnp.float32)
    mean_sq = jnp.mean(wide * wide, axis=-1, keepdims=True)
    normed = (wide * lax.rsqrt(mean_sq + epsilon) * norm_gain[0][None, :]).astype(jnp.bfloat16)
    logits = jnp.dot(normed, router[0], preferred_element_type=jnp.float32)
    route_ids = expert_ids[0]
    expert_table = lax.broadcasted_iota(jnp.int32, (1, 1, EXPERTS), 2)
    picked = jnp.sum(
        jnp.where(route_ids[:, :, None] == expert_table, logits[:, None, :], 0.0), axis=-1
    )
    first_gate = jax.nn.sigmoid(picked[:, 0] - picked[:, 1])
    gate_pair = jnp.stack([first_gate, 1.0 - first_gate], axis=-1).astype(jnp.bfloat16)
    flat_ids = route_ids.reshape(-1)
    onehot = (flat_ids[:, None] == expert_table[0]).astype(jnp.int32)
    slot_rank = jnp.sum((jnp.cumsum(onehot, axis=0) - onehot) * onehot, axis=-1)
    exp_count = lax.axis_size("exp")
    per_owner = EXPERTS // exp_count
    target = flat_ids % per_owner * (exp_count * CAP) + flat_ids // per_owner * CAP + slot_rank
    slots_all = EXPERTS * CAP
    placement = (target[None, :] == lax.broadcasted_iota(jnp.int32, (slots_all, 1), 0)).astype(
        jnp.bfloat16
    )
    doubled = jnp.repeat(normed, 2, axis=0)
    send_rows = jnp.dot(placement, doubled, preferred_element_type=jnp.float32).astype(jnp.bfloat16)
    send_rows = send_rows.reshape(per_owner, exp_count, CAP, normed.shape[1])
    send_gates = jnp.dot(
        placement, gate_pair.reshape(-1), preferred_element_type=jnp.float32
    ).astype(jnp.bfloat16)
    send_gates = send_gates.reshape(per_owner, exp_count, CAP)
    owner_rows, owner_gates = (
        lax.all_to_all(send_rows, "exp", split_axis=1, concat_axis=1, tiled=True),
        lax.all_to_all(send_gates, "exp", split_axis=1, concat_axis=1, tiled=True),
    )
    return (owner_rows[None, None], owner_gates[None, None])


def solution(mesh):
    placed = (
        P("section", "ctx", "exp"),
        P("section", "ctx", "exp"),
        P("section", "ctx", "exp"),
        P("section", "exp", "ctx"),
        P("section", "exp", None),
        P("section", ("ctx", "exp"), None),
        P("section", None),
        P("section", None, None),
        P("section", ("ctx", "exp"), None),
    )
    return jax.shard_map(
        on_device,
        mesh=mesh,
        in_specs=placed,
        out_specs=(
            P("section", "ctx", "exp", None, None, None),
            P("section", "ctx", "exp", None, None),
        ),
        check_vma=False,
    )
```

profile of v0, /device:TPU:0, one launch (start us, length us, event | category | flops | bytes accessed | tf_op | source)
XLA Modules:
  0.0 109.4 jit_solution(2191618030032967499)
XLA Ops:
  7.2 0.0 reduce-scatter.2.cloned.1.call-start
  7.2 0.7 negate_bitcast_fusion
  7.9 0.2 reduce_window_sum.23
  8.2 0.2 fusion.37
  8.4 0.2 slice_reduce_fusion
  8.6 1.2 %dynamic-slice = u32[1]{0:T(128)} dynamic-slice(u32[32]{0:T(128)} %constant.82, u32[]{:T(128)S(6)} %add.73), dynamic_slice_sizes={1} | dynamic-slice | bytes 12
  10.5 0.2 dynamic-update-slice
  10.7 13.4 %all-reduce = bf16[16]{0:T(256)(128)(2,1)S(1)} all-reduce(bf16[16]{0:T(256)(128)(2,1)S(1)} %dynamic-update-slice), channel_id=2, replica_groups=mesh['section'=2,'ctx'=4,'exp'=4] {'ctx'}, use_global_device_ids=true, to_apply=%add | all-reduce | flops 16 | bytes 64
  24.2 0.1 reshape.118
  24.3 0.1 exponential_bitcast_fusion.2
  24.3 0.9 reshape_squeeze.13
  25.2 0.9 reshape_squeeze.14
  26.1 0.9 reshape_squeeze.15
  26.9 0.5 convolution_convert_fusion.2
  27.4 14.8 %all-gather.1 = bf16[16,128,128]{2,1,0:T(8,128)(2,1)S(1)} all-gather(bf16[4,128,128]{2,1,0:T(8,128)(2,1)S(1)} %convolution_convert_fusion.2), channel_id=3, replica_groups=mesh['section'=2,'ctx'=4,'exp'=4] {'ctx'}, dimensions={0}, use_global_device_ids=true | all-gather | bytes 655360 | tf_op jit(solution)/shard_map/all_gather | solution.py:19
  42.2 0.2 fusion.3
  42.5 0.3 fusion.6
  42.8 4.9 %convolution_convert_fusion.1 = bf16[64,6144]{1,0:T(8,128)(2,1)} fusion(bf16[1,512,6144]{2,1,0:T(8,128)(2,1)} %param.15, bf16[4,8,8,128]{3,2,1,0:T(8,128)(2,1)S(1)} %fusion.6), kind=kOutput, calls=%fused_computation.3 | convolution fusion | flops 403046400 | bytes 7143424 | tf_op jit(solution)/shard_map/dot_general | solution.py:89
  47.7 0.0 reduce-scatter.2.cloned.1.call-update
  47.7 0.1 copy.38
  47.8 0.1 reshape_squeeze.12
  47.9 0.1 fusion.36
  48.0 0.1 reduce_window_sum.22
  48.0 0.2 select_reduce_fusion.1
  48.2 21.6 %reduce-scatter.2.cloned.1.call-done = bf16[16,6144]{1,0:T(8,128)(2,1)} async-done(((bf16[64,6144]{1,0:T(8,128)(2,1)}), bf16[16,6144]{1,0:T(8,128)(2,1)}) %reduce-scatter.2.cloned.1.call-update) | async-done | bytes 196624 | tf_op jit(solution)/shard_map/reduce_scatter | solution.py:88
  69.8 1.0 fusion.11
  70.8 1.5 %collective-permute-start = (bf16[16,6144]{1,0:T(8,128)(2,1)S(1)}, bf16[16,6144]{1,0:T(8,128)(2,1)S(1)}, u32[]{:S(2)}, u32[]{:S(2)}) collective-permute-start(bf16[16,6144]{1,0:T(8,128)(2,1)S(1)} %fusion.11), channel_id=1, source_target_pairs={{16,0},{0,16},{17,1},{1,17},{18,2},{2,18},{19,3},{3,19},{20,4},{4,... | collective-permute-start | bytes 589832 | tf_op jit(solution)/shard_map/ppermute | solution.py:39
  72.3 5.2 %collective-permute-done = bf16[16,6144]{1,0:T(8,128)(2,1)S(1)} collective-permute-done((bf16[16,6144]{1,0:T(8,128)(2,1)S(1)}, bf16[16,6144]{1,0:T(8,128)(2,1)S(1)}, u32[]{:S(2)}, u32[]{:S(2)}) %collective-permute-start) | collective-permute-done | bytes 196640 | tf_op jit(solution)/shard_map/ppermute | solution.py:39
  77.5 0.2 fusion.8
  77.7 0.1 fusion.10
  77.8 0.2 fusion.12
  78.0 0.2 select_reduce_fusion
  78.2 0.1 copy.47
  78.3 0.1 reshape.126
  78.4 0.1 fusion.7
  78.6 0.1 reshape.115
  78.7 0.6 copy.48
  79.3 3.2 %all-to-all-start.1 = ((bf16[4,4,4]{2,0,1:T(4,128)(2,1)}), bf16[4,4,4]{2,0,1:T(4,128)(2,1)S(1)}, u32[]{:S(2)}, u32[]{:S(2)}) async-start(bf16[4,4,4]{2,0,1:T(4,128)(2,1)} %copy.48), calls=%async_computation.2 | async-start | bytes 8192 | tf_op jit(solution)/shard_map/all_to_all | solution.py:126
  82.5 0.2 broadcast_in_dim.41
  82.8 0.1 reshape.113
  82.9 0.3 convolution_convert_fusion
  83.3 0.3 reshape.114
  83.6 1.2 %copy.46 = bf16[4,4,4,6144]{3,2,0,1:T(4,128)(2,1)} copy(bf16[4,4,4,6144]{3,2,1,0:T(4,128)(2,1)S(1)} %reshape.114) | data formatting | bytes 1572864 | tf_op jit(solution)/shard_map/reshape | solution.py:119
  84.7 1.6 %all-to-all-done.1 = bf16[4,4,4]{2,0,1:T(4,128)(2,1)S(1)} async-done(((bf16[4,4,4]{2,0,1:T(4,128)(2,1)}), bf16[4,4,4]{2,0,1:T(4,128)(2,1)S(1)}, u32[]{:S(2)}, u32[]{:S(2)}) %all-to-all-start.1) | async-done | bytes 160 | tf_op jit(solution)/shard_map/all_to_all | solution.py:126
  86.3 3.5 %all-to-all-start = ((bf16[4,4,4,6144]{3,2,0,1:T(4,128)(2,1)}), bf16[4,4,4,6144]{3,2,0,1:T(4,128)(2,1)S(1)}, u32[]{:S(2)}, u32[]{:S(2)}) async-start(bf16[4,4,4,6144]{3,2,0,1:T(4,128)(2,1)} %copy.46), calls=%async_computation.1 | async-start | bytes 1572864 | tf_op jit(solution)/shard_map/all_to_all | solution.py:125
  89.8 0.6 copy.73
  90.4 11.0 %all-to-all-done = bf16[4,4,4,6144]{3,2,0,1:T(4,128)(2,1)S(1)} async-done(((bf16[4,4,4,6144]{3,2,0,1:T(4,128)(2,1)}), bf16[4,4,4,6144]{3,2,0,1:T(4,128)(2,1)S(1)}, u32[]{:S(2)}, u32[]{:S(2)}) %all-to-all-start) | async-done | bytes 786464 | tf_op jit(solution)/shard_map/all_to_all | solution.py:125
  101.4 1.2 %copy.50 = bf16[1,1,4,4,4,6144]{5,4,3,2,1,0:T(4,128)(2,1)} copy(bf16[1,1,4,4,4,6144]{5,4,2,3,1,0:T(4,128)(2,1)S(1)} %bitcast.57) | data formatting | bytes 1572864
  (17 shorter events, 0.1 us)
Async XLA Ops:
  7.2 70.7 %copy-start = (bf16[1,6144,16]{1,2,0:T(8,128)(2,1)S(1)}, bf16[1,6144,16]{1,2,0:T(8,128)(2,1)}, u32[]{:S(2)}) copy-start(bf16[1,6144,16]{1,2,0:T(8,128)(2,1)} %param.18) | copy-start | bytes 589828
  7.2 62.6 %reduce-scatter.2.cloned.1.call-start = ((), (), s32[]{:S(2)}) async-start(), calls=%async_computation.3 | async-start | bytes 983040 | tf_op jit(solution)/shard_map/reduce_scatter | solution.py:88
  42.2 5.5 %copy-start.3 = (s32[1,16,2]{1,2,0:T(2,128)S(1)}, s32[1,16,2]{1,2,0:T(2,128)}, u32[]{:S(2)}) copy-start(s32[1,16,2]{1,2,0:T(2,128)} %param.19) | copy-start | bytes 388
  42.2 27.6 %copy-start.1 = (bf16[1,16,6144]{2,1,0:T(8,128)(2,1)S(1)}, bf16[1,16,6144]{2,1,0:T(8,128)(2,1)}, u32[]{:S(2)}) copy-start(bf16[1,16,6144]{2,1,0:T(8,128)(2,1)} %param.16) | copy-start | bytes 589828
  42.5 35.2 %copy-start.2 = (f32[1,6144]{1,0:T(1,128)S(1)}, f32[1,6144]{1,0:T(1,128)}, u32[]{:S(2)}) copy-start(f32[1,6144]{1,0:T(1,128)} %param.17) | copy-start | bytes 73732
  70.8 6.7 %collective-permute-start = (bf16[16,6144]{1,0:T(8,128)(2,1)S(1)}, bf16[16,6144]{1,0:T(8,128)(2,1)S(1)}, u32[]{:S(2)}, u32[]{:S(2)}) collective-permute-start(bf16[16,6144]{1,0:T(8,128)(2,1)S(1)} %fusion.11), channel_id=1, source_target_pairs={{16,0},{0,16},{17,1},{1,17},{18,2},{2,18},{19,3},{3,19},{20,4},{4,... | collective-permute-start | bytes 589832 | tf_op jit(solution)/shard_map/ppermute | solution.py:39
  79.3 7.0 %all-to-all-start.1 = ((bf16[4,4,4]{2,0,1:T(4,128)(2,1)}), bf16[4,4,4]{2,0,1:T(4,128)(2,1)S(1)}, u32[]{:S(2)}, u32[]{:S(2)}) async-start(bf16[4,4,4]{2,0,1:T(4,128)(2,1)} %copy.48), calls=%async_computation.2 | async-start | bytes 8192 | tf_op jit(solution)/shard_map/all_to_all | solution.py:126
  86.3 15.1 %all-to-all-start = ((bf16[4,4,4,6144]{3,2,0,1:T(4,128)(2,1)}), bf16[4,4,4,6144]{3,2,0,1:T(4,128)(2,1)S(1)}, u32[]{:S(2)}, u32[]{:S(2)}) async-start(bf16[4,4,4,6144]{3,2,0,1:T(4,128)(2,1)} %copy.46), calls=%async_computation.1 | async-start | bytes 1572864 | tf_op jit(solution)/shard_map/all_to_all | solution.py:125
Sparse Core Ops, SparseCore 0:
  47.8 21.9 reduce-scatter.1
where the time goes:
time: 110 us; the launch traced here: 109 us
  waiting for transfers between devices  39.4 us (36%)
  blocking collectives  28.2 us (26%)
  between operations  14.9 us (14%)
  local copies, waits for them, and re-layouts  9.26 us (8%)
  starting transfers between devices  8.31 us (8%)
  matrix products  6.53 us (6%)
  other arithmetic  2.83 us (3%)
    reduce_scatter x1, waiting for transfers between devices, on_device(): lax.psum_scatter(jnp.dot(attended, projection, preferred_element_type=jnp...  21.6 us
    all_gather x1, blocking collectives, entering(): lax.all_gather(a.astype(kind), axis)  14.8 us
    unnamed x1, blocking collectives  13.4 us
    all_to_all x1, waiting for transfers between devices, on_device(): lax.all_to_all(send_rows, 'exp', split_axis=1, concat_axis=1, tiled=True)  11 us
    ppermute x1, waiting for transfers between devices, from_behind(): return lax.ppermute(block, axis, route)  5.17 us
    dot_general x1, matrix products, on_device(): jnp.dot(attended, projection, preferred_element_type=jnp.float32)  4.87 us
    all_to_all x1, starting transfers between devices, on_device(): lax.all_to_all(send_rows, 'exp', split_axis=1, concat_axis=1, tiled=True)  3.49 us
    all_to_all x1, starting transfers between devices, on_device(): lax.all_to_all(send_gates, 'exp', split_axis=1, concat_axis=1, tiled=True)  3.25 us
  transfers between devices with their start and end apart: 4, of which 4 were waited for; matrix products, arithmetic and copies ran while one was open for 3% of the time, Pallas kernels for 0%

commit v1 on v0

v1 whole, which is shorter than its diff:
```python
import functools

import jax
import jax.numpy as jnp
from jax import lax
from jax.experimental import pallas as pl
from jax.experimental.pallas import tpu as pltpu
from jax.sharding import PartitionSpec as P

HEADS_LOCAL = 4
CAP = 4
EPSILON = 1e-05
LANES = 128
ROWS = 16
MIB = 1 << 20

VMEM = pl.BlockSpec(memory_space=pltpu.VMEM)
ANY = pl.BlockSpec(memory_space=pl.ANY)
bf16 = jnp.bfloat16
f32 = jnp.float32


def iota(shape, dim):
    return lax.broadcasted_iota(jnp.int32, shape, dim)


def mm(a, b, dims):
    return lax.dot_general(a, b, (dims, ((), ())), preferred_element_type=f32)


NN = ((1,), (0,))
NT = ((1,), (1,))
TN = ((0,), (0,))


def to_column(row):
    n = row.shape[1]
    square = jnp.broadcast_to(row, (n, n))
    return jnp.sum(jnp.where(iota((n, n), 0) == iota((n, n), 1), square, jnp.zeros_like(square)), axis=1, keepdims=True)


def cumulative(row):
    n = row.shape[1]
    at, of = iota((n, n), 0), iota((n, n), 1)
    column = -jnp.sum(jnp.where(of <= at, jnp.broadcast_to(row, (n, n)), 0.0), axis=1, keepdims=True)
    along = jnp.sum(jnp.where(at == of, jnp.broadcast_to(column, (n, n)), 0.0), axis=0, keepdims=True)
    return column, along


def pad_rows(heads):
    return -(-3 * heads // ROWS) * ROWS


def put_log(ref, base, heads, h, value):
    for part in range(3):
        piece = value.astype(bf16)
        ref[base + part * heads + h : base + part * heads + h + 1, :] = piece
        value = value - piece.astype(f32)


def get_log(block, heads, h):
    return block[h : h + 1] + block[heads + h : heads + h + 1] + block[2 * heads + h : 2 * heads + h + 1]


def state_kernel(k_ref, v_ref, decay_ref, msg_ref):
    heads = decay_ref.shape[0]
    dh = k_ref.shape[1] // heads
    base = heads * dh
    msg_ref[base:, :] = jnp.zeros((msg_ref.shape[0] - base, dh), bf16)
    for h in range(heads):
        row = decay_ref[h : h + 1, :]
        column, along = cumulative(row)
        last = along[:, -1:]
        tail = jnp.exp(last - column)
        keyed = (k_ref[:, h * dh : (h + 1) * dh].astype(f32) * tail).astype(bf16)
        msg_ref[h * dh : (h + 1) * dh, :] = mm(keyed, v_ref[:, h * dh : (h + 1) * dh], TN).astype(bf16)
        put_log(msg_ref, base, heads, h, jnp.broadcast_to(last, (1, dh)))


def join_kernel(heads, bit, own_ref, got_ref, msg_ref):
    dh = own_ref.shape[1]
    base = heads * dh
    upper = (lax.axis_index("ctx") >> bit) & 1
    is_upper = jnp.full((1, dh), upper, jnp.int32) == 1
    msg_ref[base:, :] = jnp.zeros((msg_ref.shape[0] - base, dh), bf16)
    own_block = own_ref[base:, :].astype(f32)
    got_block = got_ref[base:, :].astype(f32)
    for h in range(heads):
        own_log, got_log = get_log(own_block, heads, h), get_log(got_block, heads, h)
        own = own_ref[h * dh : (h + 1) * dh, :].astype(f32)
        got = got_ref[h * dh : (h + 1) * dh, :].astype(f32)
        scale_own = jnp.where(is_upper, 1.0, jnp.exp(got_log))
        scale_got = jnp.where(is_upper, jnp.exp(own_log), 1.0)
        msg_ref[h * dh : (h + 1) * dh, :] = (scale_own * own + scale_got * got).astype(bf16)
        put_log(msg_ref, base, heads, h, own_log + got_log)


def inside_kernel(q_ref, k_ref, v_ref, decay_ref, ids_ref, weight_ref, inside_ref, slots_ref, weight_out, sem):
    copy = pltpu.make_async_copy(weight_ref, weight_out, sem)
    copy.start()
    heads = decay_ref.shape[0]
    length = q_ref.shape[0]
    dh = q_ref.shape[1] // heads
    causal = iota((length, length), 0) >= iota((length, length), 1)
    for h in range(heads):
        cols = slice(h * dh, (h + 1) * dh)
        column, along = cumulative(decay_ref[h : h + 1, :])
        scores = mm(q_ref[:, cols], k_ref[:, cols], NT)
        weights = jnp.where(causal, scores * jnp.exp(jnp.minimum(column - along, 0.0)), 0.0).astype(bf16)
        inside_ref[:, cols] = mm(weights, v_ref[:, cols], NN)
    n = ids_ref.shape[1]
    earlier = iota((n, n), 1) < iota((n, n), 0)
    rows = [ids_ref[c : c + 1, :] for c in range(2)]
    places = []
    for c in range(2):
        mine = to_column(rows[c])
        rank = jnp.zeros((n, 1), jnp.int32)
        for other in range(2):
            rank += jnp.sum(jnp.where(earlier & (mine == rows[other]), 1, 0), axis=1, keepdims=True)
        places.append(mine * CAP + rank)
    lane = iota((n, LANES), 1)
    slots_ref[...] = jnp.where(lane == 0, places[0], jnp.where(lane == 1, places[1], 0))
    copy.wait()


def project_kernel(bits, order, q_ref, decay_ref, inside_ref, weight_ref, *rest):
    got_refs, (keep_ref, send_ref, attended) = rest[:bits], rest[bits:]
    heads = decay_ref.shape[0]
    dh = q_ref.shape[1] // heads
    base = heads * dh
    place = lax.axis_index("ctx")
    me = lax.axis_index("exp")
    blocks = [ref[base:, :].astype(f32) for ref in got_refs]
    uppers = [jnp.full((1, dh), (place >> bit) & 1, jnp.int32) == 1 for bit in range(bits)]
    for h in range(heads):
        cols = slice(h * dh, (h + 1) * dh)
        column, _ = cumulative(decay_ref[h : h + 1, :])
        incoming = jnp.zeros((dh, dh), f32)
        before = jnp.zeros((1, dh), f32)
        for bit in range(bits):
            got = got_refs[bit][h * dh : (h + 1) * dh, :].astype(f32)
            incoming += jnp.where(uppers[bit], jnp.exp(before), 0.0) * got
            before += jnp.where(uppers[bit], get_log(blocks[bit], heads, h), 0.0)
        high = incoming.astype(bf16)
        low = (incoming - high.astype(f32)).astype(bf16)
        outside = mm(q_ref[:, cols], high, NN) + mm(q_ref[:, cols], low, NN)
        attended[:, cols] = (inside_ref[:, cols] + jnp.exp(column) * outside).astype(bf16)
    share = q_ref.shape[0] // len(order)
    mixed = jnp.concatenate(
        [attended[pl.ds(pl.multiple_of((me ^ k) * share, share), share), :] for k in order], axis=0
    )
    half = mixed.shape[0] // 2
    width = weight_ref.shape[1]
    step = 1024 if width % 1024 == 0 else width
    for start in range(0, width, step):
        part = mm(mixed, weight_ref[:, start : start + step], NN).astype(bf16)
        keep_ref[:, start : start + step] = part[:half]
        send_ref[:, start : start + step] = part[half:]


def norm_kernel(got_ref, gain_ref, router_ref, ids_ref, slots_ref, msg_ref):
    wide = got_ref[...].astype(f32)
    tokens, width = wide.shape
    mean_sq = jnp.sum(wide * wide, axis=1, keepdims=True) * (1.0 / width)
    normed = (wide * lax.rsqrt(mean_sq + EPSILON) * gain_ref[...]).astype(bf16)
    msg_ref[:, :width] = normed
    logits = mm(normed, router_ref[...], NT)
    expert = iota(logits.shape, 1)
    picked = [
        jnp.sum(jnp.where(to_column(ids_ref[c : c + 1, :]) == expert, logits, 0.0), axis=1, keepdims=True)
        for c in range(2)
    ]
    first = 1.0 / (1.0 + jnp.exp(picked[1] - picked[0]))
    lane = iota((tokens, LANES), 1)
    slots = slots_ref[...].astype(f32)
    meta = jnp.where(lane == 2, first, jnp.where(lane == 3, 1.0 - first, slots))
    msg_ref[:, width:] = meta.astype(bf16)


def place_kernel(exp_count, *refs):
    groups, (rows_ref, gates_ref) = refs[:exp_count], refs[exp_count:]
    per_owner, _, cap, width = rows_ref.shape
    me = lax.axis_index("exp")
    tokens = groups[0].shape[0]
    slots = per_owner * exp_count * cap
    wheres, gates = [[], []], [[], []]
    for k in range(exp_count):
        sender = me ^ k
        meta = groups[k][:, width:].astype(f32)
        for c in range(2):
            place = meta[:, c : c + 1].astype(jnp.int32) - me * (per_owner * cap)
            expert, rank = place // cap, place % cap
            mine = (place >= 0) & (place < per_owner * cap)
            wheres[c].append(jnp.where(mine, (expert * exp_count + sender) * cap + rank, -1))
            gates[c].append(meta[:, 2 + c : 3 + c])
    wheres = [jnp.concatenate(w, axis=0) for w in wheres]
    gates = [jnp.concatenate(g, axis=0) for g in gates]
    total = tokens * exp_count
    slot = iota((total, slots), 1)
    chosen = ((wheres[0] == slot) | (wheres[1] == slot)).astype(f32).astype(bf16)
    hit_row = iota((total, per_owner * exp_count), 1)
    hit_rank = iota((total, LANES), 1)
    gate_rows = jnp.zeros((per_owner * exp_count, LANES), f32)
    for c in range(2):
        left = jnp.where((wheres[c] >= 0) & (wheres[c] // cap == hit_row), gates[c], 0.0).astype(bf16)
        right = jnp.where(wheres[c] % cap == hit_rank, 1.0, 0.0).astype(bf16)
        gate_rows += mm(left, right, TN)
    gate_rows = gate_rows.astype(bf16)
    for e in range(per_owner):
        gates_ref[e] = gate_rows[e * exp_count : (e + 1) * exp_count, :cap]
    step = 1024 if width % 1024 == 0 else width
    for start in range(0, width, step):
        block = jnp.concatenate([g[:, start : start + step] for g in groups], axis=0)
        out = mm(chosen, block, TN).astype(bf16)
        rows_ref[:, :, :, start : start + step] = out.reshape(per_owner, exp_count, cap, out.shape[1])


def swap(block, axis, mask):
    return lax.ppermute(block, axis, [(i, i ^ mask) for i in range(lax.axis_size(axis))])


def call(kernel, out, *args, specs=None, out_specs=None, scratch=(), flops=0, moved=0, limit=16 * MIB):
    single = not isinstance(out, (tuple, list))
    return pl.pallas_call(
        kernel,
        out_shape=out,
        in_specs=specs or [VMEM] * len(args),
        out_specs=out_specs or (VMEM if single else (VMEM,) * len(out)),
        scratch_shapes=scratch,
        compiler_params=pltpu.CompilerParams(vmem_limit_bytes=limit),
        cost_estimate=pl.CostEstimate(flops=flops, bytes_accessed=moved, transcendentals=0),
    )(*args)


def on_device(queries, keys_in, values, decay_rate, out_weight, residual, norm_gain, router, expert_ids):
    q, k, v, decay, weight = queries[0], keys_in[0], values[0], decay_rate[0], out_weight[0]
    ids = jnp.swapaxes(expert_ids[0], 0, 1)
    router_t = jnp.swapaxes(router[0], 0, 1)
    length, heads = q.shape[0], decay.shape[0]
    dh = q.shape[1] // heads
    width = weight.shape[1]
    tokens = residual.shape[1]
    exp_count, ctx_count = lax.axis_size("exp"), lax.axis_size("ctx")
    exp_bits, ctx_bits = exp_count.bit_length() - 1, ctx_count.bit_length() - 1
    per_owner = router.shape[2] // exp_count
    shape = jax.ShapeDtypeStruct

    msg_shape = shape((heads * dh + pad_rows(heads), dh), bf16)
    msg = call(state_kernel, msg_shape, k, v, decay)
    got = []
    for bit in range(ctx_bits):
        got.append(swap(msg, "ctx", (2 << bit) - 1))
        if bit < ctx_bits - 1:
            msg = call(functools.partial(join_kernel, heads, bit), msg_shape, msg, got[-1])

    inside, slots, weight_near = call(
        inside_kernel,
        (shape((length, heads * dh), f32), shape((tokens, LANES), jnp.int32), shape(weight.shape, bf16)),
        q, k, v, decay, ids, weight,
        specs=[VMEM] * 5 + [ANY],
        out_specs=(VMEM, VMEM, ANY),
        scratch=[pltpu.SemaphoreType.DMA],
        moved=2 * weight.size * 2,
    )
    order = [sum(((i >> b) & 1) << (exp_bits - 1 - b) for b in range(exp_bits)) for i in range(exp_count)]
    half = shape((length // 2, width), bf16)
    keep, send = call(
        functools.partial(project_kernel, ctx_bits, order),
        (half, half),
        q, decay, inside, weight_near, *got,
        scratch=[pltpu.VMEM((length, heads * dh), bf16)],
        flops=2 * length * weight.size,
        limit=32 * MIB,
    )
    total = keep.astype(f32)
    for bit in range(exp_bits):
        total = total + swap(send, "exp", 1 << bit).astype(f32)
        if bit < exp_bits - 1:
            middle = total.shape[0] // 2
            send, total = total[middle:].astype(bf16), total[:middle]
    hidden = (residual[0].astype(f32) + total).astype(bf16)
    sections = lax.axis_size("section")
    received = lax.ppermute(hidden, "section", [(i, (i + 1) % sections) for i in range(sections)])
    groups = [
        call(norm_kernel, shape((tokens, width + LANES), bf16), received, norm_gain, router_t, ids, slots)
    ]
    for index in range(1, exp_count):
        groups.append(swap(groups[index & (index - 1)], "exp", index & -index))
    rows, gates = call(
        functools.partial(place_kernel, exp_count),
        (shape((per_owner, exp_count, CAP, width), bf16), shape((per_owner, exp_count, CAP), bf16)),
        *groups,
    )
    return rows[None, None], gates[None, None]


def solution(mesh):
    placed = (
        P("section", "ctx", "exp"),
        P("section", "ctx", "exp"),
        P("section", "ctx", "exp"),
        P("section", "exp", "ctx"),
        P("section", "exp", None),
        P("section", ("ctx", "exp"), None),
        P("section", None),
        P("section", None, None),
        P("section", ("ctx", "exp"), None),
    )
    return jax.shard_map(
        on_device,
        mesh=mesh,
        in_specs=placed,
        out_specs=(
            P("section", "ctx", "exp", None, None, None),
            P("section", "ctx", "exp", None, None),
        ),
        check_vma=False,
    )
```

time: 110 us -> 48.1 us (0.44)
  blocking collectives: 28.2 us -> 0 us
  waiting for transfers between devices: 39.4 us -> 21 us
  between operations: 14.9 us -> 0.77 us
  matrix products: 6.53 us -> 0 us
  Pallas kernels: 0 us -> 4.9 us
  starting transfers between devices: 8.31 us -> 11.7 us
  other arithmetic: 2.83 us -> 0.14 us
    reduce_scatter x1 -> x0, waiting for transfers between devices: 21.6 us -> none  [on_device(): lax.psum_scatter(jnp.dot(attended, projection, preferred_element_type=jnp...]
    ppermute x1 -> x8, waiting for transfers between devices: 5.17 us -> 21 us  [the longest x7 16.4 us: swap(): lax.ppermute(block, axis, [(i, i ^ mask) for i in range(lax.axis_size(axi...]
    all_gather x1 -> x0, blocking collectives: 14.8 us -> none  [entering(): lax.all_gather(a.astype(kind), axis)]
    unnamed x1 -> x0, blocking collectives: 13.4 us -> none
    all_to_all x2 -> x0, waiting for transfers between devices: 12.6 us -> none  [the longest x1 11 us: on_device(): lax.all_to_all(send_rows, 'exp', split_axis=1, concat_axis=1, tiled=True)]
    ppermute x1 -> x8, starting transfers between devices: 1.53 us -> 11.7 us  [the longest x7 10.2 us: swap(): lax.ppermute(block, axis, [(i, i ^ mask) for i in range(lax.axis_size(axi...]
    all_to_all x2 -> x0, starting transfers between devices: 6.74 us -> none  [the longest x1 3.49 us: on_device(): lax.all_to_all(send_rows, 'exp', split_axis=1, concat_axis=1, tiled=True)]
    dot_general x7 -> x0, matrix products: 6.53 us -> none  [the longest x1 4.87 us: on_device(): jnp.dot(attended, projection, preferred_element_type=jnp.float32)]
  transfers between devices with their start and end apart: 4 -> 8, of which waited for: 4 -> 6; matrix products, arithmetic and copies ran while one was open for 3% -> 0% of each run, Pallas kernels for 0% -> 2%
where the time goes in v1:
time: 48.1 us; the launch traced here: 47.6 us
  waiting for transfers between devices  21 us (44%)
  starting transfers between devices  11.7 us (24%)
  local copies, waits for them, and re-layouts  9.1 us (19%)
  Pallas kernels  4.9 us (10%)
  between operations  0.77 us (2%)
    ppermute x7, waiting for transfers between devices, swap(): lax.ppermute(block, axis, [(i, i ^ mask) for i in range(lax.axis_size(axi...  16.4 us
    ppermute x7, starting transfers between devices, swap(): lax.ppermute(block, axis, [(i, i ^ mask) for i in range(lax.axis_size(axi...  10.2 us
    unnamed x30, local copies, waits for them, and re-layouts  9.08 us
    pallas_call x6, Pallas kernels, call(): pl.pallas_call(kernel, out_shape=out, in_specs=specs or [VMEM] * len(args...  4.9 us
    ppermute x1, waiting for transfers between devices, on_device(): lax.ppermute(hidden, 'section', [(i, (i + 1) % sections) for i in range(s...  4.63 us
    ppermute x1, starting transfers between devices, on_device(): lax.ppermute(hidden, 'section', [(i, (i + 1) % sections) for i in range(s...  1.55 us
  transfers between devices with their start and end apart: 8, of which 6 were waited for; matrix products, arithmetic and copies ran while one was open for 0% of the time, Pallas kernels for 2%

profile of v1, /device:TPU:0, one launch (start us, length us, event | category | flops | bytes accessed | tf_op | source)
XLA Modules:
  0.0 47.6 jit_solution(6259394437190999613)
XLA Ops:
  0.6 0.0 copy-start.2
  0.6 0.0 copy-start.3
  0.7 0.9 %copy-done.3 = bf16[1,64,512]{2,1,0:T(8,128)(2,1)S(1)} copy-done((bf16[1,64,512]{2,1,0:T(8,128)(2,1)S(1)}, bf16[1,64,512]{2,1,0:T(8,128)(2,1)}, u32[]{:S(2)}) %copy-start.3) | copy-done | bytes 65560
  1.5 0.0 copy-start.5
  1.5 0.8 %copy-done.5 = bf16[1,64,512]{2,1,0:T(8,128)(2,1)S(1)} copy-done((bf16[1,64,512]{2,1,0:T(8,128)(2,1)S(1)}, bf16[1,64,512]{2,1,0:T(8,128)(2,1)}, u32[]{:S(2)}) %copy-start.5) | copy-done | bytes 65560
  2.4 0.0 copy-start.9
  2.4 0.7 %copy-done.9 = f32[1,4,64]{2,1,0:T(4,128)S(1)} copy-done((f32[1,4,64]{2,1,0:T(4,128)S(1)}, f32[1,4,64]{2,1,0:T(4,128)}, u32[]{:S(2)}) %copy-start.9) | copy-done | bytes 1048
  3.0 0.0 copy-start.11
  3.0 0.4 shard_map.105.own_ref
  3.5 3.1 %collective-permute-start = (bf16[528,128]{1,0:T(8,128)(2,1)S(1)}, bf16[528,128]{1,0:T(8,128)(2,1)S(1)}, u32[]{:S(2)}, u32[]{:S(2)}) collective-permute-start(bf16[528,128]{1,0:T(8,128)(2,1)S(1)} %shard_map.105.own_ref), channel_id=1, source_target_pairs={{0,4},{4,0},{8,12},{12,8},{1,5},{5,1},{9,13},{13,9},{2,6},{6,2},{1... | collective-permute-start | bytes 405512 | tf_op jit(solution)/shard_map/ppermute | solution.py:219
  6.6 3.6 %collective-permute-done.got_ref.rest_0_ = bf16[528,128]{1,0:T(8,128)(2,1)S(1)} collective-permute-done((bf16[528,128]{1,0:T(8,128)(2,1)S(1)}, bf16[528,128]{1,0:T(8,128)(2,1)S(1)}, u32[]{:S(2)}, u32[]{:S(2)}) %collective-permute-start) | collective-permute-done | bytes 135200 | tf_op jit(solution)/shard_map/ppermute | solution.py:219
  10.2 0.1 shard_map.106
  10.2 3.8 %collective-permute-start.1 = (bf16[528,128]{1,0:T(8,128)(2,1)S(1)}, bf16[528,128]{1,0:T(8,128)(2,1)S(1)}, u32[]{:S(2)}, u32[]{:S(2)}) collective-permute-start(bf16[528,128]{1,0:T(8,128)(2,1)S(1)} %shard_map.106), channel_id=1, source_target_pairs={{0,12},{4,8},{8,4},{12,0},{1,13},{5,9},{9,5},{13,1},{2,14},{6,10},... | collective-permute-start | bytes 405512 | tf_op jit(solution)/shard_map/ppermute | solution.py:219
  14.1 0.0 copy-start
  14.1 2.8 %copy-done = bf16[1,512,6144]{2,1,0:T(8,128)(2,1)S(1)} copy-done((bf16[1,512,6144]{2,1,0:T(8,128)(2,1)S(1)}, bf16[1,512,6144]{2,1,0:T(8,128)(2,1)}, u32[]{:S(2)}) %copy-start) | copy-done | bytes 6291480
  16.8 0.8 %copy-done.1 = bf16[1,64,512]{2,1,0:T(8,128)(2,1)S(1)} copy-done((bf16[1,64,512]{2,1,0:T(8,128)(2,1)S(1)}, bf16[1,64,512]{2,1,0:T(8,128)(2,1)}, u32[]{:S(2)}) %copy-start.1) | copy-done | bytes 65560
  17.7 0.8 %copy-done.4 = bf16[1,64,512]{2,1,0:T(8,128)(2,1)S(1)} copy-done((bf16[1,64,512]{2,1,0:T(8,128)(2,1)S(1)}, bf16[1,64,512]{2,1,0:T(8,128)(2,1)}, u32[]{:S(2)}) %copy-start.4) | copy-done | bytes 65560
  18.5 0.8 %copy-done.6 = bf16[1,64,512]{2,1,0:T(8,128)(2,1)S(1)} copy-done((bf16[1,64,512]{2,1,0:T(8,128)(2,1)S(1)}, bf16[1,64,512]{2,1,0:T(8,128)(2,1)}, u32[]{:S(2)}) %copy-start.6) | copy-done | bytes 65560
  19.4 0.7 %copy-done.10 = f32[1,4,64]{2,1,0:T(4,128)S(1)} copy-done((f32[1,4,64]{2,1,0:T(4,128)S(1)}, f32[1,4,64]{2,1,0:T(4,128)}, u32[]{:S(2)}) %copy-start.10) | copy-done | bytes 1048
  20.0 0.7 %copy-done.12 = s32[1,16,2]{1,2,0:T(2,128)S(1)} copy-done((s32[1,16,2]{1,2,0:T(2,128)S(1)}, s32[1,16,2]{1,2,0:T(2,128)}, u32[]{:S(2)}) %copy-start.12) | copy-done | bytes 152
  20.7 1.1 %shard_map.104 = (f32[64,512]{1,0:T(8,128)S(1)}, s32[16,128]{1,0:T(8,128)S(1)}, bf16[512,6144]{1,0:T(8,128)(2,1)S(1)}) custom-call(bf16[64,512]{1,0:T(8,128)(2,1)S(1)} %bitcast.17, bf16[64,512]{1,0:T(8,128)(2,1)S(1)} %bitcast.20, bf16[64,512]{1,0:T(8,128)(2,1)S(1)} %bitcast.22, f32[4,64]{1,0:T(4,128)S(1)} %bitcast.25, s32[2,16]{1,0:T(2,128)S(1)} %bitcast.27, ...), custom_call_target="tpu_custom_call" | custom-call | bytes 12582912 | tf_op jit(solution)/shard_map/pallas_call | solution.py:224
  21.8 0.0 copy-start.7
  21.8 0.0 copy-start.8
  21.8 0.0 copy-start.13
  21.9 0.0 collective-permute-done.1.rest_1_
  21.9 0.0 copy-done.2
  21.9 0.0 copy-done.11
  21.9 1.4 %shard_map.107 = (bf16[32,6144]{1,0:T(8,128)(2,1)S(1)}, bf16[32,6144]{1,0:T(8,128)(2,1)S(1)}) custom-call(bf16[64,512]{1,0:T(8,128)(2,1)S(1)} %bitcast.18, f32[4,64]{1,0:T(4,128)S(1)} %bitcast.26, f32[64,512]{1,0:T(8,128)S(1)} %get-tuple-element.9.inside_ref, bf16[512,6144]{1,0:T(8,128)(2,1)S(1)} %get-tuple-element.10.weight_ref, ...), custom_call_target="tpu_custom_call" | custom-call | flops 402653184 | tf_op jit(solution)/shard_map/pallas_call | solution.py:224
  23.3 0.1 collective-permute-start.2
  23.4 1.7 %collective-permute-done.2 = bf16[32,6144]{1,0:T(8,128)(2,1)S(1)} collective-permute-done((bf16[32,6144]{1,0:T(8,128)(2,1)S(1)}, bf16[32,6144]{1,0:T(8,128)(2,1)S(1)}, u32[]{:S(2)}, u32[]{:S(2)}) %collective-permute-start.2) | collective-permute-done | bytes 393248 | tf_op jit(solution)/shard_map/ppermute | solution.py:219
  25.1 0.1 convert_add_fusion
  25.2 1.6 %collective-permute-start.3 = (bf16[16,6144]{1,0:T(8,128)(2,1)S(1)}, bf16[16,6144]{1,0:T(8,128)(2,1)S(1)}, u32[]{:S(2)}, u32[]{:S(2)}) collective-permute-start(bf16[16,6144]{1,0:T(8,128)(2,1)S(1)} %slice.17), channel_id=1, source_target_pairs={{0,2},{1,3},{2,0},{3,1},{4,6},{5,7},{6,4},{7,5},{8,10},{9,11},{10,... | collective-permute-start | bytes 589832 | tf_op jit(solution)/shard_map/ppermute | solution.py:219
  26.8 5.4 %collective-permute-done.3 = bf16[16,6144]{1,0:T(8,128)(2,1)S(1)} collective-permute-done((bf16[16,6144]{1,0:T(8,128)(2,1)S(1)}, bf16[16,6144]{1,0:T(8,128)(2,1)S(1)}, u32[]{:S(2)}, u32[]{:S(2)}) %collective-permute-start.3) | collective-permute-done | bytes 196640 | tf_op jit(solution)/shard_map/ppermute | solution.py:219
  32.2 0.0 copy-done.14
  32.2 0.1 fusion.1
  32.3 1.6 %collective-permute-start.4 = (bf16[16,6144]{1,0:T(8,128)(2,1)S(1)}, bf16[16,6144]{1,0:T(8,128)(2,1)S(1)}, u32[]{:S(2)}, u32[]{:S(2)}) collective-permute-start(bf16[16,6144]{1,0:T(8,128)(2,1)S(1)} %fusion.1), channel_id=1, source_target_pairs={{0,16},{16,0},{1,17},{17,1},{2,18},{18,2},{3,19},{19,3},{4,20},{20... | collective-permute-start | bytes 589832 | tf_op jit(solution)/shard_map/ppermute | solution.py:283
  33.8 4.6 %collective-permute-done.4.got_ref = bf16[16,6144]{1,0:T(8,128)(2,1)S(1)} collective-permute-done((bf16[16,6144]{1,0:T(8,128)(2,1)S(1)}, bf16[16,6144]{1,0:T(8,128)(2,1)S(1)}, u32[]{:S(2)}, u32[]{:S(2)}) %collective-permute-start.4) | collective-permute-done | bytes 196640 | tf_op jit(solution)/shard_map/ppermute | solution.py:283
  38.5 0.0 copy-done.7
  38.5 0.0 copy-done.8
  38.5 0.0 copy-done.13
  38.5 0.4 shard_map.108.refs_0_
  38.9 1.6 %collective-permute-start.6 = (bf16[16,6272]{1,0:T(8,128)(2,1)S(1)}, bf16[16,6272]{1,0:T(8,128)(2,1)S(1)}, u32[]{:S(2)}, u32[]{:S(2)}) collective-permute-start(bf16[16,6272]{1,0:T(8,128)(2,1)S(1)} %shard_map.108.refs_0_), channel_id=1, source_target_pairs={{0,2},{1,3},{2,0},{3,1},{4,6},{5,7},{6,4},{7,5},{8,10},{9,11},{10,... | collective-permute-start | bytes 602120 | tf_op jit(solution)/shard_map/ppermute | solution.py:219
  40.5 0.0 collective-permute-start.5
  40.5 4.2 %collective-permute-done.6.refs_2_ = bf16[16,6272]{1,0:T(8,128)(2,1)S(1)} collective-permute-done((bf16[16,6272]{1,0:T(8,128)(2,1)S(1)}, bf16[16,6272]{1,0:T(8,128)(2,1)S(1)}, u32[]{:S(2)}, u32[]{:S(2)}) %collective-permute-start.6) | collective-permute-done | bytes 200736 | tf_op jit(solution)/shard_map/ppermute | solution.py:219
  44.7 0.0 collective-permute-start.7
  44.7 0.0 collective-permute-done.5.refs_1_
  44.7 1.4 %collective-permute-done.7.refs_3_ = bf16[16,6272]{1,0:T(8,128)(2,1)S(1)} collective-permute-done((bf16[16,6272]{1,0:T(8,128)(2,1)S(1)}, bf16[16,6272]{1,0:T(8,128)(2,1)S(1)}, u32[]{:S(2)}, u32[]{:S(2)}) %collective-permute-start.7) | collective-permute-done | bytes 200736 | tf_op jit(solution)/shard_map/ppermute | solution.py:219
  46.2 1.5 %shard_map.109 = (bf16[4,4,4,6144]{3,2,1,0:T(4,128)(2,1)}, bf16[4,4,4]{2,1,0:T(4,128)(2,1)}) custom-call(bf16[16,6272]{1,0:T(8,128)(2,1)S(1)} %shard_map.108.refs_0_, bf16[16,6272]{1,0:T(8,128)(2,1)S(1)} %collective-permute-done.5.refs_1_, bf16[16,6272]{1,0:T(8,128)(2,1)S(1)} %collective-permute-done.6.refs_2_, ...), custom_call_target="tpu_custom_call" | custom-call | tf_op jit(solution)/shard_map/pallas_call | solution.py:224
  (7 shorter events, 0.0 us)
Async XLA Ops:
  0.6 21.2 %copy-start.2 = (bf16[1,64,512]{2,1,0:T(8,128)(2,1)S(1)}, bf16[1,64,512]{2,1,0:T(8,128)(2,1)}, u32[]{:S(2)}) copy-start(bf16[1,64,512]{2,1,0:T(8,128)(2,1)} %param.9) | copy-start | bytes 196612
  0.6 0.9 %copy-start.3 = (bf16[1,64,512]{2,1,0:T(8,128)(2,1)S(1)}, bf16[1,64,512]{2,1,0:T(8,128)(2,1)}, u32[]{:S(2)}) copy-start(bf16[1,64,512]{2,1,0:T(8,128)(2,1)} %param.10) | copy-start | bytes 196612
  1.5 0.8 %copy-start.5 = (bf16[1,64,512]{2,1,0:T(8,128)(2,1)S(1)}, bf16[1,64,512]{2,1,0:T(8,128)(2,1)}, u32[]{:S(2)}) copy-start(bf16[1,64,512]{2,1,0:T(8,128)(2,1)} %param.11) | copy-start | bytes 196612
  2.4 0.7 %copy-start.9 = (f32[1,4,64]{2,1,0:T(4,128)S(1)}, f32[1,4,64]{2,1,0:T(4,128)}, u32[]{:S(2)}) copy-start(f32[1,4,64]{2,1,0:T(4,128)} %param.12) | copy-start | bytes 3076
  3.0 18.8 %copy-start.11 = (f32[1,4,64]{2,1,0:T(4,128)S(1)}, f32[1,4,64]{2,1,0:T(4,128)}, u32[]{:S(2)}) copy-start(f32[1,4,64]{2,1,0:T(4,128)} %param.12) | copy-start | bytes 3076
  3.5 6.7 %collective-permute-start = (bf16[528,128]{1,0:T(8,128)(2,1)S(1)}, bf16[528,128]{1,0:T(8,128)(2,1)S(1)}, u32[]{:S(2)}, u32[]{:S(2)}) collective-permute-start(bf16[528,128]{1,0:T(8,128)(2,1)S(1)} %shard_map.105.own_ref), channel_id=1, source_target_pairs={{0,4},{4,0},{8,12},{12,8},{1,5},{5,1},{9,13},{13,9},{2,6},{6,2},{1... | collective-permute-start | bytes 405512 | tf_op jit(solution)/shard_map/ppermute | solution.py:219
  10.2 11.6 %collective-permute-start.1 = (bf16[528,128]{1,0:T(8,128)(2,1)S(1)}, bf16[528,128]{1,0:T(8,128)(2,1)S(1)}, u32[]{:S(2)}, u32[]{:S(2)}) collective-permute-start(bf16[528,128]{1,0:T(8,128)(2,1)S(1)} %shard_map.106), channel_id=1, source_target_pairs={{0,12},{4,8},{8,4},{12,0},{1,13},{5,9},{9,5},{13,1},{2,14},{6,10},... | collective-permute-start | bytes 405512 | tf_op jit(solution)/shard_map/ppermute | solution.py:219
  14.1 2.8 %copy-start = (bf16[1,512,6144]{2,1,0:T(8,128)(2,1)S(1)}, bf16[1,512,6144]{2,1,0:T(8,128)(2,1)}, u32[]{:S(2)}) copy-start(bf16[1,512,6144]{2,1,0:T(8,128)(2,1)} %param.13) | copy-start | bytes 18874372
  16.8 0.8 %copy-start.1 = (bf16[1,64,512]{2,1,0:T(8,128)(2,1)S(1)}, bf16[1,64,512]{2,1,0:T(8,128)(2,1)}, u32[]{:S(2)}) copy-start(bf16[1,64,512]{2,1,0:T(8,128)(2,1)} %param.9) | copy-start | bytes 196612
  17.7 0.8 %copy-start.4 = (bf16[1,64,512]{2,1,0:T(8,128)(2,1)S(1)}, bf16[1,64,512]{2,1,0:T(8,128)(2,1)}, u32[]{:S(2)}) copy-start(bf16[1,64,512]{2,1,0:T(8,128)(2,1)} %param.10) | copy-start | bytes 196612
  18.5 0.8 %copy-start.6 = (bf16[1,64,512]{2,1,0:T(8,128)(2,1)S(1)}, bf16[1,64,512]{2,1,0:T(8,128)(2,1)}, u32[]{:S(2)}) copy-start(bf16[1,64,512]{2,1,0:T(8,128)(2,1)} %param.11) | copy-start | bytes 196612
  19.4 0.7 %copy-start.10 = (f32[1,4,64]{2,1,0:T(4,128)S(1)}, f32[1,4,64]{2,1,0:T(4,128)}, u32[]{:S(2)}) copy-start(f32[1,4,64]{2,1,0:T(4,128)} %param.12) | copy-start | bytes 3076
  20.0 0.7 %copy-start.12 = (s32[1,16,2]{1,2,0:T(2,128)S(1)}, s32[1,16,2]{1,2,0:T(2,128)}, u32[]{:S(2)}) copy-start(s32[1,16,2]{1,2,0:T(2,128)} %param.17) | copy-start | bytes 388
  20.7 11.5 %copy-start.14 = (bf16[1,16,6144]{2,1,0:T(8,128)(2,1)S(1)}, bf16[1,16,6144]{2,1,0:T(8,128)(2,1)}, u32[]{:S(2)}) copy-start(bf16[1,16,6144]{2,1,0:T(8,128)(2,1)} %param.14) | copy-start | bytes 589828
  21.8 16.6 %copy-start.7 = (bf16[1,6144,16]{1,2,0:T(8,128)(2,1)S(1)}, bf16[1,6144,16]{1,2,0:T(8,128)(2,1)}, u32[]{:S(2)}) copy-start(bf16[1,6144,16]{1,2,0:T(8,128)(2,1)} %param.16) | copy-start | bytes 589828
  21.8 16.6 %copy-start.8 = (f32[1,6144]{1,0:T(1,128)S(1)}, f32[1,6144]{1,0:T(1,128)}, u32[]{:S(2)}) copy-start(f32[1,6144]{1,0:T(1,128)} %gain_ref.1) | copy-start | bytes 73732
  21.8 16.6 %copy-start.13 = (s32[1,16,2]{1,2,0:T(2,128)S(1)}, s32[1,16,2]{1,2,0:T(2,128)}, u32[]{:S(2)}) copy-start(s32[1,16,2]{1,2,0:T(2,128)} %param.17) | copy-start | bytes 388
  23.3 1.8 %collective-permute-start.2 = (bf16[32,6144]{1,0:T(8,128)(2,1)S(1)}, bf16[32,6144]{1,0:T(8,128)(2,1)S(1)}, u32[]{:S(2)}, u32[]{:S(2)}) collective-permute-start(bf16[32,6144]{1,0:T(8,128)(2,1)S(1)} %get-tuple-element.12), channel_id=1, source_target_pairs={{0,1},{1,0},{2,3},{3,2},{4,5},{5,4},{6,7},{7,6},{8,9},{9,8},{10,11... | collective-permute-start | bytes 1179656 | tf_op jit(solution)/shard_map/ppermute | solution.py:219
  25.2 7.0 %collective-permute-start.3 = (bf16[16,6144]{1,0:T(8,128)(2,1)S(1)}, bf16[16,6144]{1,0:T(8,128)(2,1)S(1)}, u32[]{:S(2)}, u32[]{:S(2)}) collective-permute-start(bf16[16,6144]{1,0:T(8,128)(2,1)S(1)} %slice.17), channel_id=1, source_target_pairs={{0,2},{1,3},{2,0},{3,1},{4,6},{5,7},{6,4},{7,5},{8,10},{9,11},{10,... | collective-permute-start | bytes 589832 | tf_op jit(solution)/shard_map/ppermute | solution.py:219
  32.3 6.2 %collective-permute-start.4 = (bf16[16,6144]{1,0:T(8,128)(2,1)S(1)}, bf16[16,6144]{1,0:T(8,128)(2,1)S(1)}, u32[]{:S(2)}, u32[]{:S(2)}) collective-permute-start(bf16[16,6144]{1,0:T(8,128)(2,1)S(1)} %fusion.1), channel_id=1, source_target_pairs={{0,16},{16,0},{1,17},{17,1},{2,18},{18,2},{3,19},{19,3},{4,20},{20... | collective-permute-start | bytes 589832 | tf_op jit(solution)/shard_map/ppermute | solution.py:283
  38.9 5.8 %collective-permute-start.6 = (bf16[16,6272]{1,0:T(8,128)(2,1)S(1)}, bf16[16,6272]{1,0:T(8,128)(2,1)S(1)}, u32[]{:S(2)}, u32[]{:S(2)}) collective-permute-start(bf16[16,6272]{1,0:T(8,128)(2,1)S(1)} %shard_map.108.refs_0_), channel_id=1, source_target_pairs={{0,2},{1,3},{2,0},{3,1},{4,6},{5,7},{6,4},{7,5},{8,10},{9,11},{10,... | collective-permute-start | bytes 602120 | tf_op jit(solution)/shard_map/ppermute | solution.py:219
  40.5 4.2 %collective-permute-start.5 = (bf16[16,6272]{1,0:T(8,128)(2,1)S(1)}, bf16[16,6272]{1,0:T(8,128)(2,1)S(1)}, u32[]{:S(2)}, u32[]{:S(2)}) collective-permute-start(bf16[16,6272]{1,0:T(8,128)(2,1)S(1)} %shard_map.108.refs_0_), channel_id=1, source_target_pairs={{0,1},{1,0},{2,3},{3,2},{4,5},{5,4},{6,7},{7,6},{8,9},{9,8},{10,11... | collective-permute-start | bytes 602120 | tf_op jit(solution)/shard_map/ppermute | solution.py:219
  44.7 1.4 %collective-permute-start.7 = (bf16[16,6272]{1,0:T(8,128)(2,1)S(1)}, bf16[16,6272]{1,0:T(8,128)(2,1)S(1)}, u32[]{:S(2)}, u32[]{:S(2)}) collective-permute-start(bf16[16,6272]{1,0:T(8,128)(2,1)S(1)} %collective-permute-done.6.refs_2_), channel_id=1, source_target_pairs={{0,1},{1,0},{2,3},{3,2},{4,5},{5,4},{6,7},{7,6},{8,9},{9,8},{10,11... | collective-permute-start | bytes 602120 | tf_op jit(solution)/shard_map/ppermute | solution.py:219

commit v2 on v1

v2 whole, which is shorter than its diff:
```python
import functools

import jax
import jax.numpy as jnp
from jax import lax
from jax.experimental import pallas as pl
from jax.experimental.pallas import tpu as pltpu
from jax.sharding import PartitionSpec as P

CAP = 4
EPSILON = 1e-05
LANES = 128
ROWS = 16
MIB = 1 << 20
PARTS = 2

VMEM = pl.BlockSpec(memory_space=pltpu.VMEM)
HBM = pl.BlockSpec(memory_space=pltpu.HBM)
bf16 = jnp.bfloat16
f32 = jnp.float32


def iota(shape, dim):
    return lax.broadcasted_iota(jnp.int32, shape, dim)


def mm(a, b, dims):
    return lax.dot_general(a, b, (dims, ((), ())), preferred_element_type=f32)


NN = ((1,), (0,))
NT = ((1,), (1,))
TN = ((0,), (0,))


def to_column(row):
    n = row.shape[1]
    square = jnp.broadcast_to(row, (n, n))
    return jnp.sum(jnp.where(iota((n, n), 0) == iota((n, n), 1), square, jnp.zeros_like(square)), axis=1, keepdims=True)


def cumulative(row):
    n = row.shape[1]
    at, of = iota((n, n), 0), iota((n, n), 1)
    column = -jnp.sum(jnp.where(of <= at, jnp.broadcast_to(row, (n, n)), 0.0), axis=1, keepdims=True)
    along = jnp.sum(jnp.where(at == of, jnp.broadcast_to(column, (n, n)), 0.0), axis=0, keepdims=True)
    return column, along


def pad_rows(heads):
    return -(-3 * heads // ROWS) * ROWS


def put_log(ref, base, heads, h, value):
    for part in range(3):
        piece = value.astype(bf16)
        ref[base + part * heads + h : base + part * heads + h + 1, :] = piece
        value = value - piece.astype(f32)


def get_log(block, heads, h):
    return block[h : h + 1] + block[heads + h : heads + h + 1] + block[2 * heads + h : 2 * heads + h + 1]


def fetch(sources, places, sems):
    copies = [pltpu.make_async_copy(s, p, sems.at[i]) for i, (s, p) in enumerate(zip(sources, places, strict=True))]
    for copy in copies:
        copy.start()
    return copies


def state_kernel(k_hbm, v_hbm, decay_hbm, msg_ref, k_ref, v_ref, decay_ref, sems):
    copies = fetch((decay_hbm, k_hbm, v_hbm), (decay_ref, k_ref, v_ref), sems)
    heads = decay_ref.shape[0]
    dh = k_ref.shape[1] // heads
    base = heads * dh
    msg_ref[base:, :] = jnp.zeros((msg_ref.shape[0] - base, dh), bf16)
    copies[0].wait()
    tails = []
    for h in range(heads):
        column, along = cumulative(decay_ref[h : h + 1, :])
        last = along[:, -1:]
        tails.append(jnp.exp(last - column))
        put_log(msg_ref, base, heads, h, jnp.broadcast_to(last, (1, dh)))
    copies[1].wait()
    copies[2].wait()
    for h in range(heads):
        keyed = (k_ref[:, h * dh : (h + 1) * dh].astype(f32) * tails[h]).astype(bf16)
        msg_ref[h * dh : (h + 1) * dh, :] = mm(keyed, v_ref[:, h * dh : (h + 1) * dh], TN).astype(bf16)


def joined(heads, bit, own_ref, got_ref):
    dh = own_ref.shape[1]
    base = heads * dh
    upper = (lax.axis_index("ctx") >> bit) & 1
    is_upper = jnp.full((1, dh), upper, jnp.int32) == 1
    own_block = own_ref[base:, :].astype(f32)
    got_block = got_ref[base:, :].astype(f32)
    for h in range(heads):
        own_log, got_log = get_log(own_block, heads, h), get_log(got_block, heads, h)
        own = own_ref[h * dh : (h + 1) * dh, :].astype(f32)
        got = got_ref[h * dh : (h + 1) * dh, :].astype(f32)
        scale_own = jnp.where(is_upper, 1.0, jnp.exp(got_log))
        scale_got = jnp.where(is_upper, jnp.exp(own_log), 1.0)
        yield scale_own * own + scale_got * got, own_log + got_log


def join_kernel(heads, bit, own_ref, got_ref, msg_ref):
    dh = own_ref.shape[1]
    base = heads * dh
    msg_ref[base:, :] = jnp.zeros((msg_ref.shape[0] - base, dh), bf16)
    for h, (state, log) in enumerate(joined(heads, bit, own_ref, got_ref)):
        msg_ref[h * dh : (h + 1) * dh, :] = state.astype(bf16)
        put_log(msg_ref, base, heads, h, log)


def split_mm(a, state):
    high = state.astype(bf16)
    low = (state - high.astype(f32)).astype(bf16)
    return mm(a, high, NN) + mm(a, low, NN)


def inside_kernel(q_hbm, k_hbm, v_hbm, decay_hbm, ids_hbm, weight_hbm, inside_ref, slots_ref, weight_ref, q_ref, growth_ref,
                  k_ref, v_ref, decay_ref, ids_ref, sems):
    copies = fetch(
        (decay_hbm, ids_hbm, q_hbm, k_hbm, v_hbm, weight_hbm), (decay_ref, ids_ref, q_ref, k_ref, v_ref, weight_ref), sems
    )
    for copy in copies[:-1]:
        copy.wait()
    heads = decay_ref.shape[0]
    length = q_ref.shape[0]
    dh = q_ref.shape[1] // heads
    causal = iota((length, length), 0) >= iota((length, length), 1)
    lane = iota((length, LANES), 1)
    growth = jnp.zeros((length, LANES), f32)
    for h in range(heads):
        cols = slice(h * dh, (h + 1) * dh)
        column, along = cumulative(decay_ref[h : h + 1, :])
        scores = mm(q_ref[:, cols], k_ref[:, cols], NT)
        weights = jnp.where(causal, scores * jnp.exp(jnp.minimum(column - along, 0.0)), 0.0).astype(bf16)
        inside_ref[:, cols] = mm(weights, v_ref[:, cols], NN)
        growth = jnp.where(lane == h, jnp.exp(column), growth)
    growth_ref[...] = growth
    n = ids_ref.shape[1]
    earlier = iota((n, n), 1) < iota((n, n), 0)
    rows = [ids_ref[c : c + 1, :] for c in range(2)]
    places = []
    for c in range(2):
        mine = to_column(rows[c])
        rank = jnp.zeros((n, 1), jnp.int32)
        for other in range(2):
            rank += jnp.sum(jnp.where(earlier & (mine == rows[other]), 1, 0), axis=1, keepdims=True)
        places.append(mine * CAP + rank)
    lane = iota((n, LANES), 1)
    slots_ref[...] = jnp.where(lane == 0, places[0], jnp.where(lane == 1, places[1], 0))
    copies[-1].wait()


def base_kernel(heads, q_ref, inside_ref, growth_ref, *rest):
    got_refs, (base_ref, scale_ref) = rest[:-2], rest[-2:]
    bits = len(got_refs)
    dh = q_ref.shape[1] // heads
    base = heads * dh
    place = lax.axis_index("ctx")
    blocks = [ref[base:, :].astype(f32) for ref in got_refs]
    uppers = [jnp.full((1, dh), (place >> bit) & 1, jnp.int32) == 1 for bit in range(bits + 1)]
    lane = iota(scale_ref.shape, 1)
    scale = jnp.zeros(scale_ref.shape, f32)
    for h in range(heads):
        cols = slice(h * dh, (h + 1) * dh)
        incoming = jnp.zeros((dh, dh), f32)
        before = jnp.zeros((1, dh), f32)
        for bit in range(bits):
            got = got_refs[bit][h * dh : (h + 1) * dh, :].astype(f32)
            incoming += jnp.where(uppers[bit], jnp.exp(before), 0.0) * got
            before += jnp.where(uppers[bit], get_log(blocks[bit], heads, h), 0.0)
        growth = growth_ref[:, h : h + 1]
        base_ref[:, cols] = inside_ref[:, cols] + growth * split_mm(q_ref[:, cols], incoming)
        factor = jnp.where(uppers[bits], jnp.exp(before), 0.0)
        scale = jnp.where(lane == h, growth * factor[:, :1], scale)
    scale_ref[...] = scale


def mix_kernel(heads, order, start, stop, q_ref, base_ref, scale_ref, got_ref, weight_ref, mixed_ref, keep_ref, send_ref, attended):
    dh = base_ref.shape[1] // heads
    me = lax.axis_index("exp")
    for h in range(heads):
        cols = slice(h * dh, (h + 1) * dh)
        outside = mm(q_ref[:, cols], got_ref[h * dh : (h + 1) * dh, :], NN)
        attended[:, cols] = (base_ref[:, cols] + scale_ref[:, h : h + 1] * outside).astype(bf16)
    share = base_ref.shape[0] // len(order)
    for i, k in enumerate(order):
        mixed_ref[i * share : (i + 1) * share, :] = attended[pl.ds(pl.multiple_of((me ^ k) * share, share), share), :]
    project_kernel(start, stop, mixed_ref, weight_ref, keep_ref, send_ref)


def project_kernel(start, stop, mixed_ref, weight_ref, keep_ref, send_ref):
    half = mixed_ref.shape[0] // 2
    mixed = mixed_ref[...]
    for at, to in pieces(start, stop):
        part = mm(mixed, weight_ref[:, at:to], NN).astype(bf16)
        keep_ref[:, at - start : to - start] = part[:half]
        send_ref[:, at - start : to - start] = part[half:]


def pieces(start, stop, step=1024):
    return [(at, min(at + step, stop)) for at in range(start, stop, step)]


def halve_kernel(keep_ref, got_ref, send_ref, own_ref):
    half = own_ref.shape[0]
    own_ref[...] = keep_ref[:half, :].astype(f32) + got_ref[:half, :].astype(f32)
    send_ref[...] = (keep_ref[half:, :].astype(f32) + got_ref[half:, :].astype(f32)).astype(bf16)


def hidden_kernel(start, own_ref, got_ref, residual_ref, out_ref):
    stop = start + own_ref.shape[1]
    total = own_ref[...].astype(f32) + got_ref[...].astype(f32)
    out_ref[...] = (residual_ref[:, start:stop].astype(f32) + total).astype(bf16)


def tag_kernel(got_ref, slots_ref, msg_ref):
    size = got_ref.shape[1]
    msg_ref[:, :size] = got_ref[...]
    msg_ref[:, size:] = slots_ref[...].astype(f32).astype(bf16)


def partial(groups, gain, router, start):
    square, logits = 0.0, 0.0
    for at, to in pieces(0, groups[0].shape[1] // LANES * LANES):
        wide = jnp.concatenate([g[:, at:to] for g in groups], axis=0).astype(f32)
        square += jnp.sum(wide * wide, axis=1, keepdims=True)
        gained = (wide * gain[:, start + at : start + to]).astype(bf16)
        logits += mm(gained, router[:, start + at : start + to], NT)
    return square, logits


def ahead_kernel(exp_count, experts, *refs):
    groups, (gain_ref, router_ref, chosen_ref, target_ref, square_ref, logits_ref) = refs[:exp_count], refs[exp_count:]
    size = groups[0].shape[1] - LANES
    per_owner = experts // exp_count
    me = lax.axis_index("exp")
    tokens = groups[0].shape[0]
    wheres, named = [[], []], [[], []]
    for k in range(exp_count):
        sender = me ^ k
        meta = groups[k][:, size:].astype(f32).astype(jnp.int32)
        for c in range(2):
            slot = meta[:, c : c + 1]
            place = slot - me * (per_owner * CAP)
            mine = (place >= 0) & (place < per_owner * CAP)
            wheres[c].append(jnp.where(mine, (place // CAP * exp_count + sender) * CAP + place % CAP, -1))
            named[c].append(slot // CAP)
    wheres = [jnp.concatenate(w, axis=0) for w in wheres]
    named = [jnp.concatenate(n, axis=0) for n in named]
    total = tokens * exp_count
    slot = iota(chosen_ref.shape, 1)
    chosen_ref[...] = ((wheres[0] == slot) | (wheres[1] == slot)).astype(f32).astype(bf16)
    lane = iota((total, LANES), 1)
    target = jnp.zeros((total, LANES), jnp.int32)
    for i, column in enumerate(wheres + named):
        target = jnp.where(lane == i, column, target)
    target_ref[...] = target
    square, logits = partial([g.at[:, :size] for g in groups], gain_ref, router_ref, 0)
    square_ref[...] = jnp.broadcast_to(square, square_ref.shape)
    logits_ref[...] = logits


def place_kernel(exp_count, parts, *refs):
    groups = [refs[i * exp_count : (i + 1) * exp_count] for i in range(parts)]
    chosen_ref, target_ref, square_ref, logits_ref, gain_ref, router_ref, rows_hbm, gates_ref, rows_ref, sems = refs[parts * exp_count :]
    per_owner, _, cap, width = rows_ref.shape
    sizes = [part[0].shape[1] for part in groups]
    sizes[0] -= LANES
    square, logits = square_ref[:, :1], logits_ref[...]
    at = sizes[0]
    for part, size in zip(groups[1:], sizes[1:]):
        more = partial(part, gain_ref, router_ref, at)
        square, logits = square + more[0], logits + more[1]
        at += size
    factor = lax.rsqrt(square * (1.0 / width) + EPSILON)
    chosen = chosen_ref[...]
    copies = []
    at = 0
    for part, size in zip(groups, sizes):
        for start, stop in pieces(0, size):
            wide = jnp.concatenate([g[:, start:stop] for g in part], axis=0).astype(f32)
            normed = (wide * factor * gain_ref[:, at + start : at + stop]).astype(bf16)
            out = mm(chosen, normed, TN).astype(bf16)
            window = (slice(None), slice(None), slice(None), slice(at + start, at + stop))
            rows_ref[window] = out.reshape(per_owner, exp_count, cap, stop - start)
            copies.append(pltpu.make_async_copy(rows_ref.at[window], rows_hbm.at[window], sems.at[len(copies)]))
            copies[-1].start()
        at += size
    logits = logits * factor
    target = target_ref[...]
    wheres, named = [target[:, c : c + 1] for c in range(2)], [target[:, 2 + c : 3 + c] for c in range(2)]
    expert = iota(logits.shape, 1)
    picked = [jnp.sum(jnp.where(named[c] == expert, logits, 0.0), axis=1, keepdims=True) for c in range(2)]
    first = 1.0 / (1.0 + jnp.exp(picked[1] - picked[0]))
    gates = [first, 1.0 - first]
    total = logits.shape[0]
    hit_row = iota((total, per_owner * exp_count), 1)
    hit_rank = iota((total, LANES), 1)
    gate_rows = jnp.zeros((per_owner * exp_count, LANES), f32)
    for c in range(2):
        left = jnp.where((wheres[c] >= 0) & (wheres[c] // cap == hit_row), gates[c], 0.0).astype(bf16)
        right = jnp.where(wheres[c] % cap == hit_rank, 1.0, 0.0).astype(bf16)
        gate_rows += mm(left, right, TN)
    gate_rows = gate_rows.astype(bf16)
    for e in range(per_owner):
        gates_ref[e] = gate_rows[e * exp_count : (e + 1) * exp_count, :cap]
    for copy in copies:
        copy.wait()


def swap(block, axis, mask):
    return lax.ppermute(block, axis, [(i, i ^ mask) for i in range(lax.axis_size(axis))])


def call(kernel, out, *args, specs=None, out_specs=None, scratch=(), flops=0, moved=0, limit=16 * MIB):
    single = not isinstance(out, (tuple, list))
    specs = specs or [VMEM] * len(args)
    args = [pltpu.with_memory_space_constraint(a, pltpu.HBM) if s is HBM else a for a, s in zip(args, specs, strict=True)]
    return pl.pallas_call(
        kernel,
        out_shape=out,
        in_specs=specs,
        out_specs=out_specs or (VMEM if single else (VMEM,) * len(out)),
        scratch_shapes=scratch,
        compiler_params=pltpu.CompilerParams(vmem_limit_bytes=limit),
        cost_estimate=pl.CostEstimate(flops=flops, bytes_accessed=moved, transcendentals=0),
    )(*args)


def on_device(queries, keys_in, values, decay_rate, out_weight, residual, norm_gain, router, expert_ids):
    q, k, v, decay, weight = queries[0], keys_in[0], values[0], decay_rate[0], out_weight[0]
    ids = jnp.swapaxes(expert_ids[0], 0, 1)
    router_t = jnp.swapaxes(router[0], 0, 1)
    length, heads = q.shape[0], decay.shape[0]
    dh = q.shape[1] // heads
    width = weight.shape[1]
    tokens = residual.shape[1]
    exp_count, ctx_count = lax.axis_size("exp"), lax.axis_size("ctx")
    exp_bits, ctx_bits = exp_count.bit_length() - 1, ctx_count.bit_length() - 1
    per_owner = router.shape[2] // exp_count
    shape = jax.ShapeDtypeStruct

    msg_shape = shape((heads * dh + pad_rows(heads), dh), bf16)
    part = pltpu.VMEM((length, heads * dh), bf16)
    small = pltpu.VMEM(decay.shape, f32)
    dma = pltpu.SemaphoreType.DMA
    msg = call(state_kernel, msg_shape, k, v, decay, specs=[HBM] * 3, scratch=[part, part, small, dma((3,))])
    got = []
    for bit in range(ctx_bits):
        got.append(swap(msg, "ctx", (2 << bit) - 1))
        if bit < ctx_bits - 1:
            msg = call(functools.partial(join_kernel, heads, bit), msg_shape, msg, got[-1])
    inside, slots, weight_near, q_near, growth = call(
        inside_kernel,
        (
            shape((length, heads * dh), f32),
            shape((tokens, LANES), jnp.int32),
            shape(weight.shape, bf16),
            shape(q.shape, bf16),
            shape((length, LANES), f32),
        ),
        q, k, v, decay, ids, weight,
        specs=[HBM] * 6,
        scratch=[part, part, small, pltpu.VMEM(ids.shape, jnp.int32), dma((6,))],
        moved=weight.size * 2,
    )
    base, scale = call(
        functools.partial(base_kernel, heads),
        (shape((length, heads * dh), f32), shape((length, LANES), f32)),
        q_near, inside, growth, *got[:-1],
    )
    order = [sum(((i >> b) & 1) << (exp_bits - 1 - b) for b in range(exp_bits)) for i in range(exp_count)]
    cuts = [width * i // PARTS // LANES * LANES for i in range(PARTS + 1)]
    mixed, groups = None, []
    for start, stop in zip(cuts, cuts[1:]):
        half = shape((length // 2, stop - start), bf16)
        if mixed is None:
            mixed, keep, send = call(
                functools.partial(mix_kernel, heads, order, start, stop),
                (shape((length, heads * dh), bf16), half, half),
                q_near, base, scale, got[-1], weight_near,
                scratch=[part],
                flops=2 * length * heads * dh * (stop - start),
            )
        else:
            keep, send = call(
                functools.partial(project_kernel, start, stop),
                (half, half),
                mixed, weight_near,
                flops=2 * length * heads * dh * (stop - start),
            )
        for bit in range(exp_bits - 1):
            rest = (keep.shape[0] // 2, stop - start)
            send, keep = call(halve_kernel, (shape(rest, bf16), shape(rest, f32)), keep, swap(send, "exp", 1 << bit))
        hidden = call(
            functools.partial(hidden_kernel, start),
            shape((tokens, stop - start), bf16),
            keep, swap(send, "exp", exp_count // 2), residual[0],
        )
        sections = lax.axis_size("section")
        received = lax.ppermute(hidden, "section", [(i, (i + 1) % sections) for i in range(sections)])
        if not groups:
            received = call(tag_kernel, shape((tokens, stop - start + LANES), bf16), received, slots)
        groups.append([received])
        for index in range(1, exp_count):
            groups[-1].append(swap(groups[-1][index & (index - 1)], "exp", index & -index))
    rows_shape = (per_owner, exp_count, CAP, width)
    count = sum(len(pieces(start, stop)) for start, stop in zip(cuts, cuts[1:]))
    all_tokens, experts = exp_count * tokens, per_owner * exp_count
    facts = call(
        functools.partial(ahead_kernel, exp_count, experts),
        (
            shape((all_tokens, experts * CAP), bf16),
            shape((all_tokens, LANES), jnp.int32),
            shape((all_tokens, LANES), f32),
            shape((all_tokens, experts), f32),
        ),
        *groups[0], norm_gain, router_t,
    )
    rows, gates = call(
        functools.partial(place_kernel, exp_count, PARTS),
        (shape(rows_shape, bf16), shape((per_owner, exp_count, CAP), bf16)),
        *[g for part_groups in groups for g in part_groups], *facts, norm_gain, router_t,
        out_specs=(HBM, VMEM),
        scratch=[pltpu.VMEM(rows_shape, bf16), dma((count,))],
    )
    return rows[None, None], gates[None, None]


def solution(mesh):
    placed = (
        P("section", "ctx", "exp"),
        P("section", "ctx", "exp"),
        P("section", "ctx", "exp"),
        P("section", "exp", "ctx"),
        P("section", "exp", None),
        P("section", ("ctx", "exp"), None),
        P("section", None),
        P("section", None, None),
        P("section", ("ctx", "exp"), None),
    )
    return jax.shard_map(
        on_device,
        mesh=mesh,
        in_specs=placed,
        out_specs=(
            P("section", "ctx", "exp", None, None, None),
            P("section", "ctx", "exp", None, None),
        ),
        check_vma=False,
    )
```

time: 48.1 us -> 38.9 us (0.81)
  local copies, waits for them, and re-layouts: 9.1 us -> 0.02 us
  waiting for transfers between devices: 21 us -> 13.6 us
  starting transfers between devices: 11.7 us -> 15.9 us
  Pallas kernels: 4.9 us -> 8.45 us
    unnamed x30 -> x6, local copies, waits for them, and re-layouts: 9.08 us -> 0.02 us
    ppermute x7 -> x12, waiting for transfers between devices: 16.4 us -> 11 us  [swap(): lax.ppermute(block, axis, [(i, i ^ mask) for i in range(lax.axis_size(axi...]
    pallas_call x6 -> x13, Pallas kernels: 4.9 us -> 8.45 us  [call(): pl.pallas_call(kernel, out_shape=out, in_specs=specs, out_specs=out_specs...]
    ppermute x7 -> x12, starting transfers between devices: 10.2 us -> 13 us  [swap(): lax.ppermute(block, axis, [(i, i ^ mask) for i in range(lax.axis_size(axi...]
    ppermute x1 -> x2, waiting for transfers between devices: 4.63 us -> 2.57 us  [on_device(): lax.ppermute(hidden, 'section', [(i, (i + 1) % sections) for i in range(s...]
    ppermute x1 -> x2, starting transfers between devices: 1.55 us -> 2.88 us  [on_device(): lax.ppermute(hidden, 'section', [(i, (i + 1) % sections) for i in range(s...]
  transfers between devices with their start and end apart: 8 -> 14, of which waited for: 6 -> 7; matrix products, arithmetic and copies ran while one was open for 0% -> 0% of each run, Pallas kernels for 2% -> 11%
where the time goes in v2:
time: 38.9 us; the launch traced here: 38.7 us
  starting transfers between devices  15.9 us (41%)
  waiting for transfers between devices  13.6 us (35%)
  Pallas kernels  8.45 us (22%)
  between operations  0.78 us (2%)
    ppermute x12, starting transfers between devices, swap(): lax.ppermute(block, axis, [(i, i ^ mask) for i in range(lax.axis_size(axi...  13 us
    ppermute x12, waiting for transfers between devices, swap(): lax.ppermute(block, axis, [(i, i ^ mask) for i in range(lax.axis_size(axi...  11 us
    pallas_call x13, Pallas kernels, call(): pl.pallas_call(kernel, out_shape=out, in_specs=specs, out_specs=out_specs...  8.45 us
    ppermute x2, starting transfers between devices, on_device(): lax.ppermute(hidden, 'section', [(i, (i + 1) % sections) for i in range(s...  2.88 us
    ppermute x2, waiting for transfers between devices, on_device(): lax.ppermute(hidden, 'section', [(i, (i + 1) % sections) for i in range(s...  2.57 us
  transfers between devices with their start and end apart: 14, of which 7 were waited for; matrix products, arithmetic and copies ran while one was open for 0% of the time, Pallas kernels for 11%

profile of v2, /device:TPU:0, one launch (start us, length us, event | category | flops | bytes accessed | tf_op | source)
XLA Modules:
  0.0 38.7 jit_solution(18252103116939505385)
XLA Ops:
  0.6 1.2 %shard_map.105.own_ref = bf16[528,128]{1,0:T(8,128)(2,1)S(1)} custom-call(bf16[64,512]{1,0:T(8,128)(2,1)} %bitcast.19, bf16[64,512]{1,0:T(8,128)(2,1)} %bitcast.21, f32[4,64]{1,0:T(4,128)} %bitcast.24), custom_call_target="tpu_custom_call" | custom-call | tf_op jit(solution)/shard_map/pallas_call | solution.py:325
  1.9 3.1 %collective-permute-start = (bf16[528,128]{1,0:T(8,128)(2,1)S(1)}, bf16[528,128]{1,0:T(8,128)(2,1)S(1)}, u32[]{:S(2)}, u32[]{:S(2)}) collective-permute-start(bf16[528,128]{1,0:T(8,128)(2,1)S(1)} %shard_map.105.own_ref), channel_id=1, source_target_pairs={{0,4},{4,0},{8,12},{12,8},{1,5},{5,1},{9,13},{13,9},{2,6},{6,2},{1... | collective-permute-start | bytes 405512 | tf_op jit(solution)/shard_map/ppermute | solution.py:318
  5.0 3.6 %collective-permute-done.rest_0_.got_ref = bf16[528,128]{1,0:T(8,128)(2,1)S(1)} collective-permute-done((bf16[528,128]{1,0:T(8,128)(2,1)S(1)}, bf16[528,128]{1,0:T(8,128)(2,1)S(1)}, u32[]{:S(2)}, u32[]{:S(2)}) %collective-permute-start) | collective-permute-done | bytes 135200 | tf_op jit(solution)/shard_map/ppermute | solution.py:318
  8.6 0.1 shard_map.107
  8.6 3.8 %collective-permute-start.1 = (bf16[528,128]{1,0:T(8,128)(2,1)S(1)}, bf16[528,128]{1,0:T(8,128)(2,1)S(1)}, u32[]{:S(2)}, u32[]{:S(2)}) collective-permute-start(bf16[528,128]{1,0:T(8,128)(2,1)S(1)} %shard_map.107), channel_id=1, source_target_pairs={{0,12},{4,8},{8,4},{12,0},{1,13},{5,9},{9,5},{13,1},{2,14},{6,10},... | collective-permute-start | bytes 405512 | tf_op jit(solution)/shard_map/ppermute | solution.py:318
  12.5 3.0 %shard_map.104 = (f32[64,512]{1,0:T(8,128)S(1)}, s32[16,128]{1,0:T(8,128)S(1)}, bf16[512,6144]{1,0:T(8,128)(2,1)S(1)}, bf16[64,512]{1,0:T(8,128)(2,1)S(1)}, f32[64,128]{1,0:T(8,128)S(1)}) custom-call(bf16[64,512]{1,0:T(8,128)(2,1)} %bitcast.23, bf16[64,512]{1,0:T(8,128)(2,1)} %bitcast.20, bf16[64,512]{1,0:T(8,128)(2,1)} %bitcast.22, f32[4,64]{1,0:T(4,128)} %bitcast.25, ...), custom_call_target="tpu_custom_call" | custom-call | bytes 6291456 | tf_op jit(solution)/shard_map/pallas_call | solution.py:325
  15.4 0.2 shard_map.106
  15.7 0.0 collective-permute-done.1.got_ref
  15.7 0.0 copy-start
  15.7 0.0 copy-start.1
  15.7 0.0 copy-start.2
  15.7 0.8 %shard_map.108 = (bf16[64,512]{1,0:T(8,128)(2,1)S(1)}, bf16[32,3072]{1,0:T(8,128)(2,1)S(1)}, bf16[32,3072]{1,0:T(8,128)(2,1)S(1)}) custom-call(bf16[64,512]{1,0:T(8,128)(2,1)S(1)} %get-tuple-element.24.q_ref, f32[64,512]{1,0:T(8,128)S(1)} %get-tuple-element.27.base_ref, f32[64,128]{1,0:T(8,128)S(1)} %get-tuple-element.28.scale_ref, ...), custom_call_target="tpu_custom_call" | custom-call | flops 201326592 | tf_op jit(solution)/shard_map/pallas_call | solution.py:325
  16.5 0.1 collective-permute-start.2
  16.6 0.7 %shard_map.112 = (bf16[32,3072]{1,0:T(8,128)(2,1)S(1)}, bf16[32,3072]{1,0:T(8,128)(2,1)S(1)}) custom-call(bf16[64,512]{1,0:T(8,128)(2,1)S(1)} %get-tuple-element.35.mixed_ref, bf16[512,6144]{1,0:T(8,128)(2,1)S(1)} %get-tuple-element.29.weight_ref), custom_call_target="tpu_custom_call" | custom-call | flops 201326592 | tf_op jit(solution)/shard_map/pallas_call | solution.py:325
  17.3 0.6 %collective-permute-start.8 = (bf16[32,3072]{1,0:T(8,128)(2,1)S(1)}, bf16[32,3072]{1,0:T(8,128)(2,1)S(1)}, u32[]{:S(2)}, u32[]{:S(2)}) collective-permute-start(bf16[32,3072]{1,0:T(8,128)(2,1)S(1)} %get-tuple-element.37), channel_id=1, source_target_pairs={{0,1},{1,0},{2,3},{3,2},{4,5},{5,4},{6,7},{7,6},{8,9},{9,8},{10,11... | collective-permute-start | bytes 589832 | tf_op jit(solution)/shard_map/ppermute | solution.py:318
  17.8 0.2 collective-permute-done.2.got_ref
  18.1 1.6 %collective-permute-start.3 = (bf16[16,3072]{1,0:T(8,128)(2,1)S(1)}, bf16[16,3072]{1,0:T(8,128)(2,1)S(1)}, u32[]{:S(2)}, u32[]{:S(2)}) collective-permute-start(bf16[16,3072]{1,0:T(8,128)(2,1)S(1)} %get-tuple-element.33), channel_id=1, source_target_pairs={{0,2},{1,3},{2,0},{3,1},{4,6},{5,7},{6,4},{7,5},{8,10},{9,11},{10,... | collective-permute-start | bytes 294920 | tf_op jit(solution)/shard_map/ppermute | solution.py:318
  19.7 0.0 collective-permute-done.8.got_ref
  19.7 0.8 %collective-permute-start.9 = (bf16[16,3072]{1,0:T(8,128)(2,1)S(1)}, bf16[16,3072]{1,0:T(8,128)(2,1)S(1)}, u32[]{:S(2)}, u32[]{:S(2)}) collective-permute-start(bf16[16,3072]{1,0:T(8,128)(2,1)S(1)} %get-tuple-element.39), channel_id=1, source_target_pairs={{0,2},{1,3},{2,0},{3,1},{4,6},{5,7},{6,4},{7,5},{8,10},{9,11},{10,... | collective-permute-start | bytes 294920 | tf_op jit(solution)/shard_map/ppermute | solution.py:318
  20.6 3.2 %collective-permute-done.3.got_ref = bf16[16,3072]{1,0:T(8,128)(2,1)S(1)} collective-permute-done((bf16[16,3072]{1,0:T(8,128)(2,1)S(1)}, bf16[16,3072]{1,0:T(8,128)(2,1)S(1)}, u32[]{:S(2)}, u32[]{:S(2)}) %collective-permute-start.3) | collective-permute-done | bytes 98336 | tf_op jit(solution)/shard_map/ppermute | solution.py:318
  23.7 0.0 copy-done
  23.8 1.6 %collective-permute-start.4 = (bf16[16,3072]{1,0:T(8,128)(2,1)S(1)}, bf16[16,3072]{1,0:T(8,128)(2,1)S(1)}, u32[]{:S(2)}, u32[]{:S(2)}) collective-permute-start(bf16[16,3072]{1,0:T(8,128)(2,1)S(1)} %shard_map.110), channel_id=1, source_target_pairs={{0,16},{16,0},{1,17},{17,1},{2,18},{18,2},{3,19},{19,3},{4,20},{20... | collective-permute-start | bytes 294920 | tf_op jit(solution)/shard_map/ppermute | solution.py:407
  25.3 0.0 collective-permute-done.9.got_ref
  25.4 1.3 %collective-permute-start.10 = (bf16[16,3072]{1,0:T(8,128)(2,1)S(1)}, bf16[16,3072]{1,0:T(8,128)(2,1)S(1)}, u32[]{:S(2)}, u32[]{:S(2)}) collective-permute-start(bf16[16,3072]{1,0:T(8,128)(2,1)S(1)} %shard_map.114), channel_id=1, source_target_pairs={{0,16},{16,0},{1,17},{17,1},{2,18},{18,2},{3,19},{19,3},{4,20},{20... | collective-permute-start | bytes 294920 | tf_op jit(solution)/shard_map/ppermute | solution.py:407
  26.7 2.6 %collective-permute-done.4.got_ref = bf16[16,3072]{1,0:T(8,128)(2,1)S(1)} collective-permute-done((bf16[16,3072]{1,0:T(8,128)(2,1)S(1)}, bf16[16,3072]{1,0:T(8,128)(2,1)S(1)}, u32[]{:S(2)}, u32[]{:S(2)}) %collective-permute-start.4) | collective-permute-done | bytes 98336 | tf_op jit(solution)/shard_map/ppermute | solution.py:407
  29.3 1.5 %collective-permute-start.6 = (bf16[16,3200]{1,0:T(8,128)(2,1)S(1)}, bf16[16,3200]{1,0:T(8,128)(2,1)S(1)}, u32[]{:S(2)}, u32[]{:S(2)}) collective-permute-start(bf16[16,3200]{1,0:T(8,128)(2,1)S(1)} %shard_map.111.refs_0_), channel_id=1, source_target_pairs={{0,2},{1,3},{2,0},{3,1},{4,6},{5,7},{6,4},{7,5},{8,10},{9,11},{10,... | collective-permute-start | bytes 307208 | tf_op jit(solution)/shard_map/ppermute | solution.py:318
  30.8 0.0 collective-permute-done.10.refs_4_
  30.8 1.0 %collective-permute-start.12 = (bf16[16,3072]{1,0:T(8,128)(2,1)S(1)}, bf16[16,3072]{1,0:T(8,128)(2,1)S(1)}, u32[]{:S(2)}, u32[]{:S(2)}) collective-permute-start(bf16[16,3072]{1,0:T(8,128)(2,1)S(1)} %collective-permute-done.10.refs_4_), channel_id=1, source_target_pairs={{0,2},{1,3},{2,0},{3,1},{4,6},{5,7},{6,4},{7,5},{8,10},{9,11},{10,... | collective-permute-start | bytes 294920 | tf_op jit(solution)/shard_map/ppermute | solution.py:318
  31.8 0.0 collective-permute-start.5
  31.8 2.2 %collective-permute-done.6.refs_2_ = bf16[16,3200]{1,0:T(8,128)(2,1)S(1)} collective-permute-done((bf16[16,3200]{1,0:T(8,128)(2,1)S(1)}, bf16[16,3200]{1,0:T(8,128)(2,1)S(1)}, u32[]{:S(2)}, u32[]{:S(2)}) %collective-permute-start.6) | collective-permute-done | bytes 102432 | tf_op jit(solution)/shard_map/ppermute | solution.py:318
  34.0 0.0 collective-permute-start.7
  34.0 0.5 %collective-permute-start.11 = (bf16[16,3072]{1,0:T(8,128)(2,1)S(1)}, bf16[16,3072]{1,0:T(8,128)(2,1)S(1)}, u32[]{:S(2)}, u32[]{:S(2)}) collective-permute-start(bf16[16,3072]{1,0:T(8,128)(2,1)S(1)} %collective-permute-done.10.refs_4_), channel_id=1, source_target_pairs={{0,1},{1,0},{2,3},{3,2},{4,5},{5,4},{6,7},{7,6},{8,9},{9,8},{10,11... | collective-permute-start | bytes 294920 | tf_op jit(solution)/shard_map/ppermute | solution.py:318
  34.5 0.9 %collective-permute-done.12.refs_6_ = bf16[16,3072]{1,0:T(8,128)(2,1)S(1)} collective-permute-done((bf16[16,3072]{1,0:T(8,128)(2,1)S(1)}, bf16[16,3072]{1,0:T(8,128)(2,1)S(1)}, u32[]{:S(2)}, u32[]{:S(2)}) %collective-permute-start.12) | collective-permute-done | bytes 98336 | tf_op jit(solution)/shard_map/ppermute | solution.py:318
  35.4 0.0 collective-permute-start.13
  35.4 0.0 collective-permute-done.5.refs_1_
  35.4 0.0 collective-permute-done.7.refs_3_
  35.4 0.0 copy-done.1
  35.4 0.0 copy-done.2
  35.5 0.3 shard_map.115
  35.8 0.0 collective-permute-done.11.refs_5_
  35.8 0.9 %collective-permute-done.13.refs_7_ = bf16[16,3072]{1,0:T(8,128)(2,1)S(1)} collective-permute-done((bf16[16,3072]{1,0:T(8,128)(2,1)S(1)}, bf16[16,3072]{1,0:T(8,128)(2,1)S(1)}, u32[]{:S(2)}, u32[]{:S(2)}) %collective-permute-start.13) | collective-permute-done | bytes 98336 | tf_op jit(solution)/shard_map/ppermute | solution.py:318
  36.7 2.0 %shard_map.116 = (bf16[4,4,4,6144]{3,2,1,0:T(4,128)(2,1)}, bf16[4,4,4]{2,1,0:T(4,128)(2,1)}) custom-call(bf16[16,3200]{1,0:T(8,128)(2,1)S(1)} %shard_map.111.refs_0_, bf16[16,3200]{1,0:T(8,128)(2,1)S(1)} %collective-permute-done.5.refs_1_, bf16[16,3200]{1,0:T(8,128)(2,1)S(1)} %collective-permute-done.6.refs_2_, ...), custom_call_target="tpu_custom_call" | custom-call | tf_op jit(solution)/shard_map/pallas_call | solution.py:325
  (5 shorter events, 0.2 us)
Async XLA Ops:
  1.9 6.7 %collective-permute-start = (bf16[528,128]{1,0:T(8,128)(2,1)S(1)}, bf16[528,128]{1,0:T(8,128)(2,1)S(1)}, u32[]{:S(2)}, u32[]{:S(2)}) collective-permute-start(bf16[528,128]{1,0:T(8,128)(2,1)S(1)} %shard_map.105.own_ref), channel_id=1, source_target_pairs={{0,4},{4,0},{8,12},{12,8},{1,5},{5,1},{9,13},{13,9},{2,6},{6,2},{1... | collective-permute-start | bytes 405512 | tf_op jit(solution)/shard_map/ppermute | solution.py:318
  8.6 7.1 %collective-permute-start.1 = (bf16[528,128]{1,0:T(8,128)(2,1)S(1)}, bf16[528,128]{1,0:T(8,128)(2,1)S(1)}, u32[]{:S(2)}, u32[]{:S(2)}) collective-permute-start(bf16[528,128]{1,0:T(8,128)(2,1)S(1)} %shard_map.107), channel_id=1, source_target_pairs={{0,12},{4,8},{8,4},{12,0},{1,13},{5,9},{9,5},{13,1},{2,14},{6,10},... | collective-permute-start | bytes 405512 | tf_op jit(solution)/shard_map/ppermute | solution.py:318
  15.7 8.0 %copy-start = (bf16[1,16,6144]{2,1,0:T(8,128)(2,1)S(1)}, bf16[1,16,6144]{2,1,0:T(8,128)(2,1)}, u32[]{:S(2)}) copy-start(bf16[1,16,6144]{2,1,0:T(8,128)(2,1)} %param.14) | copy-start | bytes 589828
  15.7 19.7 %copy-start.1 = (bf16[1,6144,16]{1,2,0:T(8,128)(2,1)S(1)}, bf16[1,6144,16]{1,2,0:T(8,128)(2,1)}, u32[]{:S(2)}) copy-start(bf16[1,6144,16]{1,2,0:T(8,128)(2,1)} %param.16) | copy-start | bytes 589828
  15.7 19.7 %copy-start.2 = (f32[1,6144]{1,0:T(1,128)S(1)}, f32[1,6144]{1,0:T(1,128)}, u32[]{:S(2)}) copy-start(f32[1,6144]{1,0:T(1,128)} %refs_12_.1) | copy-start | bytes 73732
  16.5 1.5 %collective-permute-start.2 = (bf16[32,3072]{1,0:T(8,128)(2,1)S(1)}, bf16[32,3072]{1,0:T(8,128)(2,1)S(1)}, u32[]{:S(2)}, u32[]{:S(2)}) collective-permute-start(bf16[32,3072]{1,0:T(8,128)(2,1)S(1)} %get-tuple-element.31), channel_id=1, source_target_pairs={{0,1},{1,0},{2,3},{3,2},{4,5},{5,4},{6,7},{7,6},{8,9},{9,8},{10,11... | collective-permute-start | bytes 589832 | tf_op jit(solution)/shard_map/ppermute | solution.py:318
  17.3 2.4 %collective-permute-start.8 = (bf16[32,3072]{1,0:T(8,128)(2,1)S(1)}, bf16[32,3072]{1,0:T(8,128)(2,1)S(1)}, u32[]{:S(2)}, u32[]{:S(2)}) collective-permute-start(bf16[32,3072]{1,0:T(8,128)(2,1)S(1)} %get-tuple-element.37), channel_id=1, source_target_pairs={{0,1},{1,0},{2,3},{3,2},{4,5},{5,4},{6,7},{7,6},{8,9},{9,8},{10,11... | collective-permute-start | bytes 589832 | tf_op jit(solution)/shard_map/ppermute | solution.py:318
  18.1 5.7 %collective-permute-start.3 = (bf16[16,3072]{1,0:T(8,128)(2,1)S(1)}, bf16[16,3072]{1,0:T(8,128)(2,1)S(1)}, u32[]{:S(2)}, u32[]{:S(2)}) collective-permute-start(bf16[16,3072]{1,0:T(8,128)(2,1)S(1)} %get-tuple-element.33), channel_id=1, source_target_pairs={{0,2},{1,3},{2,0},{3,1},{4,6},{5,7},{6,4},{7,5},{8,10},{9,11},{10,... | collective-permute-start | bytes 294920 | tf_op jit(solution)/shard_map/ppermute | solution.py:318
  19.7 5.6 %collective-permute-start.9 = (bf16[16,3072]{1,0:T(8,128)(2,1)S(1)}, bf16[16,3072]{1,0:T(8,128)(2,1)S(1)}, u32[]{:S(2)}, u32[]{:S(2)}) collective-permute-start(bf16[16,3072]{1,0:T(8,128)(2,1)S(1)} %get-tuple-element.39), channel_id=1, source_target_pairs={{0,2},{1,3},{2,0},{3,1},{4,6},{5,7},{6,4},{7,5},{8,10},{9,11},{10,... | collective-permute-start | bytes 294920 | tf_op jit(solution)/shard_map/ppermute | solution.py:318
  23.8 5.5 %collective-permute-start.4 = (bf16[16,3072]{1,0:T(8,128)(2,1)S(1)}, bf16[16,3072]{1,0:T(8,128)(2,1)S(1)}, u32[]{:S(2)}, u32[]{:S(2)}) collective-permute-start(bf16[16,3072]{1,0:T(8,128)(2,1)S(1)} %shard_map.110), channel_id=1, source_target_pairs={{0,16},{16,0},{1,17},{17,1},{2,18},{18,2},{3,19},{19,3},{4,20},{20... | collective-permute-start | bytes 294920 | tf_op jit(solution)/shard_map/ppermute | solution.py:407
  25.4 5.4 %collective-permute-start.10 = (bf16[16,3072]{1,0:T(8,128)(2,1)S(1)}, bf16[16,3072]{1,0:T(8,128)(2,1)S(1)}, u32[]{:S(2)}, u32[]{:S(2)}) collective-permute-start(bf16[16,3072]{1,0:T(8,128)(2,1)S(1)} %shard_map.114), channel_id=1, source_target_pairs={{0,16},{16,0},{1,17},{17,1},{2,18},{18,2},{3,19},{19,3},{4,20},{20... | collective-permute-start | bytes 294920 | tf_op jit(solution)/shard_map/ppermute | solution.py:407
  29.3 4.7 %collective-permute-start.6 = (bf16[16,3200]{1,0:T(8,128)(2,1)S(1)}, bf16[16,3200]{1,0:T(8,128)(2,1)S(1)}, u32[]{:S(2)}, u32[]{:S(2)}) collective-permute-start(bf16[16,3200]{1,0:T(8,128)(2,1)S(1)} %shard_map.111.refs_0_), channel_id=1, source_target_pairs={{0,2},{1,3},{2,0},{3,1},{4,6},{5,7},{6,4},{7,5},{8,10},{9,11},{10,... | collective-permute-start | bytes 307208 | tf_op jit(solution)/shard_map/ppermute | solution.py:318
  30.8 4.6 %collective-permute-start.12 = (bf16[16,3072]{1,0:T(8,128)(2,1)S(1)}, bf16[16,3072]{1,0:T(8,128)(2,1)S(1)}, u32[]{:S(2)}, u32[]{:S(2)}) collective-permute-start(bf16[16,3072]{1,0:T(8,128)(2,1)S(1)} %collective-permute-done.10.refs_4_), channel_id=1, source_target_pairs={{0,2},{1,3},{2,0},{3,1},{4,6},{5,7},{6,4},{7,5},{8,10},{9,11},{10,... | collective-permute-start | bytes 294920 | tf_op jit(solution)/shard_map/ppermute | solution.py:318
  31.8 3.7 %collective-permute-start.5 = (bf16[16,3200]{1,0:T(8,128)(2,1)S(1)}, bf16[16,3200]{1,0:T(8,128)(2,1)S(1)}, u32[]{:S(2)}, u32[]{:S(2)}) collective-permute-start(bf16[16,3200]{1,0:T(8,128)(2,1)S(1)} %shard_map.111.refs_0_), channel_id=1, source_target_pairs={{0,1},{1,0},{2,3},{3,2},{4,5},{5,4},{6,7},{7,6},{8,9},{9,8},{10,11... | collective-permute-start | bytes 307208 | tf_op jit(solution)/shard_map/ppermute | solution.py:318
  34.0 1.4 %collective-permute-start.7 = (bf16[16,3200]{1,0:T(8,128)(2,1)S(1)}, bf16[16,3200]{1,0:T(8,128)(2,1)S(1)}, u32[]{:S(2)}, u32[]{:S(2)}) collective-permute-start(bf16[16,3200]{1,0:T(8,128)(2,1)S(1)} %collective-permute-done.6.refs_2_), channel_id=1, source_target_pairs={{0,1},{1,0},{2,3},{3,2},{4,5},{5,4},{6,7},{7,6},{8,9},{9,8},{10,11... | collective-permute-start | bytes 307208 | tf_op jit(solution)/shard_map/ppermute | solution.py:318
  34.0 1.8 %collective-permute-start.11 = (bf16[16,3072]{1,0:T(8,128)(2,1)S(1)}, bf16[16,3072]{1,0:T(8,128)(2,1)S(1)}, u32[]{:S(2)}, u32[]{:S(2)}) collective-permute-start(bf16[16,3072]{1,0:T(8,128)(2,1)S(1)} %collective-permute-done.10.refs_4_), channel_id=1, source_target_pairs={{0,1},{1,0},{2,3},{3,2},{4,5},{5,4},{6,7},{7,6},{8,9},{9,8},{10,11... | collective-permute-start | bytes 294920 | tf_op jit(solution)/shard_map/ppermute | solution.py:318
  35.4 1.3 %collective-permute-start.13 = (bf16[16,3072]{1,0:T(8,128)(2,1)S(1)}, bf16[16,3072]{1,0:T(8,128)(2,1)S(1)}, u32[]{:S(2)}, u32[]{:S(2)}) collective-permute-start(bf16[16,3072]{1,0:T(8,128)(2,1)S(1)} %collective-permute-done.12.refs_6_), channel_id=1, source_target_pairs={{0,1},{1,0},{2,3},{3,2},{4,5},{5,4},{6,7},{7,6},{8,9},{9,8},{10,11... | collective-permute-start | bytes 294920 | tf_op jit(solution)/shard_map/ppermute | solution.py:318

commit v3 on v2

--- a/solution.py
+++ b/solution.py
@@ -181,7 +181,7 @@
     scale_ref[...] = scale
 
 
-def mix_kernel(heads, order, start, stop, q_ref, base_ref, scale_ref, got_ref, weight_ref, mixed_ref, keep_ref, send_ref, attended):
+def mix_kernel(heads, order, stop, q_ref, base_ref, scale_ref, got_ref, weight_ref, slots_ref, mixed_ref, keep_ref, send_ref, attended):
     dh = base_ref.shape[1] // heads
     me = lax.axis_index("exp")
     for h in range(heads):
@@ -191,7 +191,8 @@
     share = base_ref.shape[0] // len(order)
     for i, k in enumerate(order):
         mixed_ref[i * share : (i + 1) * share, :] = attended[pl.ds(pl.multiple_of((me ^ k) * share, share), share), :]
-    project_kernel(start, stop, mixed_ref, weight_ref, keep_ref, send_ref)
+    project_kernel(0, stop, mixed_ref, weight_ref, keep_ref, send_ref)
+    put_lanes(send_ref, slots_ref[...].astype(f32))
 
 
 def project_kernel(start, stop, mixed_ref, weight_ref, keep_ref, send_ref):
@@ -207,50 +208,77 @@
     return [(at, min(at + step, stop)) for at in range(start, stop, step)]
 
 
-def halve_kernel(keep_ref, got_ref, send_ref, own_ref):
-    half = own_ref.shape[0]
-    own_ref[...] = keep_ref[:half, :].astype(f32) + got_ref[:half, :].astype(f32)
-    send_ref[...] = (keep_ref[half:, :].astype(f32) + got_ref[half:, :].astype(f32)).astype(bf16)
-
-
-def hidden_kernel(start, own_ref, got_ref, residual_ref, out_ref):
-    stop = start + own_ref.shape[1]
-    total = own_ref[...].astype(f32) + got_ref[...].astype(f32)
-    out_ref[...] = (residual_ref[:, start:stop].astype(f32) + total).astype(bf16)
-
-
-def tag_kernel(got_ref, slots_ref, msg_ref):
-    size = got_ref.shape[1]
-    msg_ref[:, :size] = got_ref[...]
-    msg_ref[:, size:] = slots_ref[...].astype(f32).astype(bf16)
-
-
-def partial(groups, gain, router, start):
-    square, logits = 0.0, 0.0
-    for at, to in pieces(0, groups[0].shape[1] // LANES * LANES):
+def put_lanes(ref, lanes):
+    tokens = lanes.shape[0]
+    ref[:tokens, -LANES:] = lanes.astype(bf16)
+    if ref.shape[0] > tokens:
+        ref[tokens:, -LANES:] = jnp.zeros((ref.shape[0] - tokens, LANES), bf16)
+
+
+def widen_lanes(bit, tokens, sent_ref, got_ref):
+    own, got = sent_ref[:tokens, -LANES:].astype(f32), got_ref[:tokens, -LANES:].astype(f32)
+    filled = 2 << bit
+    return jnp.where(iota(own.shape, 1) < filled, own, jnp.roll(got, filled, axis=1))
+
+
+def halve_kernel(bit, tokens, tagged, keep_ref, sent_ref, got_ref, send_ref, own_ref):
+    half, width = own_ref.shape
+    own_ref[...] = keep_ref[:half, :].astype(f32) + got_ref[:half, :width].astype(f32)
+    send_ref[:, :width] = (keep_ref[half:, :].astype(f32) + got_ref[half:, :width].astype(f32)).astype(bf16)
+    if tagged:
+        put_lanes(send_ref, widen_lanes(bit, tokens, sent_ref, got_ref))
+
+
+def carry_kernel(bit, start, tagged, keep_ref, sent_ref, got_ref, residual_ref, out_ref):
+    tokens = residual_ref.shape[0]
+    width = keep_ref.shape[1]
+    total = keep_ref[...].astype(f32) + got_ref[:, :width].astype(f32)
+    own = total[:tokens] + residual_ref[:, start : start + width].astype(f32)
+    out_ref[:tokens, :width] = own.astype(bf16)
+    out_ref[tokens:, :width] = total[tokens:].astype(bf16)
+    if tagged:
+        put_lanes(out_ref, widen_lanes(bit, tokens, sent_ref, got_ref))
+
+
+def combine_kernel(own_ref, got_ref, out_ref):
+    rows, width = out_ref.shape
+    half = rows // 2
+    out_ref[:half, :] = (own_ref[:half, :width].astype(f32) + got_ref[half:, :width].astype(f32)).astype(bf16)
+    out_ref[half:, :] = (own_ref[half:, :width].astype(f32) + got_ref[:half, :width].astype(f32)).astype(bf16)
+
+
+def squares(groups, size):
+    total = 0.0
+    for at, to in pieces(0, size):
         wide = jnp.concatenate([g[:, at:to] for g in groups], axis=0).astype(f32)
-        square += jnp.sum(wide * wide, axis=1, keepdims=True)
+        total += jnp.sum(wide * wide, axis=1, keepdims=True)
+    return total
+
+
+def products(groups, size, gain, router, start):
+    total = 0.0
+    for at, to in pieces(0, size):
+        wide = jnp.concatenate([g[:, at:to] for g in groups], axis=0).astype(f32)
         gained = (wide * gain[:, start + at : start + to]).astype(bf16)
-        logits += mm(gained, router[:, start + at : start + to], NT)
-    return square, logits
-
-
-def ahead_kernel(exp_count, experts, *refs):
-    groups, (gain_ref, router_ref, chosen_ref, target_ref, square_ref, logits_ref) = refs[:exp_count], refs[exp_count:]
-    size = groups[0].shape[1] - LANES
+        total += mm(gained, router[:, start + at : start + to], NT)
+    return total
+
+
+def facts_kernel(exp_count, experts, tokens, own_ref, got_ref, chosen_ref, target_ref):
     per_owner = experts // exp_count
+    top = exp_count // 2
     me = lax.axis_index("exp")
-    tokens = groups[0].shape[0]
+    lanes = [ref[:tokens, -LANES:].astype(f32).astype(jnp.int32) for ref in (own_ref, got_ref)]
     wheres, named = [[], []], [[], []]
-    for k in range(exp_count):
-        sender = me ^ k
-        meta = groups[k][:, size:].astype(f32).astype(jnp.int32)
-        for c in range(2):
-            slot = meta[:, c : c + 1]
-            place = slot - me * (per_owner * CAP)
-            mine = (place >= 0) & (place < per_owner * CAP)
-            wheres[c].append(jnp.where(mine, (place // CAP * exp_count + sender) * CAP + place % CAP, -1))
-            named[c].append(slot // CAP)
+    for j in range(top):
+        for side in range(2):
+            sender = me ^ (j + side * top)
+            for c in range(2):
+                slot = lanes[side][:, 2 * j + c : 2 * j + c + 1]
+                place = slot - me * (per_owner * CAP)
+                mine = (place >= 0) & (place < per_owner * CAP)
+                wheres[c].append(jnp.where(mine, (place // CAP * exp_count + sender) * CAP + place % CAP, -1))
+                named[c].append(slot // CAP)
     wheres = [jnp.concatenate(w, axis=0) for w in wheres]
     named = [jnp.concatenate(n, axis=0) for n in named]
     total = tokens * exp_count
@@ -261,36 +289,32 @@
     for i, column in enumerate(wheres + named):
         target = jnp.where(lane == i, column, target)
     target_ref[...] = target
-    square, logits = partial([g.at[:, :size] for g in groups], gain_ref, router_ref, 0)
-    square_ref[...] = jnp.broadcast_to(square, square_ref.shape)
-    logits_ref[...] = logits
-
-
-def place_kernel(exp_count, parts, *refs):
-    groups = [refs[i * exp_count : (i + 1) * exp_count] for i in range(parts)]
-    chosen_ref, target_ref, square_ref, logits_ref, gain_ref, router_ref, rows_hbm, gates_ref, rows_ref, sems = refs[parts * exp_count :]
+
+
+def ahead_kernel(count, *refs):
+    blocks, (gain_ref, router_ref, square_ref, logits_ref) = refs[:count], refs[count:]
+    size = blocks[0].shape[1]
+    square_ref[...] = jnp.broadcast_to(squares(blocks, size), square_ref.shape)
+    logits_ref[...] = products(blocks, size, gain_ref, router_ref, 0)
+
+
+def place_kernel(count, parts, *refs):
+    groups = [refs[i * count : (i + 1) * count] for i in range(parts)]
+    exp_count = 2 * count
+    chosen_ref, target_ref, square_ref, logits_ref, gain_ref, router_ref, *outs = refs[parts * count :]
+    rows_hbm, gates_hbm, rows_ref, gates_ref, sems = outs
     per_owner, _, cap, width = rows_ref.shape
     sizes = [part[0].shape[1] for part in groups]
-    sizes[0] -= LANES
-    square, logits = square_ref[:, :1], logits_ref[...]
-    at = sizes[0]
+    square = square_ref[:, :1]
     for part, size in zip(groups[1:], sizes[1:]):
-        more = partial(part, gain_ref, router_ref, at)
-        square, logits = square + more[0], logits + more[1]
-        at += size
+        square += squares(part, size)
     factor = lax.rsqrt(square * (1.0 / width) + EPSILON)
     chosen = chosen_ref[...]
     copies = []
-    at = 0
-    for part, size in zip(groups, sizes):
-        for start, stop in pieces(0, size):
-            wide = jnp.concatenate([g[:, start:stop] for g in part], axis=0).astype(f32)
-            normed = (wide * factor * gain_ref[:, at + start : at + stop]).astype(bf16)
-            out = mm(chosen, normed, TN).astype(bf16)
-            window = (slice(None), slice(None), slice(None), slice(at + start, at + stop))
-            rows_ref[window] = out.reshape(per_owner, exp_count, cap, stop - start)
-            copies.append(pltpu.make_async_copy(rows_ref.at[window], rows_hbm.at[window], sems.at[len(copies)]))
-            copies[-1].start()
+    logits = logits_ref[...]
+    at = sizes[0]
+    for part, size in zip(groups[1:], sizes[1:]):
+        logits += products(part, size, gain_ref, router_ref, at)
         at += size
     logits = logits * factor
     target = target_ref[...]
@@ -310,6 +334,19 @@
     gate_rows = gate_rows.astype(bf16)
     for e in range(per_owner):
         gates_ref[e] = gate_rows[e * exp_count : (e + 1) * exp_count, :cap]
+    copies.append(pltpu.make_async_copy(gates_ref, gates_hbm, sems.at[len(copies)]))
+    copies[-1].start()
+    at = 0
+    for part, size in zip(groups, sizes):
+        for start, stop in pieces(0, size):
+            wide = jnp.concatenate([g[:, start:stop] for g in part], axis=0).astype(f32)
+            normed = (wide * factor * gain_ref[:, at + start : at + stop]).astype(bf16)
+            out = mm(chosen, normed, TN).astype(bf16)
+            window = (slice(None), slice(None), slice(None), slice(at + start, at + stop))
+            rows_ref[window] = out.reshape(per_owner, exp_count, cap, stop - start)
+            copies.append(pltpu.make_async_copy(rows_ref.at[window], rows_hbm.at[window], sems.at[len(copies)]))
+            copies[-1].start()
+        at += size
     for copy in copies:
         copy.wait()
 
@@ -377,58 +414,71 @@
     )
     order = [sum(((i >> b) & 1) << (exp_bits - 1 - b) for b in range(exp_bits)) for i in range(exp_count)]
     cuts = [width * i // PARTS // LANES * LANES for i in range(PARTS + 1)]
+    sections = lax.axis_size("section")
+    top = exp_count // 2
+
+    def relay(block):
+        return lax.ppermute(block, "section", [(i, (i + 1) % sections) for i in range(sections)])
+
     mixed, groups = None, []
     for start, stop in zip(cuts, cuts[1:]):
-        half = shape((length // 2, stop - start), bf16)
-        if mixed is None:
+        first = mixed is None
+        size = stop - start
+        extra = LANES if first else 0
+        halves = (shape((length // 2, size), bf16), shape((length // 2, size + extra), bf16))
+        cost = 2 * length * heads * dh * size
+        if first:
             mixed, keep, send = call(
-                functools.partial(mix_kernel, heads, order, start, stop),
-                (shape((length, heads * dh), bf16), half, half),
-                q_near, base, scale, got[-1], weight_near,
+                functools.partial(mix_kernel, heads, order, stop),
+                (shape((length, heads * dh), bf16), *halves),
+                q_near, base, scale, got[-1], weight_near, slots,
                 scratch=[part],
-                flops=2 * length * heads * dh * (stop - start),
+                flops=cost,
             )
         else:
-            keep, send = call(
-                functools.partial(project_kernel, start, stop),
-                (half, half),
-                mixed, weight_near,
-                flops=2 * length * heads * dh * (stop - start),
+            keep, send = call(functools.partial(project_kernel, start, stop), halves, mixed, weight_near, flops=cost)
+        for bit in range(exp_bits - 2):
+            rest = keep.shape[0] // 2
+            send, keep = call(
+                functools.partial(halve_kernel, bit, tokens, first),
+                (shape((rest, size + extra), bf16), shape((rest, size), f32)),
+                keep, send, swap(send, "exp", 1 << bit),
             )
-        for bit in range(exp_bits - 1):
-            rest = (keep.shape[0] // 2, stop - start)
-            send, keep = call(halve_kernel, (shape(rest, bf16), shape(rest, f32)), keep, swap(send, "exp", 1 << bit))
-        hidden = call(
-            functools.partial(hidden_kernel, start),
-            shape((tokens, stop - start), bf16),
-            keep, swap(send, "exp", exp_count // 2), residual[0],
+        own = call(
+            functools.partial(carry_kernel, exp_bits - 2, start, first),
+            shape((2 * tokens, size + extra), bf16),
+            keep, send, swap(send, "exp", top // 2), residual[0],
         )
-        sections = lax.axis_size("section")
-        received = lax.ppermute(hidden, "section", [(i, (i + 1) % sections) for i in range(sections)])
-        if not groups:
-            received = call(tag_kernel, shape((tokens, stop - start + LANES), bf16), received, slots)
-        groups.append([received])
-        for index in range(1, exp_count):
+        whole = shape((2 * tokens, size), bf16)
+        if first:
+            other = swap(own, "exp", top)
+            tagged = (own, other)
+            block = relay(call(combine_kernel, whole, own, other))
+        else:
+            own = relay(own)
+            block = call(combine_kernel, whole, own, swap(own, "exp", top))
+        groups.append([block])
+        for index in range(1, top):
             groups[-1].append(swap(groups[-1][index & (index - 1)], "exp", index & -index))
     rows_shape = (per_owner, exp_count, CAP, width)
     count = sum(len(pieces(start, stop)) for start, stop in zip(cuts, cuts[1:]))
     all_tokens, experts = exp_count * tokens, per_owner * exp_count
     facts = call(
-        functools.partial(ahead_kernel, exp_count, experts),
-        (
-            shape((all_tokens, experts * CAP), bf16),
-            shape((all_tokens, LANES), jnp.int32),
-            shape((all_tokens, LANES), f32),
-            shape((all_tokens, experts), f32),
-        ),
+        functools.partial(facts_kernel, exp_count, experts, tokens),
+        (shape((all_tokens, per_owner * exp_count * CAP), bf16), shape((all_tokens, LANES), jnp.int32)),
+        *tagged,
+    )
+    sums = call(
+        functools.partial(ahead_kernel, top),
+        (shape((all_tokens, LANES), f32), shape((all_tokens, experts), f32)),
         *groups[0], norm_gain, router_t,
     )
     rows, gates = call(
-        functools.partial(place_kernel, exp_count, PARTS),
+        functools.partial(place_kernel, top, PARTS),
         (shape(rows_shape, bf16), shape((per_owner, exp_count, CAP), bf16)),
-        *[g for part_groups in groups for g in part_groups], *facts, norm_gain, router_t,
-        out_specs=(HBM, VMEM),
-        scratch=[pltpu.VMEM(rows_shape, bf16), dma((count,))],
+        *[g for part_groups in groups for g in part_groups], *facts, *sums, norm_gain, router_t,
+        out_specs=(HBM, HBM),
+        scratch=[pltpu.VMEM(rows_shape, bf16), pltpu.VMEM(rows_shape[:-1], bf16), dma((count + 1,))],
     )
     return rows[None, None], gates[None, None]
 

time: 38.9 us -> 36.1 us (0.928)
  starting transfers between devices: 15.9 us -> 13.9 us
  waiting for transfers between devices: 13.6 us -> 13 us
    ppermute x12 -> x8, starting transfers between devices: 13 us -> 10.7 us  [swap(): lax.ppermute(block, axis, [(i, i ^ mask) for i in range(lax.axis_size(axi...]
    ppermute x12 -> x8, waiting for transfers between devices: 11 us -> 9.94 us  [swap(): lax.ppermute(block, axis, [(i, i ^ mask) for i in range(lax.axis_size(axi...]
    ppermute x2, waiting for transfers between devices: 2.57 us -> 3.09 us  [relay(): lax.ppermute(block, 'section', [(i, (i + 1) % sections) for i in range(se...]
  transfers between devices with their start and end apart: 14 -> 10, of which waited for: 7 -> 6; matrix products, arithmetic and copies ran while one was open for 0% -> 0% of each run, Pallas kernels for 11% -> 13%
where the time goes in v3:
time: 36.1 us; the launch traced here: 35.9 us
  starting transfers between devices  13.9 us (39%)
  waiting for transfers between devices  13 us (36%)
  Pallas kernels  8.21 us (23%)
  between operations  0.78 us (2%)
    ppermute x8, starting transfers between devices, swap(): lax.ppermute(block, axis, [(i, i ^ mask) for i in range(lax.axis_size(axi...  10.7 us
    ppermute x8, waiting for transfers between devices, swap(): lax.ppermute(block, axis, [(i, i ^ mask) for i in range(lax.axis_size(axi...  9.94 us
    pallas_call x13, Pallas kernels, call(): pl.pallas_call(kernel, out_shape=out, in_specs=specs, out_specs=out_specs...  8.21 us
    ppermute x2, starting transfers between devices, relay(): lax.ppermute(block, 'section', [(i, (i + 1) % sections) for i in range(se...  3.13 us
    ppermute x2, waiting for transfers between devices, relay(): lax.ppermute(block, 'section', [(i, (i + 1) % sections) for i in range(se...  3.09 us
  transfers between devices with their start and end apart: 10, of which 6 were waited for; matrix products, arithmetic and copies ran while one was open for 0% of the time, Pallas kernels for 13%

profile of v3, /device:TPU:0, one launch (start us, length us, event | category | flops | bytes accessed | tf_op | source)
XLA Modules:
  0.0 35.9 jit_solution(17997594057245127781)
XLA Ops:
  0.6 1.2 %shard_map.105.own_ref = bf16[528,128]{1,0:T(8,128)(2,1)S(1)} custom-call(bf16[64,512]{1,0:T(8,128)(2,1)} %bitcast.19, bf16[64,512]{1,0:T(8,128)(2,1)} %bitcast.21, f32[4,64]{1,0:T(4,128)} %bitcast.24), custom_call_target="tpu_custom_call" | custom-call | tf_op jit(solution)/shard_map/pallas_call | solution.py:362
  1.9 3.1 %collective-permute-start = (bf16[528,128]{1,0:T(8,128)(2,1)S(1)}, bf16[528,128]{1,0:T(8,128)(2,1)S(1)}, u32[]{:S(2)}, u32[]{:S(2)}) collective-permute-start(bf16[528,128]{1,0:T(8,128)(2,1)S(1)} %shard_map.105.own_ref), channel_id=1, source_target_pairs={{0,4},{4,0},{8,12},{12,8},{1,5},{5,1},{9,13},{13,9},{2,6},{6,2},{1... | collective-permute-start | bytes 405512 | tf_op jit(solution)/shard_map/ppermute | solution.py:355
  5.0 3.6 %collective-permute-done.rest_0_.got_ref = bf16[528,128]{1,0:T(8,128)(2,1)S(1)} collective-permute-done((bf16[528,128]{1,0:T(8,128)(2,1)S(1)}, bf16[528,128]{1,0:T(8,128)(2,1)S(1)}, u32[]{:S(2)}, u32[]{:S(2)}) %collective-permute-start) | collective-permute-done | bytes 135200 | tf_op jit(solution)/shard_map/ppermute | solution.py:355
  8.6 0.1 shard_map.107
  8.6 3.8 %collective-permute-start.1 = (bf16[528,128]{1,0:T(8,128)(2,1)S(1)}, bf16[528,128]{1,0:T(8,128)(2,1)S(1)}, u32[]{:S(2)}, u32[]{:S(2)}) collective-permute-start(bf16[528,128]{1,0:T(8,128)(2,1)S(1)} %shard_map.107), channel_id=1, source_target_pairs={{0,12},{4,8},{8,4},{12,0},{1,13},{5,9},{9,5},{13,1},{2,14},{6,10},... | collective-permute-start | bytes 405512 | tf_op jit(solution)/shard_map/ppermute | solution.py:355
  12.5 3.0 %shard_map.104 = (f32[64,512]{1,0:T(8,128)S(1)}, s32[16,128]{1,0:T(8,128)S(1)}, bf16[512,6144]{1,0:T(8,128)(2,1)S(1)}, bf16[64,512]{1,0:T(8,128)(2,1)S(1)}, f32[64,128]{1,0:T(8,128)S(1)}) custom-call(bf16[64,512]{1,0:T(8,128)(2,1)} %bitcast.23, bf16[64,512]{1,0:T(8,128)(2,1)} %bitcast.20, bf16[64,512]{1,0:T(8,128)(2,1)} %bitcast.22, f32[4,64]{1,0:T(4,128)} %bitcast.25, ...), custom_call_target="tpu_custom_call" | custom-call | bytes 6291456 | tf_op jit(solution)/shard_map/pallas_call | solution.py:362
  15.4 0.2 shard_map.106
  15.7 0.0 collective-permute-done.1.got_ref
  15.7 0.0 copy-start.1
  15.7 0.8 %shard_map.108 = (bf16[64,512]{1,0:T(8,128)(2,1)S(1)}, bf16[32,3072]{1,0:T(8,128)(2,1)S(1)}, bf16[32,3200]{1,0:T(8,128)(2,1)S(1)}) custom-call(bf16[64,512]{1,0:T(8,128)(2,1)S(1)} %get-tuple-element.20.q_ref, f32[64,512]{1,0:T(8,128)S(1)} %get-tuple-element.23.base_ref, f32[64,128]{1,0:T(8,128)S(1)} %get-tuple-element.24.scale_ref, ...), custom_call_target="tpu_custom_call" | custom-call | flops 201326592 | tf_op jit(solution)/shard_map/pallas_call | solution.py:362
  16.5 0.0 copy-start
  16.5 0.0 copy-start.2
  16.5 0.1 collective-permute-start.2
  16.6 0.7 %shard_map.111 = (bf16[32,3072]{1,0:T(8,128)(2,1)S(1)}, bf16[32,3072]{1,0:T(8,128)(2,1)S(1)}) custom-call(bf16[64,512]{1,0:T(8,128)(2,1)S(1)} %get-tuple-element.29.mixed_ref, bf16[512,6144]{1,0:T(8,128)(2,1)S(1)} %get-tuple-element.25.weight_ref), custom_call_target="tpu_custom_call" | custom-call | flops 201326592 | tf_op jit(solution)/shard_map/pallas_call | solution.py:362
  17.3 0.6 %collective-permute-start.6 = (bf16[32,3072]{1,0:T(8,128)(2,1)S(1)}, bf16[32,3072]{1,0:T(8,128)(2,1)S(1)}, u32[]{:S(2)}, u32[]{:S(2)}) collective-permute-start(bf16[32,3072]{1,0:T(8,128)(2,1)S(1)} %get-tuple-element.31.sent_ref), channel_id=1, source_target_pairs={{0,1},{1,0},{2,3},{3,2},{4,5},{5,4},{6,7},{7,6},{8,9},{9,8},{10,11... | collective-permute-start | bytes 589832 | tf_op jit(solution)/shard_map/ppermute | solution.py:355
  17.8 0.2 collective-permute-done.2.got_ref
  18.1 0.0 copy-done.1
  18.1 0.1 shard_map.109.own_ref
  18.2 1.6 %collective-permute-start.3 = (bf16[32,3200]{1,0:T(8,128)(2,1)S(1)}, bf16[32,3200]{1,0:T(8,128)(2,1)S(1)}, u32[]{:S(2)}, u32[]{:S(2)}) collective-permute-start(bf16[32,3200]{1,0:T(8,128)(2,1)S(1)} %shard_map.109.own_ref), channel_id=1, source_target_pairs={{0,2},{1,3},{2,0},{3,1},{4,6},{5,7},{6,4},{7,5},{8,10},{9,11},{10,... | collective-permute-start | bytes 614408 | tf_op jit(solution)/shard_map/ppermute | solution.py:355
  19.8 0.0 collective-permute-done.6.got_ref
  19.8 0.1 shard_map.112
  19.8 1.6 %collective-permute-start.7 = (bf16[32,3072]{1,0:T(8,128)(2,1)S(1)}, bf16[32,3072]{1,0:T(8,128)(2,1)S(1)}, u32[]{:S(2)}, u32[]{:S(2)}) collective-permute-start(bf16[32,3072]{1,0:T(8,128)(2,1)S(1)} %shard_map.112), channel_id=1, source_target_pairs={{0,16},{16,0},{1,17},{17,1},{2,18},{18,2},{3,19},{19,3},{4,20},{20... | collective-permute-start | bytes 589832 | tf_op jit(solution)/shard_map/ppermute | solution.py:421
  21.4 4.0 %collective-permute-done.3.got_ref = bf16[32,3200]{1,0:T(8,128)(2,1)S(1)} collective-permute-done((bf16[32,3200]{1,0:T(8,128)(2,1)S(1)}, bf16[32,3200]{1,0:T(8,128)(2,1)S(1)}, u32[]{:S(2)}, u32[]{:S(2)}) %collective-permute-start.3) | collective-permute-done | bytes 204832 | tf_op jit(solution)/shard_map/ppermute | solution.py:355
  25.3 0.1 shard_map.110
  25.4 1.6 %collective-permute-start.4 = (bf16[32,3072]{1,0:T(8,128)(2,1)S(1)}, bf16[32,3072]{1,0:T(8,128)(2,1)S(1)}, u32[]{:S(2)}, u32[]{:S(2)}) collective-permute-start(bf16[32,3072]{1,0:T(8,128)(2,1)S(1)} %shard_map.110), channel_id=1, source_target_pairs={{0,16},{16,0},{1,17},{17,1},{2,18},{18,2},{3,19},{19,3},{4,20},{20... | collective-permute-start | bytes 589832 | tf_op jit(solution)/shard_map/ppermute | solution.py:421
  27.0 0.0 collective-permute-done.7.own_ref
  27.0 1.5 %collective-permute-start.8 = (bf16[32,3072]{1,0:T(8,128)(2,1)S(1)}, bf16[32,3072]{1,0:T(8,128)(2,1)S(1)}, u32[]{:S(2)}, u32[]{:S(2)}) collective-permute-start(bf16[32,3072]{1,0:T(8,128)(2,1)S(1)} %collective-permute-done.7.own_ref), channel_id=1, source_target_pairs={{0,2},{1,3},{2,0},{3,1},{4,6},{5,7},{6,4},{7,5},{8,10},{9,11},{10,... | collective-permute-start | bytes 589832 | tf_op jit(solution)/shard_map/ppermute | solution.py:355
  28.5 3.1 %collective-permute-done.4.refs_0_ = bf16[32,3072]{1,0:T(8,128)(2,1)S(1)} collective-permute-done((bf16[32,3072]{1,0:T(8,128)(2,1)S(1)}, bf16[32,3072]{1,0:T(8,128)(2,1)S(1)}, u32[]{:S(2)}, u32[]{:S(2)}) %collective-permute-start.4) | collective-permute-done | bytes 196640 | tf_op jit(solution)/shard_map/ppermute | solution.py:421
  31.6 0.0 collective-permute-start.5
  31.6 1.2 %collective-permute-done.8.got_ref = bf16[32,3072]{1,0:T(8,128)(2,1)S(1)} collective-permute-done((bf16[32,3072]{1,0:T(8,128)(2,1)S(1)}, bf16[32,3072]{1,0:T(8,128)(2,1)S(1)}, u32[]{:S(2)}, u32[]{:S(2)}) %collective-permute-start.8) | collective-permute-done | bytes 196640 | tf_op jit(solution)/shard_map/ppermute | solution.py:355
  32.9 0.1 collective-permute-start.9
  32.9 0.2 shard_map.114
  33.1 0.0 collective-permute-done.5.refs_1_
  33.1 0.0 copy-done
  33.1 0.0 copy-done.2
  33.2 0.2 shard_map.115
  33.4 1.0 %collective-permute-done.9.refs_3_ = bf16[32,3072]{1,0:T(8,128)(2,1)S(1)} collective-permute-done((bf16[32,3072]{1,0:T(8,128)(2,1)S(1)}, bf16[32,3072]{1,0:T(8,128)(2,1)S(1)}, u32[]{:S(2)}, u32[]{:S(2)}) %collective-permute-start.9) | collective-permute-done | bytes 196640 | tf_op jit(solution)/shard_map/ppermute | solution.py:355
  34.4 1.5 %shard_map.116 = (bf16[4,4,4,6144]{3,2,1,0:T(4,128)(2,1)}, bf16[4,4,4]{2,1,0:T(4,128)(2,1)}) custom-call(bf16[32,3072]{1,0:T(8,128)(2,1)S(1)} %collective-permute-done.4.refs_0_, bf16[32,3072]{1,0:T(8,128)(2,1)S(1)} %collective-permute-done.5.refs_1_, bf16[32,3072]{1,0:T(8,128)(2,1)S(1)} %shard_map.113.refs_2_, ...), custom_call_target="tpu_custom_call" | custom-call | tf_op jit(solution)/shard_map/pallas_call | solution.py:362
  (1 shorter events, 0.0 us)
Async XLA Ops:
  1.9 6.7 %collective-permute-start = (bf16[528,128]{1,0:T(8,128)(2,1)S(1)}, bf16[528,128]{1,0:T(8,128)(2,1)S(1)}, u32[]{:S(2)}, u32[]{:S(2)}) collective-permute-start(bf16[528,128]{1,0:T(8,128)(2,1)S(1)} %shard_map.105.own_ref), channel_id=1, source_target_pairs={{0,4},{4,0},{8,12},{12,8},{1,5},{5,1},{9,13},{13,9},{2,6},{6,2},{1... | collective-permute-start | bytes 405512 | tf_op jit(solution)/shard_map/ppermute | solution.py:355
  8.6 7.1 %collective-permute-start.1 = (bf16[528,128]{1,0:T(8,128)(2,1)S(1)}, bf16[528,128]{1,0:T(8,128)(2,1)S(1)}, u32[]{:S(2)}, u32[]{:S(2)}) collective-permute-start(bf16[528,128]{1,0:T(8,128)(2,1)S(1)} %shard_map.107), channel_id=1, source_target_pairs={{0,12},{4,8},{8,4},{12,0},{1,13},{5,9},{9,5},{13,1},{2,14},{6,10},... | collective-permute-start | bytes 405512 | tf_op jit(solution)/shard_map/ppermute | solution.py:355
  15.7 2.4 %copy-start.1 = (bf16[1,16,6144]{2,1,0:T(8,128)(2,1)S(1)}, bf16[1,16,6144]{2,1,0:T(8,128)(2,1)}, u32[]{:S(2)}) copy-start(bf16[1,16,6144]{2,1,0:T(8,128)(2,1)} %param.14) | copy-start | bytes 589828
  16.5 16.6 %copy-start = (bf16[1,6144,16]{1,2,0:T(8,128)(2,1)S(1)}, bf16[1,6144,16]{1,2,0:T(8,128)(2,1)}, u32[]{:S(2)}) copy-start(bf16[1,6144,16]{1,2,0:T(8,128)(2,1)} %param.16) | copy-start | bytes 589828
  16.5 16.6 %copy-start.2 = (f32[1,6144]{1,0:T(1,128)S(1)}, f32[1,6144]{1,0:T(1,128)}, u32[]{:S(2)}) copy-start(f32[1,6144]{1,0:T(1,128)} %refs_8_.1) | copy-start | bytes 73732
  16.5 1.5 %collective-permute-start.2 = (bf16[32,3200]{1,0:T(8,128)(2,1)S(1)}, bf16[32,3200]{1,0:T(8,128)(2,1)S(1)}, u32[]{:S(2)}, u32[]{:S(2)}) collective-permute-start(bf16[32,3200]{1,0:T(8,128)(2,1)S(1)} %get-tuple-element.28.sent_ref), channel_id=1, source_target_pairs={{0,1},{1,0},{2,3},{3,2},{4,5},{5,4},{6,7},{7,6},{8,9},{9,8},{10,11... | collective-permute-start | bytes 614408 | tf_op jit(solution)/shard_map/ppermute | solution.py:355
  17.3 2.5 %collective-permute-start.6 = (bf16[32,3072]{1,0:T(8,128)(2,1)S(1)}, bf16[32,3072]{1,0:T(8,128)(2,1)S(1)}, u32[]{:S(2)}, u32[]{:S(2)}) collective-permute-start(bf16[32,3072]{1,0:T(8,128)(2,1)S(1)} %get-tuple-element.31.sent_ref), channel_id=1, source_target_pairs={{0,1},{1,0},{2,3},{3,2},{4,5},{5,4},{6,7},{7,6},{8,9},{9,8},{10,11... | collective-permute-start | bytes 589832 | tf_op jit(solution)/shard_map/ppermute | solution.py:355
  18.2 7.2 %collective-permute-start.3 = (bf16[32,3200]{1,0:T(8,128)(2,1)S(1)}, bf16[32,3200]{1,0:T(8,128)(2,1)S(1)}, u32[]{:S(2)}, u32[]{:S(2)}) collective-permute-start(bf16[32,3200]{1,0:T(8,128)(2,1)S(1)} %shard_map.109.own_ref), channel_id=1, source_target_pairs={{0,2},{1,3},{2,0},{3,1},{4,6},{5,7},{6,4},{7,5},{8,10},{9,11},{10,... | collective-permute-start | bytes 614408 | tf_op jit(solution)/shard_map/ppermute | solution.py:355
  19.8 7.1 %collective-permute-start.7 = (bf16[32,3072]{1,0:T(8,128)(2,1)S(1)}, bf16[32,3072]{1,0:T(8,128)(2,1)S(1)}, u32[]{:S(2)}, u32[]{:S(2)}) collective-permute-start(bf16[32,3072]{1,0:T(8,128)(2,1)S(1)} %shard_map.112), channel_id=1, source_target_pairs={{0,16},{16,0},{1,17},{17,1},{2,18},{18,2},{3,19},{19,3},{4,20},{20... | collective-permute-start | bytes 589832 | tf_op jit(solution)/shard_map/ppermute | solution.py:421
  25.4 6.2 %collective-permute-start.4 = (bf16[32,3072]{1,0:T(8,128)(2,1)S(1)}, bf16[32,3072]{1,0:T(8,128)(2,1)S(1)}, u32[]{:S(2)}, u32[]{:S(2)}) collective-permute-start(bf16[32,3072]{1,0:T(8,128)(2,1)S(1)} %shard_map.110), channel_id=1, source_target_pairs={{0,16},{16,0},{1,17},{17,1},{2,18},{18,2},{3,19},{19,3},{4,20},{20... | collective-permute-start | bytes 589832 | tf_op jit(solution)/shard_map/ppermute | solution.py:421
  27.0 5.8 %collective-permute-start.8 = (bf16[32,3072]{1,0:T(8,128)(2,1)S(1)}, bf16[32,3072]{1,0:T(8,128)(2,1)S(1)}, u32[]{:S(2)}, u32[]{:S(2)}) collective-permute-start(bf16[32,3072]{1,0:T(8,128)(2,1)S(1)} %collective-permute-done.7.own_ref), channel_id=1, source_target_pairs={{0,2},{1,3},{2,0},{3,1},{4,6},{5,7},{6,4},{7,5},{8,10},{9,11},{10,... | collective-permute-start | bytes 589832 | tf_op jit(solution)/shard_map/ppermute | solution.py:355
  31.6 1.5 %collective-permute-start.5 = (bf16[32,3072]{1,0:T(8,128)(2,1)S(1)}, bf16[32,3072]{1,0:T(8,128)(2,1)S(1)}, u32[]{:S(2)}, u32[]{:S(2)}) collective-permute-start(bf16[32,3072]{1,0:T(8,128)(2,1)S(1)} %collective-permute-done.4.refs_0_), channel_id=1, source_target_pairs={{0,1},{1,0},{2,3},{3,2},{4,5},{5,4},{6,7},{7,6},{8,9},{9,8},{10,11... | collective-permute-start | bytes 589832 | tf_op jit(solution)/shard_map/ppermute | solution.py:355
  32.9 1.5 %collective-permute-start.9 = (bf16[32,3072]{1,0:T(8,128)(2,1)S(1)}, bf16[32,3072]{1,0:T(8,128)(2,1)S(1)}, u32[]{:S(2)}, u32[]{:S(2)}) collective-permute-start(bf16[32,3072]{1,0:T(8,128)(2,1)S(1)} %shard_map.113.refs_2_), channel_id=1, source_target_pairs={{0,1},{1,0},{2,3},{3,2},{4,5},{5,4},{6,7},{7,6},{8,9},{9,8},{10,11... | collective-permute-start | bytes 589832 | tf_op jit(solution)/shard_map/ppermute | solution.py:355

commit v4 on v3

--- a/solution.py
+++ b/solution.py
@@ -108,10 +108,13 @@
 def join_kernel(heads, bit, own_ref, got_ref, msg_ref):
     dh = own_ref.shape[1]
     base = heads * dh
-    msg_ref[base:, :] = jnp.zeros((msg_ref.shape[0] - base, dh), bf16)
+    with_logs = msg_ref.shape[0] > base
+    if with_logs:
+        msg_ref[base:, :] = jnp.zeros((msg_ref.shape[0] - base, dh), bf16)
     for h, (state, log) in enumerate(joined(heads, bit, own_ref, got_ref)):
         msg_ref[h * dh : (h + 1) * dh, :] = state.astype(bf16)
-        put_log(msg_ref, base, heads, h, log)
+        if with_logs:
+            put_log(msg_ref, base, heads, h, log)
 
 
 def split_mm(a, state):
@@ -247,21 +250,16 @@
     out_ref[half:, :] = (own_ref[half:, :width].astype(f32) + got_ref[:half, :width].astype(f32)).astype(bf16)
 
 
-def squares(groups, size):
-    total = 0.0
-    for at, to in pieces(0, size):
-        wide = jnp.concatenate([g[:, at:to] for g in groups], axis=0).astype(f32)
-        total += jnp.sum(wide * wide, axis=1, keepdims=True)
-    return total
-
-
-def products(groups, size, gain, router, start):
-    total = 0.0
-    for at, to in pieces(0, size):
-        wide = jnp.concatenate([g[:, at:to] for g in groups], axis=0).astype(f32)
-        gained = (wide * gain[:, start + at : start + to]).astype(bf16)
-        total += mm(gained, router[:, start + at : start + to], NT)
-    return total
+def sums(refs, gain, router):
+    square, logits, start = 0.0, 0.0, 0
+    for ref in refs:
+        for at, to in pieces(0, ref.shape[1]):
+            wide = ref[:, at:to].astype(f32)
+            square += jnp.sum(wide * wide, axis=1, keepdims=True)
+            cols = slice(start + at, start + to)
+            logits += mm((wide * gain[:, cols]).astype(bf16), router[:, cols], NT)
+        start += ref.shape[1]
+    return square, logits
 
 
 def facts_kernel(exp_count, experts, tokens, own_ref, got_ref, chosen_ref, target_ref):
@@ -269,7 +267,7 @@
     top = exp_count // 2
     me = lax.axis_index("exp")
     lanes = [ref[:tokens, -LANES:].astype(f32).astype(jnp.int32) for ref in (own_ref, got_ref)]
-    wheres, named = [[], []], [[], []]
+    places, wheres, named = [[], []], [[], []], [[], []]
     for j in range(top):
         for side in range(2):
             sender = me ^ (j + side * top)
@@ -277,85 +275,104 @@
                 slot = lanes[side][:, 2 * j + c : 2 * j + c + 1]
                 place = slot - me * (per_owner * CAP)
                 mine = (place >= 0) & (place < per_owner * CAP)
+                places[c].append(jnp.where(mine, side * (per_owner * CAP) + place, -1))
                 wheres[c].append(jnp.where(mine, (place // CAP * exp_count + sender) * CAP + place % CAP, -1))
                 named[c].append(slot // CAP)
-    wheres = [jnp.concatenate(w, axis=0) for w in wheres]
-    named = [jnp.concatenate(n, axis=0) for n in named]
-    total = tokens * exp_count
+    places, wheres, named = [[jnp.concatenate(column, axis=0) for column in pair] for pair in (places, wheres, named)]
     slot = iota(chosen_ref.shape, 1)
-    chosen_ref[...] = ((wheres[0] == slot) | (wheres[1] == slot)).astype(f32).astype(bf16)
-    lane = iota((total, LANES), 1)
-    target = jnp.zeros((total, LANES), jnp.int32)
+    chosen_ref[...] = ((places[0] == slot) | (places[1] == slot)).astype(f32).astype(bf16)
+    lane = iota(target_ref.shape, 1)
+    target = jnp.zeros(target_ref.shape, jnp.int32)
     for i, column in enumerate(wheres + named):
         target = jnp.where(lane == i, column, target)
     target_ref[...] = target
 
 
-def ahead_kernel(count, *refs):
-    blocks, (gain_ref, router_ref, square_ref, logits_ref) = refs[:count], refs[count:]
-    size = blocks[0].shape[1]
-    square_ref[...] = jnp.broadcast_to(squares(blocks, size), square_ref.shape)
-    logits_ref[...] = products(blocks, size, gain_ref, router_ref, 0)
-
-
-def place_kernel(count, parts, *refs):
-    groups = [refs[i * count : (i + 1) * count] for i in range(parts)]
-    exp_count = 2 * count
-    chosen_ref, target_ref, square_ref, logits_ref, gain_ref, router_ref, *outs = refs[parts * count :]
-    rows_hbm, gates_hbm, rows_ref, gates_ref, sems = outs
-    per_owner, _, cap, width = rows_ref.shape
-    sizes = [part[0].shape[1] for part in groups]
-    square = square_ref[:, :1]
-    for part, size in zip(groups[1:], sizes[1:]):
-        square += squares(part, size)
-    factor = lax.rsqrt(square * (1.0 / width) + EPSILON)
-    chosen = chosen_ref[...]
-    copies = []
-    logits = logits_ref[...]
-    at = sizes[0]
-    for part, size in zip(groups[1:], sizes[1:]):
-        logits += products(part, size, gain_ref, router_ref, at)
-        at += size
-    logits = logits * factor
-    target = target_ref[...]
+def place_rows(block, parts, factor, chosen, gain, top, held, rows_hbm, sems):
+    me = lax.axis_index("exp")
+    _, per_owner, cap, _ = held.shape
+    copies, start = [], 0
+    for ref in parts:
+        for at, to in pieces(0, ref.shape[1]):
+            cols = slice(start + at, start + to)
+            normed = (ref[:, at:to].astype(f32) * factor * gain[:, cols]).astype(bf16)
+            held[:, :, :, cols] = mm(chosen, normed, TN).astype(bf16).reshape(2, per_owner, cap, to - at)
+            for side in range(2):
+                place = rows_hbm.at[:, me ^ (block + side * top), :, cols]
+                copies.append(pltpu.make_async_copy(held.at[side, :, :, cols], place, sems.at[len(copies)]))
+                copies[-1].start()
+        start += ref.shape[1]
+    return copies
+
+
+def gates_of(logits, target, rows, cap):
     wheres, named = [target[:, c : c + 1] for c in range(2)], [target[:, 2 + c : 3 + c] for c in range(2)]
     expert = iota(logits.shape, 1)
-    picked = [jnp.sum(jnp.where(named[c] == expert, logits, 0.0), axis=1, keepdims=True) for c in range(2)]
-    first = 1.0 / (1.0 + jnp.exp(picked[1] - picked[0]))
+    toward = jnp.where(named[1] == expert, 1.0, 0.0) - jnp.where(named[0] == expert, 1.0, 0.0)
+    first = 1.0 / (1.0 + jnp.exp(jnp.sum(toward * logits, axis=1, keepdims=True)))
     gates = [first, 1.0 - first]
     total = logits.shape[0]
-    hit_row = iota((total, per_owner * exp_count), 1)
-    hit_rank = iota((total, LANES), 1)
-    gate_rows = jnp.zeros((per_owner * exp_count, LANES), f32)
+    hit_row, hit_rank = iota((total, rows), 1), iota((total, LANES), 1)
+    out = jnp.zeros((rows, LANES), f32)
     for c in range(2):
         left = jnp.where((wheres[c] >= 0) & (wheres[c] // cap == hit_row), gates[c], 0.0).astype(bf16)
         right = jnp.where(wheres[c] % cap == hit_rank, 1.0, 0.0).astype(bf16)
-        gate_rows += mm(left, right, TN)
-    gate_rows = gate_rows.astype(bf16)
-    for e in range(per_owner):
-        gates_ref[e] = gate_rows[e * exp_count : (e + 1) * exp_count, :cap]
-    copies.append(pltpu.make_async_copy(gates_ref, gates_hbm, sems.at[len(copies)]))
-    copies[-1].start()
-    at = 0
-    for part, size in zip(groups, sizes):
-        for start, stop in pieces(0, size):
-            wide = jnp.concatenate([g[:, start:stop] for g in part], axis=0).astype(f32)
-            normed = (wide * factor * gain_ref[:, at + start : at + stop]).astype(bf16)
-            out = mm(chosen, normed, TN).astype(bf16)
-            window = (slice(None), slice(None), slice(None), slice(at + start, at + stop))
-            rows_ref[window] = out.reshape(per_owner, exp_count, cap, stop - start)
-            copies.append(pltpu.make_async_copy(rows_ref.at[window], rows_hbm.at[window], sems.at[len(copies)]))
-            copies[-1].start()
-        at += size
+        out += mm(left, right, TN)
+    return out
+
+
+def near_kernel(parts, top, *refs):
+    own, refs = refs[:parts], refs[parts:]
+    early, refs = refs[: -10], refs[-10:]
+    chosen_ref, target_ref, gain_ref, router_ref, rows_hbm, gates_ref, square_ref, logits_ref, held, sems = refs
+    width = gain_ref.shape[1]
+    tokens = own[0].shape[0]
+    square, logits = sums(own, gain_ref, router_ref)
+    factor = lax.rsqrt(square * (1.0 / width) + EPSILON)
+    copies = place_rows(0, own, factor, chosen_ref[:tokens, :], gain_ref, top, held, rows_hbm, sems)
+    gates_ref[...] = gates_of(logits * factor, target_ref[:tokens, :], gates_ref.shape[0], held.shape[2])
+    for i in range(top - 1):
+        square, logits = sums(early[i * (parts - 1) : (i + 1) * (parts - 1)], gain_ref, router_ref)
+        square_ref[i * tokens : (i + 1) * tokens, :] = jnp.broadcast_to(square, (tokens, square_ref.shape[1]))
+        logits_ref[i * tokens : (i + 1) * tokens, :] = logits
     for copy in copies:
         copy.wait()
 
 
+def far_kernel(parts, top, *refs):
+    late, refs = refs[: parts * (top - 1)], refs[parts * (top - 1) :]
+    chosen_ref, target_ref, gain_ref, router_ref, near_gates, square_ref, logits_ref, _, rows_hbm, gates_hbm, held, gates_ref, sems, last = refs
+    width = gain_ref.shape[1]
+    tokens = late[0].shape[0]
+    before = width - late[parts - 1].shape[1]
+    gates = near_gates[...]
+    copies = []
+    for i in range(top - 1):
+        block = late[i * parts : (i + 1) * parts]
+        rows = slice(i * tokens, (i + 1) * tokens)
+        token_rows = slice((i + 1) * tokens, (i + 2) * tokens)
+        square, logits = sums(block[-1:], gain_ref.at[:, before:], router_ref.at[:, before:])
+        factor = lax.rsqrt((square_ref[rows, :1] + square) * (1.0 / width) + EPSILON)
+        copies += place_rows(
+            i + 1, block, factor, chosen_ref[token_rows, :], gain_ref, top, held.at[i], rows_hbm, sems.at[i]
+        )
+        logits = (logits_ref[rows, :] + logits) * factor
+        gates += gates_of(logits, target_ref[token_rows, :], gates.shape[0], held.shape[3])
+    per_owner, exp_count, cap = gates_ref.shape
+    gates = gates.astype(bf16)
+    for e in range(per_owner):
+        gates_ref[e] = gates[e * exp_count : (e + 1) * exp_count, :cap]
+    copies.append(pltpu.make_async_copy(gates_ref, gates_hbm, last))
+    copies[-1].start()
+    for copy in copies:
+        copy.wait()
+
+
 def swap(block, axis, mask):
     return lax.ppermute(block, axis, [(i, i ^ mask) for i in range(lax.axis_size(axis))])
 
 
-def call(kernel, out, *args, specs=None, out_specs=None, scratch=(), flops=0, moved=0, limit=16 * MIB):
+def call(kernel, out, *args, specs=None, out_specs=None, scratch=(), flops=0, moved=0, limit=16 * MIB, aliases=None):
     single = not isinstance(out, (tuple, list))
     specs = specs or [VMEM] * len(args)
     args = [pltpu.with_memory_space_constraint(a, pltpu.HBM) if s is HBM else a for a, s in zip(args, specs, strict=True)]
@@ -365,6 +382,7 @@
         in_specs=specs,
         out_specs=out_specs or (VMEM if single else (VMEM,) * len(out)),
         scratch_shapes=scratch,
+        input_output_aliases=aliases or {},
         compiler_params=pltpu.CompilerParams(vmem_limit_bytes=limit),
         cost_estimate=pl.CostEstimate(flops=flops, bytes_accessed=moved, transcendentals=0),
     )(*args)
@@ -392,7 +410,9 @@
     for bit in range(ctx_bits):
         got.append(swap(msg, "ctx", (2 << bit) - 1))
         if bit < ctx_bits - 1:
-            msg = call(functools.partial(join_kernel, heads, bit), msg_shape, msg, got[-1])
+            last_shape = shape((heads * dh, dh), bf16)
+            out = msg_shape if bit < ctx_bits - 2 else last_shape
+            msg = call(functools.partial(join_kernel, heads, bit), out, msg, got[-1])
     inside, slots, weight_near, q_near, growth = call(
         inside_kernel,
         (
@@ -420,6 +440,7 @@
     def relay(block):
         return lax.ppermute(block, "section", [(i, (i + 1) % sections) for i in range(sections)])
 
+    all_tokens, experts = exp_count * tokens, per_owner * exp_count
     mixed, groups = None, []
     for start, stop in zip(cuts, cuts[1:]):
         first = mixed is None
@@ -452,33 +473,51 @@
         whole = shape((2 * tokens, size), bf16)
         if first:
             other = swap(own, "exp", top)
-            tagged = (own, other)
+            facts = call(
+                functools.partial(facts_kernel, exp_count, experts, tokens),
+                (shape((all_tokens, 2 * per_owner * CAP), bf16), shape((all_tokens, LANES), jnp.int32)),
+                own, other,
+            )
             block = relay(call(combine_kernel, whole, own, other))
         else:
             own = relay(own)
-            block = call(combine_kernel, whole, own, swap(own, "exp", top))
+            other, *facts = lax.optimization_barrier((swap(own, "exp", top), *facts))
+            block = call(combine_kernel, whole, own, other)
         groups.append([block])
         for index in range(1, top):
             groups[-1].append(swap(groups[-1][index & (index - 1)], "exp", index & -index))
     rows_shape = (per_owner, exp_count, CAP, width)
-    count = sum(len(pieces(start, stop)) for start, stop in zip(cuts, cuts[1:]))
-    all_tokens, experts = exp_count * tokens, per_owner * exp_count
-    facts = call(
-        functools.partial(facts_kernel, exp_count, experts, tokens),
-        (shape((all_tokens, per_owner * exp_count * CAP), bf16), shape((all_tokens, LANES), jnp.int32)),
-        *tagged,
-    )
-    sums = call(
-        functools.partial(ahead_kernel, top),
-        (shape((all_tokens, LANES), f32), shape((all_tokens, experts), f32)),
-        *groups[0], norm_gain, router_t,
+    count = 2 * sum(len(pieces(0, part_groups[0].shape[1])) for part_groups in groups)
+    late_tokens = all_tokens - 2 * tokens
+    held = (2, per_owner, CAP, width)
+    rows, *near = call(
+        functools.partial(near_kernel, PARTS, top),
+        (
+            shape(rows_shape, bf16),
+            shape((experts, LANES), f32),
+            shape((late_tokens, LANES), f32),
+            shape((late_tokens, experts), f32),
+        ),
+        *[part_groups[0] for part_groups in groups],
+        *[part_groups[i] for i in range(1, top) for part_groups in groups[:-1]],
+        *facts, norm_gain, router_t,
+        out_specs=(HBM, VMEM, VMEM, VMEM),
+        scratch=[pltpu.VMEM(held, bf16), dma((count,))],
     )
     rows, gates = call(
-        functools.partial(place_kernel, top, PARTS),
-        (shape(rows_shape, bf16), shape((per_owner, exp_count, CAP), bf16)),
-        *[g for part_groups in groups for g in part_groups], *facts, *sums, norm_gain, router_t,
+        functools.partial(far_kernel, PARTS, top),
+        (shape(rows_shape, bf16), shape(rows_shape[:-1], bf16)),
+        *[part_groups[i] for i in range(1, top) for part_groups in groups],
+        *facts, norm_gain, router_t, *near, rows,
+        specs=[VMEM] * (PARTS * (top - 1) + 7) + [HBM],
         out_specs=(HBM, HBM),
-        scratch=[pltpu.VMEM(rows_shape, bf16), pltpu.VMEM(rows_shape[:-1], bf16), dma((count + 1,))],
+        scratch=[
+            pltpu.VMEM((top - 1, *held), bf16),
+            pltpu.VMEM(rows_shape[:-1], bf16),
+            dma((top - 1, count)),
+            dma,
+        ],
+        aliases={PARTS * (top - 1) + 7: 0},
     )
     return rows[None, None], gates[None, None]
 

time: 36.1 us -> 35.8 us (level)
  waiting for transfers between devices: 13 us -> 12 us
  Pallas kernels: 8.21 us -> 8.97 us
    ppermute x8, waiting for transfers between devices: 9.94 us -> 9.1 us  [swap(): lax.ppermute(block, axis, [(i, i ^ mask) for i in range(lax.axis_size(axi...]
    pallas_call x13, Pallas kernels: 8.21 us -> 8.97 us  [call(): pl.pallas_call(kernel, out_shape=out, in_specs=specs, out_specs=out_specs...]
  transfers between devices with their start and end apart: 10 -> 10, of which waited for: 6 -> 6; matrix products, arithmetic and copies ran while one was open for 0% -> 0% of each run, Pallas kernels for 13% -> 16%
where the time goes in v4:
time: 35.8 us; the launch traced here: 35.6 us
  starting transfers between devices  13.8 us (39%)
  waiting for transfers between devices  12 us (34%)
  Pallas kernels  8.97 us (25%)
  between operations  0.76 us (2%)
    ppermute x8, starting transfers between devices, swap(): lax.ppermute(block, axis, [(i, i ^ mask) for i in range(lax.axis_size(axi...  10.7 us
    ppermute x8, waiting for transfers between devices, swap(): lax.ppermute(block, axis, [(i, i ^ mask) for i in range(lax.axis_size(axi...  9.1 us
    pallas_call x13, Pallas kernels, call(): pl.pallas_call(kernel, out_shape=out, in_specs=specs, out_specs=out_specs...  8.97 us
    ppermute x2, starting transfers between devices, relay(): lax.ppermute(block, 'section', [(i, (i + 1) % sections) for i in range(se...  3.11 us
    ppermute x2, waiting for transfers between devices, relay(): lax.ppermute(block, 'section', [(i, (i + 1) % sections) for i in range(se...  2.92 us
  transfers between devices with their start and end apart: 10, of which 6 were waited for; matrix products, arithmetic and copies ran while one was open for 0% of the time, Pallas kernels for 16%

profile of v4, /device:TPU:0, one launch (start us, length us, event | category | flops | bytes accessed | tf_op | source)
XLA Modules:
  0.0 35.6 jit_solution(1696074245904864555)
XLA Ops:
  0.6 1.2 %shard_map.105.own_ref = bf16[528,128]{1,0:T(8,128)(2,1)S(1)} custom-call(bf16[64,512]{1,0:T(8,128)(2,1)} %bitcast.20, bf16[64,512]{1,0:T(8,128)(2,1)} %bitcast.22, f32[4,64]{1,0:T(4,128)} %bitcast.25), custom_call_target="tpu_custom_call" | custom-call | tf_op jit(solution)/shard_map/pallas_call | solution.py:379
  1.9 3.1 %collective-permute-start = (bf16[528,128]{1,0:T(8,128)(2,1)S(1)}, bf16[528,128]{1,0:T(8,128)(2,1)S(1)}, u32[]{:S(2)}, u32[]{:S(2)}) collective-permute-start(bf16[528,128]{1,0:T(8,128)(2,1)S(1)} %shard_map.105.own_ref), channel_id=1, source_target_pairs={{0,4},{4,0},{8,12},{12,8},{1,5},{5,1},{9,13},{13,9},{2,6},{6,2},{1... | collective-permute-start | bytes 405512 | tf_op jit(solution)/shard_map/ppermute | solution.py:372
  5.0 3.6 %collective-permute-done.rest_0_.got_ref = bf16[528,128]{1,0:T(8,128)(2,1)S(1)} collective-permute-done((bf16[528,128]{1,0:T(8,128)(2,1)S(1)}, bf16[528,128]{1,0:T(8,128)(2,1)S(1)}, u32[]{:S(2)}, u32[]{:S(2)}) %collective-permute-start) | collective-permute-done | bytes 135200 | tf_op jit(solution)/shard_map/ppermute | solution.py:372
  8.6 0.1 shard_map.107
  8.6 3.8 %collective-permute-start.1 = (bf16[512,128]{1,0:T(8,128)(2,1)S(1)}, bf16[512,128]{1,0:T(8,128)(2,1)S(1)}, u32[]{:S(2)}, u32[]{:S(2)}) collective-permute-start(bf16[512,128]{1,0:T(8,128)(2,1)S(1)} %shard_map.107), channel_id=1, source_target_pairs={{0,12},{4,8},{8,4},{12,0},{1,13},{5,9},{9,5},{13,1},{2,14},{6,10},... | collective-permute-start | bytes 393224 | tf_op jit(solution)/shard_map/ppermute | solution.py:372
  12.4 3.0 %shard_map.104 = (f32[64,512]{1,0:T(8,128)S(1)}, s32[16,128]{1,0:T(8,128)S(1)}, bf16[512,6144]{1,0:T(8,128)(2,1)S(1)}, bf16[64,512]{1,0:T(8,128)(2,1)S(1)}, f32[64,128]{1,0:T(8,128)S(1)}) custom-call(bf16[64,512]{1,0:T(8,128)(2,1)} %bitcast.24, bf16[64,512]{1,0:T(8,128)(2,1)} %bitcast.21, bf16[64,512]{1,0:T(8,128)(2,1)} %bitcast.23, f32[4,64]{1,0:T(4,128)} %bitcast.26, ...), custom_call_target="tpu_custom_call" | custom-call | bytes 6291456 | tf_op jit(solution)/shard_map/pallas_call | solution.py:379
  15.4 0.2 shard_map.106
  15.7 0.0 collective-permute-done.1.got_ref
  15.7 0.0 copy-start.1
  15.7 0.8 %shard_map.108 = (bf16[64,512]{1,0:T(8,128)(2,1)S(1)}, bf16[32,3072]{1,0:T(8,128)(2,1)S(1)}, bf16[32,3200]{1,0:T(8,128)(2,1)S(1)}) custom-call(bf16[64,512]{1,0:T(8,128)(2,1)S(1)} %get-tuple-element.25.q_ref, f32[64,512]{1,0:T(8,128)S(1)} %get-tuple-element.28.base_ref, f32[64,128]{1,0:T(8,128)S(1)} %get-tuple-element.29.scale_ref, ...), custom_call_target="tpu_custom_call" | custom-call | flops 201326592 | tf_op jit(solution)/shard_map/pallas_call | solution.py:379
  16.5 0.0 copy-start
  16.5 0.0 copy-start.2
  16.5 0.1 collective-permute-start.2
  16.6 0.7 %shard_map.111 = (bf16[32,3072]{1,0:T(8,128)(2,1)S(1)}, bf16[32,3072]{1,0:T(8,128)(2,1)S(1)}) custom-call(bf16[64,512]{1,0:T(8,128)(2,1)S(1)} %get-tuple-element.34.mixed_ref, bf16[512,6144]{1,0:T(8,128)(2,1)S(1)} %get-tuple-element.30.weight_ref), custom_call_target="tpu_custom_call" | custom-call | flops 201326592 | tf_op jit(solution)/shard_map/pallas_call | solution.py:379
  17.3 0.6 %collective-permute-start.6 = (bf16[32,3072]{1,0:T(8,128)(2,1)S(1)}, bf16[32,3072]{1,0:T(8,128)(2,1)S(1)}, u32[]{:S(2)}, u32[]{:S(2)}) collective-permute-start(bf16[32,3072]{1,0:T(8,128)(2,1)S(1)} %get-tuple-element.36.sent_ref), channel_id=1, source_target_pairs={{0,1},{1,0},{2,3},{3,2},{4,5},{5,4},{6,7},{7,6},{8,9},{9,8},{10,11... | collective-permute-start | bytes 589832 | tf_op jit(solution)/shard_map/ppermute | solution.py:372
  17.8 0.2 collective-permute-done.2.got_ref
  18.0 0.0 copy-done.1
  18.0 0.1 shard_map.109.own_ref
  18.2 1.6 %collective-permute-start.3 = (bf16[32,3200]{1,0:T(8,128)(2,1)S(1)}, bf16[32,3200]{1,0:T(8,128)(2,1)S(1)}, u32[]{:S(2)}, u32[]{:S(2)}) collective-permute-start(bf16[32,3200]{1,0:T(8,128)(2,1)S(1)} %shard_map.109.own_ref), channel_id=1, source_target_pairs={{0,2},{1,3},{2,0},{3,1},{4,6},{5,7},{6,4},{7,5},{8,10},{9,11},{10,... | collective-permute-start | bytes 614408 | tf_op jit(solution)/shard_map/ppermute | solution.py:372
  19.7 0.0 collective-permute-done.6.got_ref
  19.7 0.1 shard_map.112
  19.8 1.6 %collective-permute-start.7 = (bf16[32,3072]{1,0:T(8,128)(2,1)S(1)}, bf16[32,3072]{1,0:T(8,128)(2,1)S(1)}, u32[]{:S(2)}, u32[]{:S(2)}) collective-permute-start(bf16[32,3072]{1,0:T(8,128)(2,1)S(1)} %shard_map.112), channel_id=1, source_target_pairs={{0,16},{16,0},{1,17},{17,1},{2,18},{18,2},{3,19},{19,3},{4,20},{20... | collective-permute-start | bytes 589832 | tf_op jit(solution)/shard_map/ppermute | solution.py:441
  21.4 4.0 %collective-permute-done.3.got_ref = bf16[32,3200]{1,0:T(8,128)(2,1)S(1)} collective-permute-done((bf16[32,3200]{1,0:T(8,128)(2,1)S(1)}, bf16[32,3200]{1,0:T(8,128)(2,1)S(1)}, u32[]{:S(2)}, u32[]{:S(2)}) %collective-permute-start.3) | collective-permute-done | bytes 204832 | tf_op jit(solution)/shard_map/ppermute | solution.py:372
  25.3 0.1 shard_map.110
  25.4 1.6 %collective-permute-start.4 = (bf16[32,3072]{1,0:T(8,128)(2,1)S(1)}, bf16[32,3072]{1,0:T(8,128)(2,1)S(1)}, u32[]{:S(2)}, u32[]{:S(2)}) collective-permute-start(bf16[32,3072]{1,0:T(8,128)(2,1)S(1)} %shard_map.110), channel_id=1, source_target_pairs={{0,16},{16,0},{1,17},{17,1},{2,18},{18,2},{3,19},{19,3},{4,20},{20... | collective-permute-start | bytes 589832 | tf_op jit(solution)/shard_map/ppermute | solution.py:441
  26.9 0.0 collective-permute-done.7.own_ref
  27.0 1.5 %collective-permute-start.8 = (bf16[32,3072]{1,0:T(8,128)(2,1)S(1)}, bf16[32,3072]{1,0:T(8,128)(2,1)S(1)}, u32[]{:S(2)}, u32[]{:S(2)}) collective-permute-start(bf16[32,3072]{1,0:T(8,128)(2,1)S(1)} %collective-permute-done.7.own_ref), channel_id=1, source_target_pairs={{0,2},{1,3},{2,0},{3,1},{4,6},{5,7},{6,4},{7,5},{8,10},{9,11},{10,... | collective-permute-start | bytes 589832 | tf_op jit(solution)/shard_map/ppermute | solution.py:372
  28.5 0.2 shard_map.113
  28.7 2.9 %collective-permute-done.4.refs_0_ = bf16[32,3072]{1,0:T(8,128)(2,1)S(1)} collective-permute-done((bf16[32,3072]{1,0:T(8,128)(2,1)S(1)}, bf16[32,3072]{1,0:T(8,128)(2,1)S(1)}, u32[]{:S(2)}, u32[]{:S(2)}) %collective-permute-start.4) | collective-permute-done | bytes 196640 | tf_op jit(solution)/shard_map/ppermute | solution.py:441
  31.6 0.0 collective-permute-start.5
  31.6 1.2 %collective-permute-done.8.got_ref = bf16[32,3072]{1,0:T(8,128)(2,1)S(1)} collective-permute-done((bf16[32,3072]{1,0:T(8,128)(2,1)S(1)}, bf16[32,3072]{1,0:T(8,128)(2,1)S(1)}, u32[]{:S(2)}, u32[]{:S(2)}) %collective-permute-start.8) | collective-permute-done | bytes 196640 | tf_op jit(solution)/shard_map/ppermute | solution.py:372
  32.8 0.1 collective-permute-start.9
  32.9 0.1 collective-permute-done.5.refs_2_.refs_0_
  33.0 0.0 copy-done
  33.0 0.0 copy-done.2
  33.0 1.3 %shard_map.115 = (bf16[4,4,4,6144]{3,2,1,0:T(4,128)(2,1)}, f32[16,128]{1,0:T(8,128)S(1)}, f32[32,128]{1,0:T(8,128)S(1)}, f32[32,16]{1,0:T(8,128)S(1)}) custom-call(bf16[32,3072]{1,0:T(8,128)(2,1)S(1)} %collective-permute-done.4.refs_0_, bf16[32,3072]{1,0:T(8,128)(2,1)S(1)} %shard_map.114.refs_1_, ...), custom_call_target="tpu_custom_call" | custom-call | tf_op jit(solution)/shard_map/pallas_call | solution.py:379
  34.3 0.0 collective-permute-done.9.refs_1_
  34.3 1.3 %shard_map.116 = (bf16[4,4,4,6144]{3,2,1,0:T(4,128)(2,1)}, bf16[4,4,4]{2,1,0:T(4,128)(2,1)}) custom-call(bf16[32,3072]{1,0:T(8,128)(2,1)S(1)} %collective-permute-done.5.refs_2_.refs_0_, bf16[32,3072]{1,0:T(8,128)(2,1)S(1)} %collective-permute-done.9.refs_1_, bf16[64,32]{1,0:T(8,128)(2,1)S(1)} %get-tuple-element.40.refs_3_.refs_2_, ...), custom_call_target="tpu_custom_call", output_to_operand_aliasing={{0}: (9, {})} | custom-call | tf_op jit(solution)/shard_map/pallas_call | solution.py:379
  (1 shorter events, 0.0 us)
Async XLA Ops:
  1.9 6.7 %collective-permute-start = (bf16[528,128]{1,0:T(8,128)(2,1)S(1)}, bf16[528,128]{1,0:T(8,128)(2,1)S(1)}, u32[]{:S(2)}, u32[]{:S(2)}) collective-permute-start(bf16[528,128]{1,0:T(8,128)(2,1)S(1)} %shard_map.105.own_ref), channel_id=1, source_target_pairs={{0,4},{4,0},{8,12},{12,8},{1,5},{5,1},{9,13},{13,9},{2,6},{6,2},{1... | collective-permute-start | bytes 405512 | tf_op jit(solution)/shard_map/ppermute | solution.py:372
  8.6 7.1 %collective-permute-start.1 = (bf16[512,128]{1,0:T(8,128)(2,1)S(1)}, bf16[512,128]{1,0:T(8,128)(2,1)S(1)}, u32[]{:S(2)}, u32[]{:S(2)}) collective-permute-start(bf16[512,128]{1,0:T(8,128)(2,1)S(1)} %shard_map.107), channel_id=1, source_target_pairs={{0,12},{4,8},{8,4},{12,0},{1,13},{5,9},{9,5},{13,1},{2,14},{6,10},... | collective-permute-start | bytes 393224 | tf_op jit(solution)/shard_map/ppermute | solution.py:372
  15.7 2.4 %copy-start.1 = (bf16[1,16,6144]{2,1,0:T(8,128)(2,1)S(1)}, bf16[1,16,6144]{2,1,0:T(8,128)(2,1)}, u32[]{:S(2)}) copy-start(bf16[1,16,6144]{2,1,0:T(8,128)(2,1)} %param.14) | copy-start | bytes 589828
  16.5 16.5 %copy-start = (bf16[1,6144,16]{1,2,0:T(8,128)(2,1)S(1)}, bf16[1,6144,16]{1,2,0:T(8,128)(2,1)}, u32[]{:S(2)}) copy-start(bf16[1,6144,16]{1,2,0:T(8,128)(2,1)} %param.16) | copy-start | bytes 589828
  16.5 16.5 %copy-start.2 = (f32[1,6144]{1,0:T(1,128)S(1)}, f32[1,6144]{1,0:T(1,128)}, u32[]{:S(2)}) copy-start(f32[1,6144]{1,0:T(1,128)} %refs_4_.1) | copy-start | bytes 73732
  16.5 1.5 %collective-permute-start.2 = (bf16[32,3200]{1,0:T(8,128)(2,1)S(1)}, bf16[32,3200]{1,0:T(8,128)(2,1)S(1)}, u32[]{:S(2)}, u32[]{:S(2)}) collective-permute-start(bf16[32,3200]{1,0:T(8,128)(2,1)S(1)} %get-tuple-element.33.sent_ref), channel_id=1, source_target_pairs={{0,1},{1,0},{2,3},{3,2},{4,5},{5,4},{6,7},{7,6},{8,9},{9,8},{10,11... | collective-permute-start | bytes 614408 | tf_op jit(solution)/shard_map/ppermute | solution.py:372
  17.3 2.5 %collective-permute-start.6 = (bf16[32,3072]{1,0:T(8,128)(2,1)S(1)}, bf16[32,3072]{1,0:T(8,128)(2,1)S(1)}, u32[]{:S(2)}, u32[]{:S(2)}) collective-permute-start(bf16[32,3072]{1,0:T(8,128)(2,1)S(1)} %get-tuple-element.36.sent_ref), channel_id=1, source_target_pairs={{0,1},{1,0},{2,3},{3,2},{4,5},{5,4},{6,7},{7,6},{8,9},{9,8},{10,11... | collective-permute-start | bytes 589832 | tf_op jit(solution)/shard_map/ppermute | solution.py:372
  18.2 7.2 %collective-permute-start.3 = (bf16[32,3200]{1,0:T(8,128)(2,1)S(1)}, bf16[32,3200]{1,0:T(8,128)(2,1)S(1)}, u32[]{:S(2)}, u32[]{:S(2)}) collective-permute-start(bf16[32,3200]{1,0:T(8,128)(2,1)S(1)} %shard_map.109.own_ref), channel_id=1, source_target_pairs={{0,2},{1,3},{2,0},{3,1},{4,6},{5,7},{6,4},{7,5},{8,10},{9,11},{10,... | collective-permute-start | bytes 614408 | tf_op jit(solution)/shard_map/ppermute | solution.py:372
  19.8 7.1 %collective-permute-start.7 = (bf16[32,3072]{1,0:T(8,128)(2,1)S(1)}, bf16[32,3072]{1,0:T(8,128)(2,1)S(1)}, u32[]{:S(2)}, u32[]{:S(2)}) collective-permute-start(bf16[32,3072]{1,0:T(8,128)(2,1)S(1)} %shard_map.112), channel_id=1, source_target_pairs={{0,16},{16,0},{1,17},{17,1},{2,18},{18,2},{3,19},{19,3},{4,20},{20... | collective-permute-start | bytes 589832 | tf_op jit(solution)/shard_map/ppermute | solution.py:441
  25.4 6.2 %collective-permute-start.4 = (bf16[32,3072]{1,0:T(8,128)(2,1)S(1)}, bf16[32,3072]{1,0:T(8,128)(2,1)S(1)}, u32[]{:S(2)}, u32[]{:S(2)}) collective-permute-start(bf16[32,3072]{1,0:T(8,128)(2,1)S(1)} %shard_map.110), channel_id=1, source_target_pairs={{0,16},{16,0},{1,17},{17,1},{2,18},{18,2},{3,19},{19,3},{4,20},{20... | collective-permute-start | bytes 589832 | tf_op jit(solution)/shard_map/ppermute | solution.py:441
  27.0 5.8 %collective-permute-start.8 = (bf16[32,3072]{1,0:T(8,128)(2,1)S(1)}, bf16[32,3072]{1,0:T(8,128)(2,1)S(1)}, u32[]{:S(2)}, u32[]{:S(2)}) collective-permute-start(bf16[32,3072]{1,0:T(8,128)(2,1)S(1)} %collective-permute-done.7.own_ref), channel_id=1, source_target_pairs={{0,2},{1,3},{2,0},{3,1},{4,6},{5,7},{6,4},{7,5},{8,10},{9,11},{10,... | collective-permute-start | bytes 589832 | tf_op jit(solution)/shard_map/ppermute | solution.py:372
  31.6 1.4 %collective-permute-start.5 = (bf16[32,3072]{1,0:T(8,128)(2,1)S(1)}, bf16[32,3072]{1,0:T(8,128)(2,1)S(1)}, u32[]{:S(2)}, u32[]{:S(2)}) collective-permute-start(bf16[32,3072]{1,0:T(8,128)(2,1)S(1)} %collective-permute-done.4.refs_0_), channel_id=1, source_target_pairs={{0,1},{1,0},{2,3},{3,2},{4,5},{5,4},{6,7},{7,6},{8,9},{9,8},{10,11... | collective-permute-start | bytes 589832 | tf_op jit(solution)/shard_map/ppermute | solution.py:372
  32.8 1.5 %collective-permute-start.9 = (bf16[32,3072]{1,0:T(8,128)(2,1)S(1)}, bf16[32,3072]{1,0:T(8,128)(2,1)S(1)}, u32[]{:S(2)}, u32[]{:S(2)}) collective-permute-start(bf16[32,3072]{1,0:T(8,128)(2,1)S(1)} %shard_map.114.refs_1_), channel_id=1, source_target_pairs={{0,1},{1,0},{2,3},{3,2},{4,5},{5,4},{6,7},{7,6},{8,9},{9,8},{10,11... | collective-permute-start | bytes 589832 | tf_op jit(solution)/shard_map/ppermute | solution.py:372

commit v5 on v4

--- a/solution.py
+++ b/solution.py
@@ -51,11 +51,15 @@
     return -(-3 * heads // ROWS) * ROWS
 
 
-def put_log(ref, base, heads, h, value):
-    for part in range(3):
-        piece = value.astype(bf16)
-        ref[base + part * heads + h : base + part * heads + h + 1, :] = piece
-        value = value - piece.astype(f32)
+def log_rows(values):
+    heads, shape = len(values), (pad_rows(len(values)), values[0].shape[1])
+    row, out = iota(shape, 0), jnp.zeros(shape, f32)
+    for h, value in enumerate(values):
+        for part in range(3):
+            piece = value.astype(bf16).astype(f32)
+            out = jnp.where(row == part * heads + h, piece, out)
+            value = value - piece
+    return out.astype(bf16)
 
 
 def get_log(block, heads, h):
@@ -74,14 +78,14 @@
     heads = decay_ref.shape[0]
     dh = k_ref.shape[1] // heads
     base = heads * dh
-    msg_ref[base:, :] = jnp.zeros((msg_ref.shape[0] - base, dh), bf16)
     copies[0].wait()
-    tails = []
+    tails, lasts = [], []
     for h in range(heads):
         column, along = cumulative(decay_ref[h : h + 1, :])
         last = along[:, -1:]
         tails.append(jnp.exp(last - column))
-        put_log(msg_ref, base, heads, h, jnp.broadcast_to(last, (1, dh)))
+        lasts.append(jnp.broadcast_to(last, (1, dh)))
+    msg_ref[base:, :] = log_rows(lasts)
     copies[1].wait()
     copies[2].wait()
     for h in range(heads):
@@ -107,14 +111,12 @@
 
 def join_kernel(heads, bit, own_ref, got_ref, msg_ref):
     dh = own_ref.shape[1]
-    base = heads * dh
-    with_logs = msg_ref.shape[0] > base
-    if with_logs:
-        msg_ref[base:, :] = jnp.zeros((msg_ref.shape[0] - base, dh), bf16)
+    logs = []
     for h, (state, log) in enumerate(joined(heads, bit, own_ref, got_ref)):
         msg_ref[h * dh : (h + 1) * dh, :] = state.astype(bf16)
-        if with_logs:
-            put_log(msg_ref, base, heads, h, log)
+        logs.append(log)
+    if msg_ref.shape[0] > heads * dh:
+        msg_ref[heads * dh :, :] = log_rows(logs)
 
 
 def split_mm(a, state):
@@ -207,7 +209,7 @@
         send_ref[:, at - start : to - start] = part[half:]
 
 
-def pieces(start, stop, step=1024):
+def pieces(start, stop, step=3072):
     return [(at, min(at + step, stop)) for at in range(start, stop, step)]
 
 
@@ -359,9 +361,8 @@
         logits = (logits_ref[rows, :] + logits) * factor
         gates += gates_of(logits, target_ref[token_rows, :], gates.shape[0], held.shape[3])
     per_owner, exp_count, cap = gates_ref.shape
-    gates = gates.astype(bf16)
     for e in range(per_owner):
-        gates_ref[e] = gates[e * exp_count : (e + 1) * exp_count, :cap]
+        gates_ref[e] = gates[e * exp_count : (e + 1) * exp_count, :cap].astype(bf16)
     copies.append(pltpu.make_async_copy(gates_ref, gates_hbm, last))
     copies[-1].start()
     for copy in copies:

time: 35.8 us -> 35.8 us (level)
  transfers between devices with their start and end apart: 10 -> 10, of which waited for: 6 -> 7; matrix products, arithmetic and copies ran while one was open for 0% -> 0% of each run, Pallas kernels for 16% -> 15%
where the time goes in v5:
time: 35.8 us; the launch traced here: 35.6 us
  starting transfers between devices  13.8 us (39%)
  waiting for transfers between devices  12.1 us (34%)
  Pallas kernels  8.81 us (25%)
  between operations  0.76 us (2%)
    ppermute x8, starting transfers between devices, swap(): lax.ppermute(block, axis, [(i, i ^ mask) for i in range(lax.axis_size(axi...  10.7 us
    ppermute x8, waiting for transfers between devices, swap(): lax.ppermute(block, axis, [(i, i ^ mask) for i in range(lax.axis_size(axi...  9.21 us
    pallas_call x13, Pallas kernels, call(): pl.pallas_call(kernel, out_shape=out, in_specs=specs, out_specs=out_specs...  8.81 us
    ppermute x2, starting transfers between devices, relay(): lax.ppermute(block, 'section', [(i, (i + 1) % sections) for i in range(se...  3.12 us
    ppermute x2, waiting for transfers between devices, relay(): lax.ppermute(block, 'section', [(i, (i + 1) % sections) for i in range(se...  2.92 us
  transfers between devices with their start and end apart: 10, of which 7 were waited for; matrix products, arithmetic and copies ran while one was open for 0% of the time, Pallas kernels for 15%

profile of v5, /device:TPU:0, one launch (start us, length us, event | category | flops | bytes accessed | tf_op | source)
XLA Modules:
  0.0 35.6 jit_solution(14456861702129540134)
XLA Ops:
  0.6 1.2 %shard_map.105.own_ref = bf16[528,128]{1,0:T(8,128)(2,1)S(1)} custom-call(bf16[64,512]{1,0:T(8,128)(2,1)} %bitcast.20, bf16[64,512]{1,0:T(8,128)(2,1)} %bitcast.22, f32[4,64]{1,0:T(4,128)} %bitcast.25), custom_call_target="tpu_custom_call" | custom-call | tf_op jit(solution)/shard_map/pallas_call | solution.py:380
  1.9 3.1 %collective-permute-start = (bf16[528,128]{1,0:T(8,128)(2,1)S(1)}, bf16[528,128]{1,0:T(8,128)(2,1)S(1)}, u32[]{:S(2)}, u32[]{:S(2)}) collective-permute-start(bf16[528,128]{1,0:T(8,128)(2,1)S(1)} %shard_map.105.own_ref), channel_id=1, source_target_pairs={{0,4},{4,0},{8,12},{12,8},{1,5},{5,1},{9,13},{13,9},{2,6},{6,2},{1... | collective-permute-start | bytes 405512 | tf_op jit(solution)/shard_map/ppermute | solution.py:373
  5.0 3.6 %collective-permute-done.rest_0_.got_ref = bf16[528,128]{1,0:T(8,128)(2,1)S(1)} collective-permute-done((bf16[528,128]{1,0:T(8,128)(2,1)S(1)}, bf16[528,128]{1,0:T(8,128)(2,1)S(1)}, u32[]{:S(2)}, u32[]{:S(2)}) %collective-permute-start) | collective-permute-done | bytes 135200 | tf_op jit(solution)/shard_map/ppermute | solution.py:373
  8.5 0.1 shard_map.107
  8.6 3.8 %collective-permute-start.1 = (bf16[512,128]{1,0:T(8,128)(2,1)S(1)}, bf16[512,128]{1,0:T(8,128)(2,1)S(1)}, u32[]{:S(2)}, u32[]{:S(2)}) collective-permute-start(bf16[512,128]{1,0:T(8,128)(2,1)S(1)} %shard_map.107), channel_id=1, source_target_pairs={{0,12},{4,8},{8,4},{12,0},{1,13},{5,9},{9,5},{13,1},{2,14},{6,10},... | collective-permute-start | bytes 393224 | tf_op jit(solution)/shard_map/ppermute | solution.py:373
  12.4 3.0 %shard_map.104 = (f32[64,512]{1,0:T(8,128)S(1)}, s32[16,128]{1,0:T(8,128)S(1)}, bf16[512,6144]{1,0:T(8,128)(2,1)S(1)}, bf16[64,512]{1,0:T(8,128)(2,1)S(1)}, f32[64,128]{1,0:T(8,128)S(1)}) custom-call(bf16[64,512]{1,0:T(8,128)(2,1)} %bitcast.24, bf16[64,512]{1,0:T(8,128)(2,1)} %bitcast.21, bf16[64,512]{1,0:T(8,128)(2,1)} %bitcast.23, f32[4,64]{1,0:T(4,128)} %bitcast.26, ...), custom_call_target="tpu_custom_call" | custom-call | bytes 6291456 | tf_op jit(solution)/shard_map/pallas_call | solution.py:380
  15.4 0.2 shard_map.106
  15.7 0.0 collective-permute-done.1.got_ref
  15.7 0.0 copy-start.1
  15.7 0.8 %shard_map.108 = (bf16[64,512]{1,0:T(8,128)(2,1)S(1)}, bf16[32,3072]{1,0:T(8,128)(2,1)S(1)}, bf16[32,3200]{1,0:T(8,128)(2,1)S(1)}) custom-call(bf16[64,512]{1,0:T(8,128)(2,1)S(1)} %get-tuple-element.25.q_ref, f32[64,512]{1,0:T(8,128)S(1)} %get-tuple-element.28.base_ref, f32[64,128]{1,0:T(8,128)S(1)} %get-tuple-element.29.scale_ref, ...), custom_call_target="tpu_custom_call" | custom-call | flops 201326592 | tf_op jit(solution)/shard_map/pallas_call | solution.py:380
  16.5 0.0 copy-start
  16.5 0.0 copy-start.2
  16.5 0.1 collective-permute-start.2
  16.6 0.7 %shard_map.111 = (bf16[32,3072]{1,0:T(8,128)(2,1)S(1)}, bf16[32,3072]{1,0:T(8,128)(2,1)S(1)}) custom-call(bf16[64,512]{1,0:T(8,128)(2,1)S(1)} %get-tuple-element.34.mixed_ref, bf16[512,6144]{1,0:T(8,128)(2,1)S(1)} %get-tuple-element.30.weight_ref), custom_call_target="tpu_custom_call" | custom-call | flops 201326592 | tf_op jit(solution)/shard_map/pallas_call | solution.py:380
  17.3 0.6 %collective-permute-start.6 = (bf16[32,3072]{1,0:T(8,128)(2,1)S(1)}, bf16[32,3072]{1,0:T(8,128)(2,1)S(1)}, u32[]{:S(2)}, u32[]{:S(2)}) collective-permute-start(bf16[32,3072]{1,0:T(8,128)(2,1)S(1)} %get-tuple-element.36.sent_ref), channel_id=1, source_target_pairs={{0,1},{1,0},{2,3},{3,2},{4,5},{5,4},{6,7},{7,6},{8,9},{9,8},{10,11... | collective-permute-start | bytes 589832 | tf_op jit(solution)/shard_map/ppermute | solution.py:373
  17.8 0.2 collective-permute-done.2.got_ref
  18.0 0.0 copy-done.1
  18.0 0.1 shard_map.109.own_ref
  18.1 1.6 %collective-permute-start.3 = (bf16[32,3200]{1,0:T(8,128)(2,1)S(1)}, bf16[32,3200]{1,0:T(8,128)(2,1)S(1)}, u32[]{:S(2)}, u32[]{:S(2)}) collective-permute-start(bf16[32,3200]{1,0:T(8,128)(2,1)S(1)} %shard_map.109.own_ref), channel_id=1, source_target_pairs={{0,2},{1,3},{2,0},{3,1},{4,6},{5,7},{6,4},{7,5},{8,10},{9,11},{10,... | collective-permute-start | bytes 614408 | tf_op jit(solution)/shard_map/ppermute | solution.py:373
  19.7 0.0 collective-permute-done.6.got_ref
  19.7 0.1 shard_map.112
  19.8 1.6 %collective-permute-start.7 = (bf16[32,3072]{1,0:T(8,128)(2,1)S(1)}, bf16[32,3072]{1,0:T(8,128)(2,1)S(1)}, u32[]{:S(2)}, u32[]{:S(2)}) collective-permute-start(bf16[32,3072]{1,0:T(8,128)(2,1)S(1)} %shard_map.112), channel_id=1, source_target_pairs={{0,16},{16,0},{1,17},{17,1},{2,18},{18,2},{3,19},{19,3},{4,20},{20... | collective-permute-start | bytes 589832 | tf_op jit(solution)/shard_map/ppermute | solution.py:442
  21.4 4.0 %collective-permute-done.3.got_ref = bf16[32,3200]{1,0:T(8,128)(2,1)S(1)} collective-permute-done((bf16[32,3200]{1,0:T(8,128)(2,1)S(1)}, bf16[32,3200]{1,0:T(8,128)(2,1)S(1)}, u32[]{:S(2)}, u32[]{:S(2)}) %collective-permute-start.3) | collective-permute-done | bytes 204832 | tf_op jit(solution)/shard_map/ppermute | solution.py:373
  25.3 0.1 shard_map.110
  25.4 1.6 %collective-permute-start.4 = (bf16[32,3072]{1,0:T(8,128)(2,1)S(1)}, bf16[32,3072]{1,0:T(8,128)(2,1)S(1)}, u32[]{:S(2)}, u32[]{:S(2)}) collective-permute-start(bf16[32,3072]{1,0:T(8,128)(2,1)S(1)} %shard_map.110), channel_id=1, source_target_pairs={{0,16},{16,0},{1,17},{17,1},{2,18},{18,2},{3,19},{19,3},{4,20},{20... | collective-permute-start | bytes 589832 | tf_op jit(solution)/shard_map/ppermute | solution.py:442
  26.9 0.0 collective-permute-done.7.own_ref
  26.9 1.5 %collective-permute-start.8 = (bf16[32,3072]{1,0:T(8,128)(2,1)S(1)}, bf16[32,3072]{1,0:T(8,128)(2,1)S(1)}, u32[]{:S(2)}, u32[]{:S(2)}) collective-permute-start(bf16[32,3072]{1,0:T(8,128)(2,1)S(1)} %collective-permute-done.7.own_ref), channel_id=1, source_target_pairs={{0,2},{1,3},{2,0},{3,1},{4,6},{5,7},{6,4},{7,5},{8,10},{9,11},{10,... | collective-permute-start | bytes 589832 | tf_op jit(solution)/shard_map/ppermute | solution.py:373
  28.5 0.2 shard_map.113
  28.6 2.9 %collective-permute-done.4.refs_0_ = bf16[32,3072]{1,0:T(8,128)(2,1)S(1)} collective-permute-done((bf16[32,3072]{1,0:T(8,128)(2,1)S(1)}, bf16[32,3072]{1,0:T(8,128)(2,1)S(1)}, u32[]{:S(2)}, u32[]{:S(2)}) %collective-permute-start.4) | collective-permute-done | bytes 196640 | tf_op jit(solution)/shard_map/ppermute | solution.py:442
  31.6 0.0 collective-permute-start.5
  31.6 1.2 %collective-permute-done.8.got_ref = bf16[32,3072]{1,0:T(8,128)(2,1)S(1)} collective-permute-done((bf16[32,3072]{1,0:T(8,128)(2,1)S(1)}, bf16[32,3072]{1,0:T(8,128)(2,1)S(1)}, u32[]{:S(2)}, u32[]{:S(2)}) %collective-permute-start.8) | collective-permute-done | bytes 196640 | tf_op jit(solution)/shard_map/ppermute | solution.py:373
  32.8 0.1 collective-permute-start.9
  32.9 0.1 collective-permute-done.5.refs_2_.refs_0_
  33.0 0.0 copy-done
  33.0 0.0 copy-done.2
  33.0 1.2 %shard_map.115 = (bf16[4,4,4,6144]{3,2,1,0:T(4,128)(2,1)}, f32[16,128]{1,0:T(8,128)S(1)}, f32[32,128]{1,0:T(8,128)S(1)}, f32[32,16]{1,0:T(8,128)S(1)}) custom-call(bf16[32,3072]{1,0:T(8,128)(2,1)S(1)} %collective-permute-done.4.refs_0_, bf16[32,3072]{1,0:T(8,128)(2,1)S(1)} %shard_map.114.refs_1_, ...), custom_call_target="tpu_custom_call" | custom-call | tf_op jit(solution)/shard_map/pallas_call | solution.py:380
  34.2 0.1 collective-permute-done.9.refs_1_
  34.3 1.2 %shard_map.116 = (bf16[4,4,4,6144]{3,2,1,0:T(4,128)(2,1)}, bf16[4,4,4]{2,1,0:T(4,128)(2,1)}) custom-call(bf16[32,3072]{1,0:T(8,128)(2,1)S(1)} %collective-permute-done.5.refs_2_.refs_0_, bf16[32,3072]{1,0:T(8,128)(2,1)S(1)} %collective-permute-done.9.refs_1_, bf16[64,32]{1,0:T(8,128)(2,1)S(1)} %get-tuple-element.40.refs_3_.refs_2_, ...), custom_call_target="tpu_custom_call", output_to_operand_aliasing={{0}: (9, {})} | custom-call | tf_op jit(solution)/shard_map/pallas_call | solution.py:380
  (1 shorter events, 0.0 us)
Async XLA Ops:
  1.9 6.7 %collective-permute-start = (bf16[528,128]{1,0:T(8,128)(2,1)S(1)}, bf16[528,128]{1,0:T(8,128)(2,1)S(1)}, u32[]{:S(2)}, u32[]{:S(2)}) collective-permute-start(bf16[528,128]{1,0:T(8,128)(2,1)S(1)} %shard_map.105.own_ref), channel_id=1, source_target_pairs={{0,4},{4,0},{8,12},{12,8},{1,5},{5,1},{9,13},{13,9},{2,6},{6,2},{1... | collective-permute-start | bytes 405512 | tf_op jit(solution)/shard_map/ppermute | solution.py:373
  8.6 7.1 %collective-permute-start.1 = (bf16[512,128]{1,0:T(8,128)(2,1)S(1)}, bf16[512,128]{1,0:T(8,128)(2,1)S(1)}, u32[]{:S(2)}, u32[]{:S(2)}) collective-permute-start(bf16[512,128]{1,0:T(8,128)(2,1)S(1)} %shard_map.107), channel_id=1, source_target_pairs={{0,12},{4,8},{8,4},{12,0},{1,13},{5,9},{9,5},{13,1},{2,14},{6,10},... | collective-permute-start | bytes 393224 | tf_op jit(solution)/shard_map/ppermute | solution.py:373
  15.7 2.4 %copy-start.1 = (bf16[1,16,6144]{2,1,0:T(8,128)(2,1)S(1)}, bf16[1,16,6144]{2,1,0:T(8,128)(2,1)}, u32[]{:S(2)}) copy-start(bf16[1,16,6144]{2,1,0:T(8,128)(2,1)} %param.14) | copy-start | bytes 589828
  16.5 16.5 %copy-start = (bf16[1,6144,16]{1,2,0:T(8,128)(2,1)S(1)}, bf16[1,6144,16]{1,2,0:T(8,128)(2,1)}, u32[]{:S(2)}) copy-start(bf16[1,6144,16]{1,2,0:T(8,128)(2,1)} %param.16) | copy-start | bytes 589828
  16.5 16.5 %copy-start.2 = (f32[1,6144]{1,0:T(1,128)S(1)}, f32[1,6144]{1,0:T(1,128)}, u32[]{:S(2)}) copy-start(f32[1,6144]{1,0:T(1,128)} %refs_4_.1) | copy-start | bytes 73732
  16.5 1.5 %collective-permute-start.2 = (bf16[32,3200]{1,0:T(8,128)(2,1)S(1)}, bf16[32,3200]{1,0:T(8,128)(2,1)S(1)}, u32[]{:S(2)}, u32[]{:S(2)}) collective-permute-start(bf16[32,3200]{1,0:T(8,128)(2,1)S(1)} %get-tuple-element.33.sent_ref), channel_id=1, source_target_pairs={{0,1},{1,0},{2,3},{3,2},{4,5},{5,4},{6,7},{7,6},{8,9},{9,8},{10,11... | collective-permute-start | bytes 614408 | tf_op jit(solution)/shard_map/ppermute | solution.py:373
  17.3 2.5 %collective-permute-start.6 = (bf16[32,3072]{1,0:T(8,128)(2,1)S(1)}, bf16[32,3072]{1,0:T(8,128)(2,1)S(1)}, u32[]{:S(2)}, u32[]{:S(2)}) collective-permute-start(bf16[32,3072]{1,0:T(8,128)(2,1)S(1)} %get-tuple-element.36.sent_ref), channel_id=1, source_target_pairs={{0,1},{1,0},{2,3},{3,2},{4,5},{5,4},{6,7},{7,6},{8,9},{9,8},{10,11... | collective-permute-start | bytes 589832 | tf_op jit(solution)/shard_map/ppermute | solution.py:373
  18.1 7.2 %collective-permute-start.3 = (bf16[32,3200]{1,0:T(8,128)(2,1)S(1)}, bf16[32,3200]{1,0:T(8,128)(2,1)S(1)}, u32[]{:S(2)}, u32[]{:S(2)}) collective-permute-start(bf16[32,3200]{1,0:T(8,128)(2,1)S(1)} %shard_map.109.own_ref), channel_id=1, source_target_pairs={{0,2},{1,3},{2,0},{3,1},{4,6},{5,7},{6,4},{7,5},{8,10},{9,11},{10,... | collective-permute-start | bytes 614408 | tf_op jit(solution)/shard_map/ppermute | solution.py:373
  19.8 7.1 %collective-permute-start.7 = (bf16[32,3072]{1,0:T(8,128)(2,1)S(1)}, bf16[32,3072]{1,0:T(8,128)(2,1)S(1)}, u32[]{:S(2)}, u32[]{:S(2)}) collective-permute-start(bf16[32,3072]{1,0:T(8,128)(2,1)S(1)} %shard_map.112), channel_id=1, source_target_pairs={{0,16},{16,0},{1,17},{17,1},{2,18},{18,2},{3,19},{19,3},{4,20},{20... | collective-permute-start | bytes 589832 | tf_op jit(solution)/shard_map/ppermute | solution.py:442
  25.4 6.2 %collective-permute-start.4 = (bf16[32,3072]{1,0:T(8,128)(2,1)S(1)}, bf16[32,3072]{1,0:T(8,128)(2,1)S(1)}, u32[]{:S(2)}, u32[]{:S(2)}) collective-permute-start(bf16[32,3072]{1,0:T(8,128)(2,1)S(1)} %shard_map.110), channel_id=1, source_target_pairs={{0,16},{16,0},{1,17},{17,1},{2,18},{18,2},{3,19},{19,3},{4,20},{20... | collective-permute-start | bytes 589832 | tf_op jit(solution)/shard_map/ppermute | solution.py:442
  26.9 5.8 %collective-permute-start.8 = (bf16[32,3072]{1,0:T(8,128)(2,1)S(1)}, bf16[32,3072]{1,0:T(8,128)(2,1)S(1)}, u32[]{:S(2)}, u32[]{:S(2)}) collective-permute-start(bf16[32,3072]{1,0:T(8,128)(2,1)S(1)} %collective-permute-done.7.own_ref), channel_id=1, source_target_pairs={{0,2},{1,3},{2,0},{3,1},{4,6},{5,7},{6,4},{7,5},{8,10},{9,11},{10,... | collective-permute-start | bytes 589832 | tf_op jit(solution)/shard_map/ppermute | solution.py:373
  31.6 1.4 %collective-permute-start.5 = (bf16[32,3072]{1,0:T(8,128)(2,1)S(1)}, bf16[32,3072]{1,0:T(8,128)(2,1)S(1)}, u32[]{:S(2)}, u32[]{:S(2)}) collective-permute-start(bf16[32,3072]{1,0:T(8,128)(2,1)S(1)} %collective-permute-done.4.refs_0_), channel_id=1, source_target_pairs={{0,1},{1,0},{2,3},{3,2},{4,5},{5,4},{6,7},{7,6},{8,9},{9,8},{10,11... | collective-permute-start | bytes 589832 | tf_op jit(solution)/shard_map/ppermute | solution.py:373
  32.8 1.5 %collective-permute-start.9 = (bf16[32,3072]{1,0:T(8,128)(2,1)S(1)}, bf16[32,3072]{1,0:T(8,128)(2,1)S(1)}, u32[]{:S(2)}, u32[]{:S(2)}) collective-permute-start(bf16[32,3072]{1,0:T(8,128)(2,1)S(1)} %shard_map.114.refs_1_), channel_id=1, source_target_pairs={{0,1},{1,0},{2,3},{3,2},{4,5},{5,4},{6,7},{7,6},{8,9},{9,8},{10,11... | collective-permute-start | bytes 589832 | tf_op jit(solution)/shard_map/ppermute | solution.py:373

commit v6 on v5

--- a/solution.py
+++ b/solution.py
@@ -125,10 +125,18 @@
     return mm(a, high, NN) + mm(a, low, NN)
 
 
+def weight_kernel(weight_hbm, out_ref, sem):
+    copy = pltpu.make_async_copy(weight_hbm.at[:, : out_ref.shape[1]], out_ref, sem)
+    copy.start()
+    copy.wait()
+
+
 def inside_kernel(q_hbm, k_hbm, v_hbm, decay_hbm, ids_hbm, weight_hbm, inside_ref, slots_ref, weight_ref, q_ref, growth_ref,
                   k_ref, v_ref, decay_ref, ids_ref, sems):
     copies = fetch(
-        (decay_hbm, ids_hbm, q_hbm, k_hbm, v_hbm, weight_hbm), (decay_ref, ids_ref, q_ref, k_ref, v_ref, weight_ref), sems
+        (decay_hbm, ids_hbm, q_hbm, k_hbm, v_hbm, weight_hbm.at[:, -weight_ref.shape[1] :]),
+        (decay_ref, ids_ref, q_ref, k_ref, v_ref, weight_ref),
+        sems,
     )
     for copy in copies[:-1]:
         copy.wait()
@@ -186,12 +194,23 @@
     scale_ref[...] = scale
 
 
-def mix_kernel(heads, order, stop, q_ref, base_ref, scale_ref, got_ref, weight_ref, slots_ref, mixed_ref, keep_ref, send_ref, attended):
+def answer_kernel(heads, asked_ref, state_ref, out_ref):
+    dh = state_ref.shape[1]
+    for h in range(heads):
+        cols = slice(h * dh, (h + 1) * dh)
+        out_ref[:, cols] = mm(asked_ref[:, cols], state_ref[h * dh : (h + 1) * dh, :], NN).astype(bf16)
+
+
+def mix_kernel(heads, order, stop, q_ref, base_ref, scale_ref, state_ref, *rest):
+    *answers, weight_ref, slots_ref, mixed_ref, keep_ref, send_ref, attended = rest
     dh = base_ref.shape[1] // heads
     me = lax.axis_index("exp")
+    last = jnp.full((base_ref.shape[0], dh), lax.axis_index("ctx"), jnp.int32) == 3
     for h in range(heads):
         cols = slice(h * dh, (h + 1) * dh)
-        outside = mm(q_ref[:, cols], got_ref[h * dh : (h + 1) * dh, :], NN)
+        outside = mm(q_ref[:, cols], state_ref[h * dh : (h + 1) * dh, :], NN)
+        for answer_ref in answers:
+            outside = jnp.where(last, answer_ref[:, cols].astype(f32), outside)
         attended[:, cols] = (base_ref[:, cols] + scale_ref[:, h : h + 1] * outside).astype(bf16)
     share = base_ref.shape[0] // len(order)
     for i, k in enumerate(order):
@@ -373,6 +392,20 @@
     return lax.ppermute(block, axis, [(i, i ^ mask) for i in range(lax.axis_size(axis))])
 
 
+def hop(block, axis, route):
+    places, exps = lax.axis_size(axis), lax.axis_size("exp")
+    pairs = [(c * exps + e, to * exps + to_e) for c in range(places) for e in range(exps) for to, to_e in [route(c, e)]]
+    return lax.ppermute(block, (axis, "exp"), pairs)
+
+
+def around(place, index):
+    return ({1: 3, 3: 2, 2: 1}[place], index) if place else (place, index ^ 1)
+
+
+def between(pair, place, index):
+    return (sum(pair) - place, index) if place in pair else (place, index ^ 1)
+
+
 def call(kernel, out, *args, specs=None, out_specs=None, scratch=(), flops=0, moved=0, limit=16 * MIB, aliases=None):
     single = not isinstance(out, (tuple, list))
     specs = specs or [VMEM] * len(args)
@@ -407,19 +440,31 @@
     small = pltpu.VMEM(decay.shape, f32)
     dma = pltpu.SemaphoreType.DMA
     msg = call(state_kernel, msg_shape, k, v, decay, specs=[HBM] * 3, scratch=[part, part, small, dma((3,))])
+    cuts = [width * i // PARTS // LANES * LANES for i in range(PARTS + 1)]
+    weight_after, msg = lax.optimization_barrier((weight, msg))
+    weight_early = call(
+        weight_kernel, shape((heads * dh, cuts[1]), bf16), weight_after, specs=[HBM], scratch=[dma], moved=weight.size
+    )
     got = []
-    for bit in range(ctx_bits):
+    for bit in range(ctx_bits - 1):
         got.append(swap(msg, "ctx", (2 << bit) - 1))
-        if bit < ctx_bits - 1:
-            last_shape = shape((heads * dh, dh), bf16)
-            out = msg_shape if bit < ctx_bits - 2 else last_shape
-            msg = call(functools.partial(join_kernel, heads, bit), out, msg, got[-1])
-    inside, slots, weight_near, q_near, growth = call(
+        if bit == 0:
+            msg, weight_early = lax.optimization_barrier((msg, weight_early))
+        outs = msg_shape if bit < ctx_bits - 2 else shape((heads * dh, dh), bf16)
+        msg = call(functools.partial(join_kernel, heads, bit), outs, msg, got[-1])
+    if ctx_bits == 2:
+        asked = hop(q, "ctx", functools.partial(between, (1, 3)))
+        near = hop(msg, "ctx", functools.partial(between, (1, 2)))
+        answer = call(functools.partial(answer_kernel, heads), shape(q.shape, bf16), asked, msg)
+        latest = [near, hop(answer, "ctx", around)]
+    else:
+        latest = [swap(msg, "ctx", ctx_count - 1)]
+    inside, slots, weight_late, q_near, growth = call(
         inside_kernel,
         (
             shape((length, heads * dh), f32),
             shape((tokens, LANES), jnp.int32),
-            shape(weight.shape, bf16),
+            shape((heads * dh, width - cuts[1]), bf16),
             shape(q.shape, bf16),
             shape((length, LANES), f32),
         ),
@@ -431,10 +476,9 @@
     base, scale = call(
         functools.partial(base_kernel, heads),
         (shape((length, heads * dh), f32), shape((length, LANES), f32)),
-        q_near, inside, growth, *got[:-1],
+        q_near, inside, growth, *got,
     )
     order = [sum(((i >> b) & 1) << (exp_bits - 1 - b) for b in range(exp_bits)) for i in range(exp_count)]
-    cuts = [width * i // PARTS // LANES * LANES for i in range(PARTS + 1)]
     sections = lax.axis_size("section")
     top = exp_count // 2
 
@@ -453,12 +497,12 @@
             mixed, keep, send = call(
                 functools.partial(mix_kernel, heads, order, stop),
                 (shape((length, heads * dh), bf16), *halves),
-                q_near, base, scale, got[-1], weight_near, slots,
+                q_near, base, scale, *latest, weight_early, slots,
                 scratch=[part],
                 flops=cost,
             )
         else:
-            keep, send = call(functools.partial(project_kernel, start, stop), halves, mixed, weight_near, flops=cost)
+            keep, send = call(functools.partial(project_kernel, 0, size), halves, mixed, weight_late, flops=cost)
         for bit in range(exp_bits - 2):
             rest = keep.shape[0] // 2
             send, keep = call(

time: 35.8 us -> 35 us (0.978)
  the two profiles are of different devices: /device:TPU:0 before, /device:TPU:29 now
where the time goes in v6:
time: 35 us; the launch traced here: 34.7 us
  waiting for transfers between devices  13.9 us (40%)
  starting transfers between devices  10.1 us (29%)
  Pallas kernels  9.97 us (28%)
  between operations  0.75 us (2%)
    pallas_call x15, Pallas kernels, call(): pl.pallas_call(kernel, out_shape=out, in_specs=specs, out_specs=out_specs...  9.97 us
    ppermute x7, waiting for transfers between devices, swap(): lax.ppermute(block, axis, [(i, i ^ mask) for i in range(lax.axis_size(axi...  8.07 us
    ppermute x7, starting transfers between devices, swap(): lax.ppermute(block, axis, [(i, i ^ mask) for i in range(lax.axis_size(axi...  5.12 us
    ppermute x2, waiting for transfers between devices, relay(): lax.ppermute(block, 'section', [(i, (i + 1) % sections) for i in range(se...  3.57 us
    ppermute x2, starting transfers between devices, relay(): lax.ppermute(block, 'section', [(i, (i + 1) % sections) for i in range(se...  2.56 us
    ppermute x3, starting transfers between devices, hop(): return lax.ppermute(block, (axis, 'exp'), pairs)  2.43 us
    ppermute x3, waiting for transfers between devices, hop(): return lax.ppermute(block, (axis, 'exp'), pairs)  2.26 us
  transfers between devices with their start and end apart: 12, of which 6 were waited for; matrix products, arithmetic and copies ran while one was open for 0% of the time, Pallas kernels for 19%

profile of v6, /device:TPU:29, one launch (start us, length us, event | category | flops | bytes accessed | tf_op | source)
XLA Modules:
  0.0 34.7 jit_solution(1658536954202465861)
XLA Ops:
  0.6 1.2 %shard_map.105.own_ref = bf16[528,128]{1,0:T(8,128)(2,1)S(1)} custom-call(bf16[64,512]{1,0:T(8,128)(2,1)} %bitcast.21, bf16[64,512]{1,0:T(8,128)(2,1)} %bitcast.23, f32[4,64]{1,0:T(4,128)} %bitcast.27), custom_call_target="tpu_custom_call" | custom-call | tf_op jit(solution)/shard_map/pallas_call | solution.py:413
  1.9 0.2 collective-permute-start
  2.1 0.1 collective-permute-start.2
  2.2 1.9 %shard_map.107.rest_1_ = bf16[512,3072]{1,0:T(8,128)(2,1)S(1)} custom-call(bf16[512,6144]{1,0:T(8,128)(2,1)} %bitcast.18), custom_call_target="tpu_custom_call" | custom-call | bytes 3145728 | tf_op jit(solution)/shard_map/pallas_call | solution.py:413
  4.1 3.0 %collective-permute-done.rest_0_.got_ref = bf16[528,128]{1,0:T(8,128)(2,1)S(1)} collective-permute-done((bf16[528,128]{1,0:T(8,128)(2,1)S(1)}, bf16[528,128]{1,0:T(8,128)(2,1)S(1)}, u32[]{:S(2)}, u32[]{:S(2)}) %collective-permute-start) | collective-permute-done | bytes 135200 | tf_op jit(solution)/shard_map/ppermute | solution.py:392
  7.1 0.1 shard_map.108.state_ref
  7.2 2.3 %collective-permute-start.1 = (bf16[512,128]{1,0:T(8,128)(2,1)S(1)}, bf16[512,128]{1,0:T(8,128)(2,1)S(1)}, u32[]{:S(2)}, u32[]{:S(2)}) collective-permute-start(bf16[512,128]{1,0:T(8,128)(2,1)S(1)} %shard_map.108.state_ref), channel_id=1, source_target_pairs={{0,1},{1,0},{2,3},{3,2},{4,8},{5,9},{6,10},{7,11},{8,4},{9,5},{10,... | collective-permute-start | bytes 393224 | tf_op jit(solution)/shard_map/ppermute | solution.py:398
  9.5 0.0 collective-permute-done.2.asked_ref
  9.5 0.2 shard_map.109
  9.6 0.1 collective-permute-start.3
  9.7 2.1 %shard_map.104 = (f32[64,512]{1,0:T(8,128)S(1)}, s32[16,128]{1,0:T(8,128)S(1)}, bf16[512,3072]{1,0:T(8,128)(2,1)S(1)}, bf16[64,512]{1,0:T(8,128)(2,1)S(1)}, f32[64,128]{1,0:T(8,128)S(1)}) custom-call(bf16[64,512]{1,0:T(8,128)(2,1)} %bitcast.26, bf16[64,512]{1,0:T(8,128)(2,1)} %bitcast.22, bf16[64,512]{1,0:T(8,128)(2,1)} %bitcast.24, f32[4,64]{1,0:T(4,128)} %bitcast.28, ...), custom_call_target="tpu_custom_call" | custom-call | bytes 6291456 | tf_op jit(solution)/shard_map/pallas_call | solution.py:413
  11.8 0.2 shard_map.106
  12.0 2.3 %collective-permute-done.3.rest_0_ = bf16[64,512]{1,0:T(8,128)(2,1)S(1)} collective-permute-done((bf16[64,512]{1,0:T(8,128)(2,1)S(1)}, bf16[64,512]{1,0:T(8,128)(2,1)S(1)}, u32[]{:S(2)}, u32[]{:S(2)}) %collective-permute-start.3) | collective-permute-done | bytes 65568 | tf_op jit(solution)/shard_map/ppermute | solution.py:398
  14.3 0.0 collective-permute-done.1.state_ref
  14.3 0.0 copy-start.1
  14.3 0.8 %shard_map.110 = (bf16[64,512]{1,0:T(8,128)(2,1)S(1)}, bf16[32,3072]{1,0:T(8,128)(2,1)S(1)}, bf16[32,3200]{1,0:T(8,128)(2,1)S(1)}) custom-call(bf16[64,512]{1,0:T(8,128)(2,1)S(1)} %get-tuple-element.29.q_ref, f32[64,512]{1,0:T(8,128)S(1)} %get-tuple-element.33.base_ref, f32[64,128]{1,0:T(8,128)S(1)} %get-tuple-element.34.scale_ref, ...), custom_call_target="tpu_custom_call" | custom-call | flops 201326592 | tf_op jit(solution)/shard_map/pallas_call | solution.py:413
  15.1 0.9 %collective-permute-start.4 = (bf16[32,3200]{1,0:T(8,128)(2,1)S(1)}, bf16[32,3200]{1,0:T(8,128)(2,1)S(1)}, u32[]{:S(2)}, u32[]{:S(2)}) collective-permute-start(bf16[32,3200]{1,0:T(8,128)(2,1)S(1)} %get-tuple-element.40.sent_ref), channel_id=1, source_target_pairs={{0,1},{1,0},{2,3},{3,2},{4,5},{5,4},{6,7},{7,6},{8,9},{9,8},{10,11... | collective-permute-start | bytes 614408 | tf_op jit(solution)/shard_map/ppermute | solution.py:392
  16.0 0.0 copy-start
  16.0 0.0 copy-start.2
  16.0 0.7 %shard_map.113 = (bf16[32,3072]{1,0:T(8,128)(2,1)S(1)}, bf16[32,3072]{1,0:T(8,128)(2,1)S(1)}) custom-call(bf16[64,512]{1,0:T(8,128)(2,1)S(1)} %get-tuple-element.41.mixed_ref, bf16[512,3072]{1,0:T(8,128)(2,1)S(1)} %get-tuple-element.42.weight_ref), custom_call_target="tpu_custom_call" | custom-call | flops 201326592 | tf_op jit(solution)/shard_map/pallas_call | solution.py:413
  16.6 0.1 collective-permute-start.8
  16.7 0.3 collective-permute-done.4.got_ref
  17.0 0.0 copy-done.1
  17.0 0.1 shard_map.111.own_ref
  17.1 0.3 collective-permute-start.5
  17.4 0.7 %collective-permute-done.8.got_ref = bf16[32,3072]{1,0:T(8,128)(2,1)S(1)} collective-permute-done((bf16[32,3072]{1,0:T(8,128)(2,1)S(1)}, bf16[32,3072]{1,0:T(8,128)(2,1)S(1)}, u32[]{:S(2)}, u32[]{:S(2)}) %collective-permute-start.8) | collective-permute-done | bytes 196640 | tf_op jit(solution)/shard_map/ppermute | solution.py:392
  18.1 0.1 shard_map.114
  18.2 1.3 %collective-permute-start.9 = (bf16[32,3072]{1,0:T(8,128)(2,1)S(1)}, bf16[32,3072]{1,0:T(8,128)(2,1)S(1)}, u32[]{:S(2)}, u32[]{:S(2)}) collective-permute-start(bf16[32,3072]{1,0:T(8,128)(2,1)S(1)} %shard_map.114), channel_id=1, source_target_pairs={{0,16},{16,0},{1,17},{17,1},{2,18},{18,2},{3,19},{19,3},{4,20},{20... | collective-permute-start | bytes 589832 | tf_op jit(solution)/shard_map/ppermute | solution.py:486
  19.5 4.0 %collective-permute-done.5.got_ref = bf16[32,3200]{1,0:T(8,128)(2,1)S(1)} collective-permute-done((bf16[32,3200]{1,0:T(8,128)(2,1)S(1)}, bf16[32,3200]{1,0:T(8,128)(2,1)S(1)}, u32[]{:S(2)}, u32[]{:S(2)}) %collective-permute-start.5) | collective-permute-done | bytes 204832 | tf_op jit(solution)/shard_map/ppermute | solution.py:392
  23.5 0.1 shard_map.112
  23.6 1.3 %collective-permute-start.6 = (bf16[32,3072]{1,0:T(8,128)(2,1)S(1)}, bf16[32,3072]{1,0:T(8,128)(2,1)S(1)}, u32[]{:S(2)}, u32[]{:S(2)}) collective-permute-start(bf16[32,3072]{1,0:T(8,128)(2,1)S(1)} %shard_map.112), channel_id=1, source_target_pairs={{0,16},{16,0},{1,17},{17,1},{2,18},{18,2},{3,19},{19,3},{4,20},{20... | collective-permute-start | bytes 589832 | tf_op jit(solution)/shard_map/ppermute | solution.py:486
  24.8 0.0 collective-permute-done.9.own_ref
  24.8 0.2 collective-permute-start.10
  25.1 0.2 shard_map.115
  25.2 3.6 %collective-permute-done.6.refs_0_ = bf16[32,3072]{1,0:T(8,128)(2,1)S(1)} collective-permute-done((bf16[32,3072]{1,0:T(8,128)(2,1)S(1)}, bf16[32,3072]{1,0:T(8,128)(2,1)S(1)}, u32[]{:S(2)}, u32[]{:S(2)}) %collective-permute-start.6) | collective-permute-done | bytes 196640 | tf_op jit(solution)/shard_map/ppermute | solution.py:486
  28.8 2.1 %collective-permute-start.7 = (bf16[32,3072]{1,0:T(8,128)(2,1)S(1)}, bf16[32,3072]{1,0:T(8,128)(2,1)S(1)}, u32[]{:S(2)}, u32[]{:S(2)}) collective-permute-start(bf16[32,3072]{1,0:T(8,128)(2,1)S(1)} %collective-permute-done.6.refs_0_), channel_id=1, source_target_pairs={{0,1},{1,0},{2,3},{3,2},{4,5},{5,4},{6,7},{7,6},{8,9},{9,8},{10,11... | collective-permute-start | bytes 589832 | tf_op jit(solution)/shard_map/ppermute | solution.py:392
  30.9 0.0 collective-permute-done.10.got_ref
  31.0 1.3 %collective-permute-start.11 = (bf16[32,3072]{1,0:T(8,128)(2,1)S(1)}, bf16[32,3072]{1,0:T(8,128)(2,1)S(1)}, u32[]{:S(2)}, u32[]{:S(2)}) collective-permute-start(bf16[32,3072]{1,0:T(8,128)(2,1)S(1)} %shard_map.116.refs_1_), channel_id=1, source_target_pairs={{0,1},{1,0},{2,3},{3,2},{4,5},{5,4},{6,7},{7,6},{8,9},{9,8},{10,11... | collective-permute-start | bytes 589832 | tf_op jit(solution)/shard_map/ppermute | solution.py:392
  32.3 0.0 collective-permute-done.7.refs_2_.refs_0_
  32.3 0.0 copy-done
  32.3 0.0 copy-done.2
  32.3 1.2 %shard_map.117 = (bf16[4,4,4,6144]{3,2,1,0:T(4,128)(2,1)}, f32[16,128]{1,0:T(8,128)S(1)}, f32[32,128]{1,0:T(8,128)S(1)}, f32[32,16]{1,0:T(8,128)S(1)}) custom-call(bf16[32,3072]{1,0:T(8,128)(2,1)S(1)} %collective-permute-done.6.refs_0_, bf16[32,3072]{1,0:T(8,128)(2,1)S(1)} %shard_map.116.refs_1_, ...), custom_call_target="tpu_custom_call" | custom-call | tf_op jit(solution)/shard_map/pallas_call | solution.py:413
  33.5 0.0 collective-permute-done.11.refs_1_
  33.5 1.2 %shard_map.118 = (bf16[4,4,4,6144]{3,2,1,0:T(4,128)(2,1)}, bf16[4,4,4]{2,1,0:T(4,128)(2,1)}) custom-call(bf16[32,3072]{1,0:T(8,128)(2,1)S(1)} %collective-permute-done.7.refs_2_.refs_0_, bf16[32,3072]{1,0:T(8,128)(2,1)S(1)} %collective-permute-done.11.refs_1_, bf16[64,32]{1,0:T(8,128)(2,1)S(1)} %get-tuple-element.48.refs_3_.refs_2_, ...), custom_call_target="tpu_custom_call", output_to_operand_aliasing={{0}: (9, {})} | custom-call | tf_op jit(solution)/shard_map/pallas_call | solution.py:413
  (1 shorter events, 0.0 us)
Async XLA Ops:
  1.9 5.2 %collective-permute-start = (bf16[528,128]{1,0:T(8,128)(2,1)S(1)}, bf16[528,128]{1,0:T(8,128)(2,1)S(1)}, u32[]{:S(2)}, u32[]{:S(2)}) collective-permute-start(bf16[528,128]{1,0:T(8,128)(2,1)S(1)} %shard_map.105.own_ref), channel_id=1, source_target_pairs={{0,4},{4,0},{8,12},{12,8},{1,5},{5,1},{9,13},{13,9},{2,6},{6,2},{1... | collective-permute-start | bytes 405512 | tf_op jit(solution)/shard_map/ppermute | solution.py:392
  2.1 7.4 %collective-permute-start.2 = (bf16[64,512]{1,0:T(8,128)(2,1)}, bf16[64,512]{1,0:T(8,128)(2,1)S(1)}, u32[]{:S(2)}, u32[]{:S(2)}) collective-permute-start(bf16[64,512]{1,0:T(8,128)(2,1)} %bitcast.25), channel_id=1, source_target_pairs={{0,1},{1,0},{2,3},{3,2},{4,12},{5,13},{6,14},{7,15},{8,9},{9,8},{1... | collective-permute-start | bytes 196616 | tf_op jit(solution)/shard_map/ppermute | solution.py:398
  7.2 7.1 %collective-permute-start.1 = (bf16[512,128]{1,0:T(8,128)(2,1)S(1)}, bf16[512,128]{1,0:T(8,128)(2,1)S(1)}, u32[]{:S(2)}, u32[]{:S(2)}) collective-permute-start(bf16[512,128]{1,0:T(8,128)(2,1)S(1)} %shard_map.108.state_ref), channel_id=1, source_target_pairs={{0,1},{1,0},{2,3},{3,2},{4,8},{5,9},{6,10},{7,11},{8,4},{9,5},{10,... | collective-permute-start | bytes 393224 | tf_op jit(solution)/shard_map/ppermute | solution.py:398
  9.6 4.7 %collective-permute-start.3 = (bf16[64,512]{1,0:T(8,128)(2,1)S(1)}, bf16[64,512]{1,0:T(8,128)(2,1)S(1)}, u32[]{:S(2)}, u32[]{:S(2)}) collective-permute-start(bf16[64,512]{1,0:T(8,128)(2,1)S(1)} %shard_map.109), channel_id=1, source_target_pairs={{0,1},{1,0},{2,3},{3,2},{4,12},{5,13},{6,14},{7,15},{8,4},{9,5},{1... | collective-permute-start | bytes 196616 | tf_op jit(solution)/shard_map/ppermute | solution.py:398
  14.3 2.7 %copy-start.1 = (bf16[1,16,6144]{2,1,0:T(8,128)(2,1)S(1)}, bf16[1,16,6144]{2,1,0:T(8,128)(2,1)}, u32[]{:S(2)}) copy-start(bf16[1,16,6144]{2,1,0:T(8,128)(2,1)} %param.14) | copy-start | bytes 589828
  15.1 1.9 %collective-permute-start.4 = (bf16[32,3200]{1,0:T(8,128)(2,1)S(1)}, bf16[32,3200]{1,0:T(8,128)(2,1)S(1)}, u32[]{:S(2)}, u32[]{:S(2)}) collective-permute-start(bf16[32,3200]{1,0:T(8,128)(2,1)S(1)} %get-tuple-element.40.sent_ref), channel_id=1, source_target_pairs={{0,1},{1,0},{2,3},{3,2},{4,5},{5,4},{6,7},{7,6},{8,9},{9,8},{10,11... | collective-permute-start | bytes 614408 | tf_op jit(solution)/shard_map/ppermute | solution.py:392
  16.0 16.3 %copy-start = (bf16[1,6144,16]{1,2,0:T(8,128)(2,1)S(1)}, bf16[1,6144,16]{1,2,0:T(8,128)(2,1)}, u32[]{:S(2)}) copy-start(bf16[1,6144,16]{1,2,0:T(8,128)(2,1)} %param.16) | copy-start | bytes 589828
  16.0 16.3 %copy-start.2 = (f32[1,6144]{1,0:T(1,128)S(1)}, f32[1,6144]{1,0:T(1,128)}, u32[]{:S(2)}) copy-start(f32[1,6144]{1,0:T(1,128)} %refs_4_.1) | copy-start | bytes 73732
  16.6 1.5 %collective-permute-start.8 = (bf16[32,3072]{1,0:T(8,128)(2,1)S(1)}, bf16[32,3072]{1,0:T(8,128)(2,1)S(1)}, u32[]{:S(2)}, u32[]{:S(2)}) collective-permute-start(bf16[32,3072]{1,0:T(8,128)(2,1)S(1)} %get-tuple-element.44.sent_ref), channel_id=1, source_target_pairs={{0,1},{1,0},{2,3},{3,2},{4,5},{5,4},{6,7},{7,6},{8,9},{9,8},{10,11... | collective-permute-start | bytes 589832 | tf_op jit(solution)/shard_map/ppermute | solution.py:392
  17.1 6.4 %collective-permute-start.5 = (bf16[32,3200]{1,0:T(8,128)(2,1)S(1)}, bf16[32,3200]{1,0:T(8,128)(2,1)S(1)}, u32[]{:S(2)}, u32[]{:S(2)}) collective-permute-start(bf16[32,3200]{1,0:T(8,128)(2,1)S(1)} %shard_map.111.own_ref), channel_id=1, source_target_pairs={{0,2},{1,3},{2,0},{3,1},{4,6},{5,7},{6,4},{7,5},{8,10},{9,11},{10,... | collective-permute-start | bytes 614408 | tf_op jit(solution)/shard_map/ppermute | solution.py:392
  18.2 6.6 %collective-permute-start.9 = (bf16[32,3072]{1,0:T(8,128)(2,1)S(1)}, bf16[32,3072]{1,0:T(8,128)(2,1)S(1)}, u32[]{:S(2)}, u32[]{:S(2)}) collective-permute-start(bf16[32,3072]{1,0:T(8,128)(2,1)S(1)} %shard_map.114), channel_id=1, source_target_pairs={{0,16},{16,0},{1,17},{17,1},{2,18},{18,2},{3,19},{19,3},{4,20},{20... | collective-permute-start | bytes 589832 | tf_op jit(solution)/shard_map/ppermute | solution.py:486
  23.6 5.3 %collective-permute-start.6 = (bf16[32,3072]{1,0:T(8,128)(2,1)S(1)}, bf16[32,3072]{1,0:T(8,128)(2,1)S(1)}, u32[]{:S(2)}, u32[]{:S(2)}) collective-permute-start(bf16[32,3072]{1,0:T(8,128)(2,1)S(1)} %shard_map.112), channel_id=1, source_target_pairs={{0,16},{16,0},{1,17},{17,1},{2,18},{18,2},{3,19},{19,3},{4,20},{20... | collective-permute-start | bytes 589832 | tf_op jit(solution)/shard_map/ppermute | solution.py:486
  24.8 6.1 %collective-permute-start.10 = (bf16[32,3072]{1,0:T(8,128)(2,1)S(1)}, bf16[32,3072]{1,0:T(8,128)(2,1)S(1)}, u32[]{:S(2)}, u32[]{:S(2)}) collective-permute-start(bf16[32,3072]{1,0:T(8,128)(2,1)S(1)} %collective-permute-done.9.own_ref), channel_id=1, source_target_pairs={{0,2},{1,3},{2,0},{3,1},{4,6},{5,7},{6,4},{7,5},{8,10},{9,11},{10,... | collective-permute-start | bytes 589832 | tf_op jit(solution)/shard_map/ppermute | solution.py:392
  28.8 3.5 %collective-permute-start.7 = (bf16[32,3072]{1,0:T(8,128)(2,1)S(1)}, bf16[32,3072]{1,0:T(8,128)(2,1)S(1)}, u32[]{:S(2)}, u32[]{:S(2)}) collective-permute-start(bf16[32,3072]{1,0:T(8,128)(2,1)S(1)} %collective-permute-done.6.refs_0_), channel_id=1, source_target_pairs={{0,1},{1,0},{2,3},{3,2},{4,5},{5,4},{6,7},{7,6},{8,9},{9,8},{10,11... | collective-permute-start | bytes 589832 | tf_op jit(solution)/shard_map/ppermute | solution.py:392
  31.0 2.5 %collective-permute-start.11 = (bf16[32,3072]{1,0:T(8,128)(2,1)S(1)}, bf16[32,3072]{1,0:T(8,128)(2,1)S(1)}, u32[]{:S(2)}, u32[]{:S(2)}) collective-permute-start(bf16[32,3072]{1,0:T(8,128)(2,1)S(1)} %shard_map.116.refs_1_), channel_id=1, source_target_pairs={{0,1},{1,0},{2,3},{3,2},{4,5},{5,4},{6,7},{7,6},{8,9},{9,8},{10,11... | collective-permute-start | bytes 589832 | tf_op jit(solution)/shard_map/ppermute | solution.py:392

commit v7 on v6

--- a/solution.py
+++ b/solution.py
@@ -131,8 +131,9 @@
     copy.wait()
 
 
-def inside_kernel(q_hbm, k_hbm, v_hbm, decay_hbm, ids_hbm, weight_hbm, inside_ref, slots_ref, weight_ref, q_ref, growth_ref,
-                  k_ref, v_ref, decay_ref, ids_ref, sems):
+def inside_kernel(q_hbm, k_hbm, v_hbm, decay_hbm, ids_hbm, weight_hbm, *refs):
+    got_refs, refs = refs[:-12], refs[-12:]
+    base_ref, scale_ref, slots_ref, weight_ref, q_ref, inside_ref, growth_ref, k_ref, v_ref, decay_ref, ids_ref, sems = refs
     copies = fetch(
         (decay_hbm, ids_hbm, q_hbm, k_hbm, v_hbm, weight_hbm.at[:, -weight_ref.shape[1] :]),
         (decay_ref, ids_ref, q_ref, k_ref, v_ref, weight_ref),
@@ -154,6 +155,7 @@
         inside_ref[:, cols] = mm(weights, v_ref[:, cols], NN)
         growth = jnp.where(lane == h, jnp.exp(column), growth)
     growth_ref[...] = growth
+    base_kernel(heads, q_ref, inside_ref, growth_ref, *got_refs, base_ref, scale_ref)
     n = ids_ref.shape[1]
     earlier = iota((n, n), 1) < iota((n, n), 0)
     rows = [ids_ref[c : c + 1, :] for c in range(2)]
@@ -398,8 +400,8 @@
     return lax.ppermute(block, (axis, "exp"), pairs)
 
 
-def around(place, index):
-    return ({1: 3, 3: 2, 2: 1}[place], index) if place else (place, index ^ 1)
+def around(ring, place, index):
+    return (ring[(ring.index(place) + 1) % len(ring)], index) if place in ring else (place, index ^ 1)
 
 
 def between(pair, place, index):
@@ -447,36 +449,38 @@
     )
     got = []
     for bit in range(ctx_bits - 1):
-        got.append(swap(msg, "ctx", (2 << bit) - 1))
+        if ctx_bits == 2:
+            got.append(lax.ppermute(msg, "ctx", [(c, (c + 1) % ctx_count) for c in range(ctx_count)]))
+        else:
+            got.append(swap(msg, "ctx", (2 << bit) - 1))
         if bit == 0:
             msg, weight_early = lax.optimization_barrier((msg, weight_early))
         outs = msg_shape if bit < ctx_bits - 2 else shape((heads * dh, dh), bf16)
         msg = call(functools.partial(join_kernel, heads, bit), outs, msg, got[-1])
     if ctx_bits == 2:
-        asked = hop(q, "ctx", functools.partial(between, (1, 3)))
+        asked = hop(q, "ctx", functools.partial(around, (3, 1, 2)))
         near = hop(msg, "ctx", functools.partial(between, (1, 2)))
         answer = call(functools.partial(answer_kernel, heads), shape(q.shape, bf16), asked, msg)
-        latest = [near, hop(answer, "ctx", around)]
+        latest = [near, hop(answer, "ctx", functools.partial(around, (1, 3, 2)))]
     else:
         latest = [swap(msg, "ctx", ctx_count - 1)]
-    inside, slots, weight_late, q_near, growth = call(
+    base, scale, slots, weight_late, q_near = call(
         inside_kernel,
         (
             shape((length, heads * dh), f32),
+            shape((length, LANES), f32),
             shape((tokens, LANES), jnp.int32),
             shape((heads * dh, width - cuts[1]), bf16),
             shape(q.shape, bf16),
-            shape((length, LANES), f32),
         ),
-        q, k, v, decay, ids, weight,
-        specs=[HBM] * 6,
-        scratch=[part, part, small, pltpu.VMEM(ids.shape, jnp.int32), dma((6,))],
+        q, k, v, decay, ids, weight, *got,
+        specs=[HBM] * 6 + [VMEM] * len(got),
+        scratch=[
+            pltpu.VMEM((length, heads * dh), f32),
+            pltpu.VMEM((length, LANES), f32),
+            part, part, small, pltpu.VMEM(ids.shape, jnp.int32), dma((6,)),
+        ],
         moved=weight.size * 2,
-    )
-    base, scale = call(
-        functools.partial(base_kernel, heads),
-        (shape((length, heads * dh), f32), shape((length, LANES), f32)),
-        q_near, inside, growth, *got,
     )
     order = [sum(((i >> b) & 1) << (exp_bits - 1 - b) for b in range(exp_bits)) for i in range(exp_count)]
     sections = lax.axis_size("section")

time: 35 us -> 34.9 us (level)
  the two profiles are of different devices: /device:TPU:29 before, /device:TPU:25 now
where the time goes in v7:
time: 34.9 us; the launch traced here: 34.7 us
  starting transfers between devices  13.5 us (39%)
  waiting for transfers between devices  10.6 us (30%)
  Pallas kernels  9.74 us (28%)
  between operations  0.75 us (2%)
    pallas_call x14, Pallas kernels, call(): pl.pallas_call(kernel, out_shape=out, in_specs=specs, out_specs=out_specs...  9.74 us
    ppermute x6, starting transfers between devices, swap(): lax.ppermute(block, axis, [(i, i ^ mask) for i in range(lax.axis_size(axi...  7.18 us
    ppermute x6, waiting for transfers between devices, swap(): lax.ppermute(block, axis, [(i, i ^ mask) for i in range(lax.axis_size(axi...  4.03 us
    ppermute x3, starting transfers between devices, hop(): return lax.ppermute(block, (axis, 'exp'), pairs)  3.72 us
    ppermute x3, waiting for transfers between devices, hop(): return lax.ppermute(block, (axis, 'exp'), pairs)  2.87 us
    ppermute x2, waiting for transfers between devices, relay(): lax.ppermute(block, 'section', [(i, (i + 1) % sections) for i in range(se...  2.56 us
    ppermute x2, starting transfers between devices, relay(): lax.ppermute(block, 'section', [(i, (i + 1) % sections) for i in range(se...  2.55 us
    ppermute x1, waiting for transfers between devices, on_device(): lax.ppermute(msg, 'ctx', [(c, (c + 1) % ctx_count) for c in range(ctx_cou...  1.19 us
  transfers between devices with their start and end apart: 12, of which 5 were waited for; matrix products, arithmetic and copies ran while one was open for 0% of the time, Pallas kernels for 19%

profile of v7, /device:TPU:25, one launch (start us, length us, event | category | flops | bytes accessed | tf_op | source)
XLA Modules:
  0.0 34.7 jit_solution(9912733782678953956)
XLA Ops:
  0.6 1.2 %shard_map.104.own_ref = bf16[528,128]{1,0:T(8,128)(2,1)S(1)} custom-call(bf16[64,512]{1,0:T(8,128)(2,1)} %bitcast.21, bf16[64,512]{1,0:T(8,128)(2,1)} %bitcast.23, f32[4,64]{1,0:T(4,128)} %bitcast.27), custom_call_target="tpu_custom_call" | custom-call | tf_op jit(solution)/shard_map/pallas_call | solution.py:415
  1.9 0.1 collective-permute-start
  1.9 1.3 %collective-permute-start.2 = (bf16[64,512]{1,0:T(8,128)(2,1)}, bf16[64,512]{1,0:T(8,128)(2,1)S(1)}, u32[]{:S(2)}, u32[]{:S(2)}) collective-permute-start(bf16[64,512]{1,0:T(8,128)(2,1)} %bitcast.25), channel_id=1, source_target_pairs={{0,1},{1,0},{2,3},{3,2},{4,8},{5,9},{6,10},{7,11},{8,12},{9,13},{1... | collective-permute-start | bytes 196616 | tf_op jit(solution)/shard_map/ppermute | solution.py:400
  3.3 1.9 %shard_map.106.rest_1_ = bf16[512,3072]{1,0:T(8,128)(2,1)S(1)} custom-call(bf16[512,6144]{1,0:T(8,128)(2,1)} %bitcast.18), custom_call_target="tpu_custom_call" | custom-call | bytes 3145728 | tf_op jit(solution)/shard_map/pallas_call | solution.py:415
  5.2 1.2 %collective-permute-done.refs_0_.got_ref = bf16[528,128]{1,0:T(8,128)(2,1)S(1)} collective-permute-done((bf16[528,128]{1,0:T(8,128)(2,1)S(1)}, bf16[528,128]{1,0:T(8,128)(2,1)S(1)}, u32[]{:S(2)}, u32[]{:S(2)}) %collective-permute-start) | collective-permute-done | bytes 135200 | tf_op jit(solution)/shard_map/ppermute | solution.py:453
  6.4 0.1 shard_map.107.state_ref
  6.4 2.3 %collective-permute-start.1 = (bf16[512,128]{1,0:T(8,128)(2,1)S(1)}, bf16[512,128]{1,0:T(8,128)(2,1)S(1)}, u32[]{:S(2)}, u32[]{:S(2)}) collective-permute-start(bf16[512,128]{1,0:T(8,128)(2,1)S(1)} %shard_map.107.state_ref), channel_id=1, source_target_pairs={{0,1},{1,0},{2,3},{3,2},{4,8},{5,9},{6,10},{7,11},{8,4},{9,5},{10,... | collective-permute-start | bytes 393224 | tf_op jit(solution)/shard_map/ppermute | solution.py:400
  8.8 0.0 collective-permute-done.2.asked_ref
  8.8 0.1 shard_map.108
  8.9 0.1 collective-permute-start.3
  9.0 2.1 %shard_map.105 = (f32[64,512]{1,0:T(8,128)S(1)}, f32[64,128]{1,0:T(8,128)S(1)}, s32[16,128]{1,0:T(8,128)S(1)}, bf16[512,3072]{1,0:T(8,128)(2,1)S(1)}, bf16[64,512]{1,0:T(8,128)(2,1)S(1)}) custom-call(bf16[64,512]{1,0:T(8,128)(2,1)} %bitcast.26, bf16[64,512]{1,0:T(8,128)(2,1)} %bitcast.22, bf16[64,512]{1,0:T(8,128)(2,1)} %bitcast.24, f32[4,64]{1,0:T(4,128)} %bitcast.28, ...), custom_call_target="tpu_custom_call" | custom-call | bytes 6291456 | tf_op jit(solution)/shard_map/pallas_call | solution.py:415
  11.1 2.9 %collective-permute-done.3.rest_0_ = bf16[64,512]{1,0:T(8,128)(2,1)S(1)} collective-permute-done((bf16[64,512]{1,0:T(8,128)(2,1)S(1)}, bf16[64,512]{1,0:T(8,128)(2,1)S(1)}, u32[]{:S(2)}, u32[]{:S(2)}) %collective-permute-start.3) | collective-permute-done | bytes 65568 | tf_op jit(solution)/shard_map/ppermute | solution.py:400
  13.9 0.0 collective-permute-done.1.state_ref
  13.9 0.0 copy-start.1
  14.0 0.8 %shard_map.109 = (bf16[64,512]{1,0:T(8,128)(2,1)S(1)}, bf16[32,3072]{1,0:T(8,128)(2,1)S(1)}, bf16[32,3200]{1,0:T(8,128)(2,1)S(1)}) custom-call(bf16[64,512]{1,0:T(8,128)(2,1)S(1)} %get-tuple-element.28.q_ref, f32[64,512]{1,0:T(8,128)S(1)} %get-tuple-element.29.base_ref, f32[64,128]{1,0:T(8,128)S(1)} %get-tuple-element.30.scale_ref, ...), custom_call_target="tpu_custom_call" | custom-call | flops 201326592 | tf_op jit(solution)/shard_map/pallas_call | solution.py:415
  14.7 1.1 %collective-permute-start.4 = (bf16[32,3200]{1,0:T(8,128)(2,1)S(1)}, bf16[32,3200]{1,0:T(8,128)(2,1)S(1)}, u32[]{:S(2)}, u32[]{:S(2)}) collective-permute-start(bf16[32,3200]{1,0:T(8,128)(2,1)S(1)} %get-tuple-element.36.sent_ref), channel_id=1, source_target_pairs={{0,1},{1,0},{2,3},{3,2},{4,5},{5,4},{6,7},{7,6},{8,9},{9,8},{10,11... | collective-permute-start | bytes 614408 | tf_op jit(solution)/shard_map/ppermute | solution.py:394
  15.9 0.0 copy-start
  15.9 0.0 copy-start.2
  15.9 0.7 %shard_map.112 = (bf16[32,3072]{1,0:T(8,128)(2,1)S(1)}, bf16[32,3072]{1,0:T(8,128)(2,1)S(1)}) custom-call(bf16[64,512]{1,0:T(8,128)(2,1)S(1)} %get-tuple-element.37.mixed_ref, bf16[512,3072]{1,0:T(8,128)(2,1)S(1)} %get-tuple-element.38.weight_ref), custom_call_target="tpu_custom_call" | custom-call | flops 201326592 | tf_op jit(solution)/shard_map/pallas_call | solution.py:415
  16.5 0.1 collective-permute-start.8
  16.6 0.3 collective-permute-done.4.got_ref
  17.0 0.0 copy-done.1
  17.0 0.1 shard_map.110.own_ref
  17.1 1.3 %collective-permute-start.5 = (bf16[32,3200]{1,0:T(8,128)(2,1)S(1)}, bf16[32,3200]{1,0:T(8,128)(2,1)S(1)}, u32[]{:S(2)}, u32[]{:S(2)}) collective-permute-start(bf16[32,3200]{1,0:T(8,128)(2,1)S(1)} %shard_map.110.own_ref), channel_id=1, source_target_pairs={{0,2},{1,3},{2,0},{3,1},{4,6},{5,7},{6,4},{7,5},{8,10},{9,11},{10,... | collective-permute-start | bytes 614408 | tf_op jit(solution)/shard_map/ppermute | solution.py:394
  18.4 0.0 collective-permute-done.8.got_ref
  18.4 0.1 shard_map.113
  18.4 1.3 %collective-permute-start.9 = (bf16[32,3072]{1,0:T(8,128)(2,1)S(1)}, bf16[32,3072]{1,0:T(8,128)(2,1)S(1)}, u32[]{:S(2)}, u32[]{:S(2)}) collective-permute-start(bf16[32,3072]{1,0:T(8,128)(2,1)S(1)} %shard_map.113), channel_id=1, source_target_pairs={{0,16},{16,0},{1,17},{17,1},{2,18},{18,2},{3,19},{19,3},{4,20},{20... | collective-permute-start | bytes 589832 | tf_op jit(solution)/shard_map/ppermute | solution.py:490
  19.7 3.7 %collective-permute-done.5.got_ref = bf16[32,3200]{1,0:T(8,128)(2,1)S(1)} collective-permute-done((bf16[32,3200]{1,0:T(8,128)(2,1)S(1)}, bf16[32,3200]{1,0:T(8,128)(2,1)S(1)}, u32[]{:S(2)}, u32[]{:S(2)}) %collective-permute-start.5) | collective-permute-done | bytes 204832 | tf_op jit(solution)/shard_map/ppermute | solution.py:394
  23.4 0.1 shard_map.111
  23.5 1.3 %collective-permute-start.6 = (bf16[32,3072]{1,0:T(8,128)(2,1)S(1)}, bf16[32,3072]{1,0:T(8,128)(2,1)S(1)}, u32[]{:S(2)}, u32[]{:S(2)}) collective-permute-start(bf16[32,3072]{1,0:T(8,128)(2,1)S(1)} %shard_map.111), channel_id=1, source_target_pairs={{0,16},{16,0},{1,17},{17,1},{2,18},{18,2},{3,19},{19,3},{4,20},{20... | collective-permute-start | bytes 589832 | tf_op jit(solution)/shard_map/ppermute | solution.py:490
  24.8 0.0 collective-permute-done.9.own_ref
  24.8 1.2 %collective-permute-start.10 = (bf16[32,3072]{1,0:T(8,128)(2,1)S(1)}, bf16[32,3072]{1,0:T(8,128)(2,1)S(1)}, u32[]{:S(2)}, u32[]{:S(2)}) collective-permute-start(bf16[32,3072]{1,0:T(8,128)(2,1)S(1)} %collective-permute-done.9.own_ref), channel_id=1, source_target_pairs={{0,2},{1,3},{2,0},{3,1},{4,6},{5,7},{6,4},{7,5},{8,10},{9,11},{10,... | collective-permute-start | bytes 589832 | tf_op jit(solution)/shard_map/ppermute | solution.py:394
  26.0 0.2 shard_map.114
  26.2 2.6 %collective-permute-done.6.refs_0_ = bf16[32,3072]{1,0:T(8,128)(2,1)S(1)} collective-permute-done((bf16[32,3072]{1,0:T(8,128)(2,1)S(1)}, bf16[32,3072]{1,0:T(8,128)(2,1)S(1)}, u32[]{:S(2)}, u32[]{:S(2)}) %collective-permute-start.6) | collective-permute-done | bytes 196640 | tf_op jit(solution)/shard_map/ppermute | solution.py:490
  28.7 2.1 %collective-permute-start.7 = (bf16[32,3072]{1,0:T(8,128)(2,1)S(1)}, bf16[32,3072]{1,0:T(8,128)(2,1)S(1)}, u32[]{:S(2)}, u32[]{:S(2)}) collective-permute-start(bf16[32,3072]{1,0:T(8,128)(2,1)S(1)} %collective-permute-done.6.refs_0_), channel_id=1, source_target_pairs={{0,1},{1,0},{2,3},{3,2},{4,5},{5,4},{6,7},{7,6},{8,9},{9,8},{10,11... | collective-permute-start | bytes 589832 | tf_op jit(solution)/shard_map/ppermute | solution.py:394
  30.9 0.0 collective-permute-done.10.got_ref
  30.9 1.3 %collective-permute-start.11 = (bf16[32,3072]{1,0:T(8,128)(2,1)S(1)}, bf16[32,3072]{1,0:T(8,128)(2,1)S(1)}, u32[]{:S(2)}, u32[]{:S(2)}) collective-permute-start(bf16[32,3072]{1,0:T(8,128)(2,1)S(1)} %shard_map.115.refs_1_), channel_id=1, source_target_pairs={{0,1},{1,0},{2,3},{3,2},{4,5},{5,4},{6,7},{7,6},{8,9},{9,8},{10,11... | collective-permute-start | bytes 589832 | tf_op jit(solution)/shard_map/ppermute | solution.py:394
  32.2 0.0 collective-permute-done.7.refs_2_.refs_0_
  32.2 0.0 copy-done
  32.2 0.0 copy-done.2
  32.2 1.2 %shard_map.116 = (bf16[4,4,4,6144]{3,2,1,0:T(4,128)(2,1)}, f32[16,128]{1,0:T(8,128)S(1)}, f32[32,128]{1,0:T(8,128)S(1)}, f32[32,16]{1,0:T(8,128)S(1)}) custom-call(bf16[32,3072]{1,0:T(8,128)(2,1)S(1)} %collective-permute-done.6.refs_0_, bf16[32,3072]{1,0:T(8,128)(2,1)S(1)} %shard_map.115.refs_1_, ...), custom_call_target="tpu_custom_call" | custom-call | tf_op jit(solution)/shard_map/pallas_call | solution.py:415
  33.4 0.0 collective-permute-done.11.refs_1_
  33.4 1.2 %shard_map.117 = (bf16[4,4,4,6144]{3,2,1,0:T(4,128)(2,1)}, bf16[4,4,4]{2,1,0:T(4,128)(2,1)}) custom-call(bf16[32,3072]{1,0:T(8,128)(2,1)S(1)} %collective-permute-done.7.refs_2_.refs_0_, bf16[32,3072]{1,0:T(8,128)(2,1)S(1)} %collective-permute-done.11.refs_1_, bf16[64,32]{1,0:T(8,128)(2,1)S(1)} %get-tuple-element.44.refs_3_.refs_2_, ...), custom_call_target="tpu_custom_call", output_to_operand_aliasing={{0}: (9, {})} | custom-call | tf_op jit(solution)/shard_map/pallas_call | solution.py:415
  (1 shorter events, 0.0 us)
Async XLA Ops:
  1.9 4.5 %collective-permute-start = (bf16[528,128]{1,0:T(8,128)(2,1)S(1)}, bf16[528,128]{1,0:T(8,128)(2,1)S(1)}, u32[]{:S(2)}, u32[]{:S(2)}) collective-permute-start(bf16[528,128]{1,0:T(8,128)(2,1)S(1)} %shard_map.104.own_ref), channel_id=1, source_target_pairs={{0,4},{4,8},{8,12},{12,0},{1,5},{5,9},{9,13},{13,1},{2,6},{6,10},{... | collective-permute-start | bytes 405512 | tf_op jit(solution)/shard_map/ppermute | solution.py:453
  1.9 6.8 %collective-permute-start.2 = (bf16[64,512]{1,0:T(8,128)(2,1)}, bf16[64,512]{1,0:T(8,128)(2,1)S(1)}, u32[]{:S(2)}, u32[]{:S(2)}) collective-permute-start(bf16[64,512]{1,0:T(8,128)(2,1)} %bitcast.25), channel_id=1, source_target_pairs={{0,1},{1,0},{2,3},{3,2},{4,8},{5,9},{6,10},{7,11},{8,12},{9,13},{1... | collective-permute-start | bytes 196616 | tf_op jit(solution)/shard_map/ppermute | solution.py:400
  6.4 7.5 %collective-permute-start.1 = (bf16[512,128]{1,0:T(8,128)(2,1)S(1)}, bf16[512,128]{1,0:T(8,128)(2,1)S(1)}, u32[]{:S(2)}, u32[]{:S(2)}) collective-permute-start(bf16[512,128]{1,0:T(8,128)(2,1)S(1)} %shard_map.107.state_ref), channel_id=1, source_target_pairs={{0,1},{1,0},{2,3},{3,2},{4,8},{5,9},{6,10},{7,11},{8,4},{9,5},{10,... | collective-permute-start | bytes 393224 | tf_op jit(solution)/shard_map/ppermute | solution.py:400
  8.9 5.0 %collective-permute-start.3 = (bf16[64,512]{1,0:T(8,128)(2,1)S(1)}, bf16[64,512]{1,0:T(8,128)(2,1)S(1)}, u32[]{:S(2)}, u32[]{:S(2)}) collective-permute-start(bf16[64,512]{1,0:T(8,128)(2,1)S(1)} %shard_map.108), channel_id=1, source_target_pairs={{0,1},{1,0},{2,3},{3,2},{4,12},{5,13},{6,14},{7,15},{8,4},{9,5},{1... | collective-permute-start | bytes 196616 | tf_op jit(solution)/shard_map/ppermute | solution.py:400
  13.9 3.0 %copy-start.1 = (bf16[1,16,6144]{2,1,0:T(8,128)(2,1)S(1)}, bf16[1,16,6144]{2,1,0:T(8,128)(2,1)}, u32[]{:S(2)}) copy-start(bf16[1,16,6144]{2,1,0:T(8,128)(2,1)} %param.14) | copy-start | bytes 589828
  14.7 2.2 %collective-permute-start.4 = (bf16[32,3200]{1,0:T(8,128)(2,1)S(1)}, bf16[32,3200]{1,0:T(8,128)(2,1)S(1)}, u32[]{:S(2)}, u32[]{:S(2)}) collective-permute-start(bf16[32,3200]{1,0:T(8,128)(2,1)S(1)} %get-tuple-element.36.sent_ref), channel_id=1, source_target_pairs={{0,1},{1,0},{2,3},{3,2},{4,5},{5,4},{6,7},{7,6},{8,9},{9,8},{10,11... | collective-permute-start | bytes 614408 | tf_op jit(solution)/shard_map/ppermute | solution.py:394
  15.9 16.3 %copy-start = (bf16[1,6144,16]{1,2,0:T(8,128)(2,1)S(1)}, bf16[1,6144,16]{1,2,0:T(8,128)(2,1)}, u32[]{:S(2)}) copy-start(bf16[1,6144,16]{1,2,0:T(8,128)(2,1)} %param.16) | copy-start | bytes 589828
  15.9 16.3 %copy-start.2 = (f32[1,6144]{1,0:T(1,128)S(1)}, f32[1,6144]{1,0:T(1,128)}, u32[]{:S(2)}) copy-start(f32[1,6144]{1,0:T(1,128)} %refs_4_.1) | copy-start | bytes 73732
  16.5 1.8 %collective-permute-start.8 = (bf16[32,3072]{1,0:T(8,128)(2,1)S(1)}, bf16[32,3072]{1,0:T(8,128)(2,1)S(1)}, u32[]{:S(2)}, u32[]{:S(2)}) collective-permute-start(bf16[32,3072]{1,0:T(8,128)(2,1)S(1)} %get-tuple-element.40.sent_ref), channel_id=1, source_target_pairs={{0,1},{1,0},{2,3},{3,2},{4,5},{5,4},{6,7},{7,6},{8,9},{9,8},{10,11... | collective-permute-start | bytes 589832 | tf_op jit(solution)/shard_map/ppermute | solution.py:394
  17.1 6.4 %collective-permute-start.5 = (bf16[32,3200]{1,0:T(8,128)(2,1)S(1)}, bf16[32,3200]{1,0:T(8,128)(2,1)S(1)}, u32[]{:S(2)}, u32[]{:S(2)}) collective-permute-start(bf16[32,3200]{1,0:T(8,128)(2,1)S(1)} %shard_map.110.own_ref), channel_id=1, source_target_pairs={{0,2},{1,3},{2,0},{3,1},{4,6},{5,7},{6,4},{7,5},{8,10},{9,11},{10,... | collective-permute-start | bytes 614408 | tf_op jit(solution)/shard_map/ppermute | solution.py:394
  18.4 6.3 %collective-permute-start.9 = (bf16[32,3072]{1,0:T(8,128)(2,1)S(1)}, bf16[32,3072]{1,0:T(8,128)(2,1)S(1)}, u32[]{:S(2)}, u32[]{:S(2)}) collective-permute-start(bf16[32,3072]{1,0:T(8,128)(2,1)S(1)} %shard_map.113), channel_id=1, source_target_pairs={{0,16},{16,0},{1,17},{17,1},{2,18},{18,2},{3,19},{19,3},{4,20},{20... | collective-permute-start | bytes 589832 | tf_op jit(solution)/shard_map/ppermute | solution.py:490
  23.5 5.3 %collective-permute-start.6 = (bf16[32,3072]{1,0:T(8,128)(2,1)S(1)}, bf16[32,3072]{1,0:T(8,128)(2,1)S(1)}, u32[]{:S(2)}, u32[]{:S(2)}) collective-permute-start(bf16[32,3072]{1,0:T(8,128)(2,1)S(1)} %shard_map.111), channel_id=1, source_target_pairs={{0,16},{16,0},{1,17},{17,1},{2,18},{18,2},{3,19},{19,3},{4,20},{20... | collective-permute-start | bytes 589832 | tf_op jit(solution)/shard_map/ppermute | solution.py:490
  24.8 6.1 %collective-permute-start.10 = (bf16[32,3072]{1,0:T(8,128)(2,1)S(1)}, bf16[32,3072]{1,0:T(8,128)(2,1)S(1)}, u32[]{:S(2)}, u32[]{:S(2)}) collective-permute-start(bf16[32,3072]{1,0:T(8,128)(2,1)S(1)} %collective-permute-done.9.own_ref), channel_id=1, source_target_pairs={{0,2},{1,3},{2,0},{3,1},{4,6},{5,7},{6,4},{7,5},{8,10},{9,11},{10,... | collective-permute-start | bytes 589832 | tf_op jit(solution)/shard_map/ppermute | solution.py:394
  28.7 3.5 %collective-permute-start.7 = (bf16[32,3072]{1,0:T(8,128)(2,1)S(1)}, bf16[32,3072]{1,0:T(8,128)(2,1)S(1)}, u32[]{:S(2)}, u32[]{:S(2)}) collective-permute-start(bf16[32,3072]{1,0:T(8,128)(2,1)S(1)} %collective-permute-done.6.refs_0_), channel_id=1, source_target_pairs={{0,1},{1,0},{2,3},{3,2},{4,5},{5,4},{6,7},{7,6},{8,9},{9,8},{10,11... | collective-permute-start | bytes 589832 | tf_op jit(solution)/shard_map/ppermute | solution.py:394
  30.9 2.5 %collective-permute-start.11 = (bf16[32,3072]{1,0:T(8,128)(2,1)S(1)}, bf16[32,3072]{1,0:T(8,128)(2,1)S(1)}, u32[]{:S(2)}, u32[]{:S(2)}) collective-permute-start(bf16[32,3072]{1,0:T(8,128)(2,1)S(1)} %shard_map.115.refs_1_), channel_id=1, source_target_pairs={{0,1},{1,0},{2,3},{3,2},{4,5},{5,4},{6,7},{7,6},{8,9},{9,8},{10,11... | collective-permute-start | bytes 589832 | tf_op jit(solution)/shard_map/ppermute | solution.py:394

commit v8 on v7

--- a/solution.py
+++ b/solution.py
@@ -125,17 +125,10 @@
     return mm(a, high, NN) + mm(a, low, NN)
 
 
-def weight_kernel(weight_hbm, out_ref, sem):
-    copy = pltpu.make_async_copy(weight_hbm.at[:, : out_ref.shape[1]], out_ref, sem)
-    copy.start()
-    copy.wait()
-
-
 def inside_kernel(q_hbm, k_hbm, v_hbm, decay_hbm, ids_hbm, weight_hbm, *refs):
-    got_refs, refs = refs[:-12], refs[-12:]
-    base_ref, scale_ref, slots_ref, weight_ref, q_ref, inside_ref, growth_ref, k_ref, v_ref, decay_ref, ids_ref, sems = refs
+    inside_ref, growth_ref, slots_ref, weight_ref, q_ref, k_ref, v_ref, decay_ref, ids_ref, sems = refs
     copies = fetch(
-        (decay_hbm, ids_hbm, q_hbm, k_hbm, v_hbm, weight_hbm.at[:, -weight_ref.shape[1] :]),
+        (decay_hbm, ids_hbm, q_hbm, k_hbm, v_hbm, weight_hbm.at[:, : weight_ref.shape[1]]),
         (decay_ref, ids_ref, q_ref, k_ref, v_ref, weight_ref),
         sems,
     )
@@ -155,7 +148,6 @@
         inside_ref[:, cols] = mm(weights, v_ref[:, cols], NN)
         growth = jnp.where(lane == h, jnp.exp(column), growth)
     growth_ref[...] = growth
-    base_kernel(heads, q_ref, inside_ref, growth_ref, *got_refs, base_ref, scale_ref)
     n = ids_ref.shape[1]
     earlier = iota((n, n), 1) < iota((n, n), 0)
     rows = [ids_ref[c : c + 1, :] for c in range(2)]
@@ -169,6 +161,14 @@
     lane = iota((n, LANES), 1)
     slots_ref[...] = jnp.where(lane == 0, places[0], jnp.where(lane == 1, places[1], 0))
     copies[-1].wait()
+
+
+def late_kernel(heads, weight_hbm, *refs):
+    *refs, weight_ref, sem = refs
+    copy = pltpu.make_async_copy(weight_hbm.at[:, -weight_ref.shape[1] :], weight_ref, sem)
+    copy.start()
+    base_kernel(heads, *refs)
+    copy.wait()
 
 
 def base_kernel(heads, q_ref, inside_ref, growth_ref, *rest):
@@ -443,9 +443,20 @@
     dma = pltpu.SemaphoreType.DMA
     msg = call(state_kernel, msg_shape, k, v, decay, specs=[HBM] * 3, scratch=[part, part, small, dma((3,))])
     cuts = [width * i // PARTS // LANES * LANES for i in range(PARTS + 1)]
-    weight_after, msg = lax.optimization_barrier((weight, msg))
-    weight_early = call(
-        weight_kernel, shape((heads * dh, cuts[1]), bf16), weight_after, specs=[HBM], scratch=[dma], moved=weight.size
+    decay_after, msg = lax.optimization_barrier((decay, msg))
+    inside, growth, slots, weight_early, q_near = call(
+        inside_kernel,
+        (
+            shape((length, heads * dh), f32),
+            shape((length, LANES), f32),
+            shape((tokens, LANES), jnp.int32),
+            shape((heads * dh, cuts[1]), bf16),
+            shape(q.shape, bf16),
+        ),
+        q, k, v, decay_after, ids, weight,
+        specs=[HBM] * 6,
+        scratch=[part, part, small, pltpu.VMEM(ids.shape, jnp.int32), dma((6,))],
+        moved=weight.size,
     )
     got = []
     for bit in range(ctx_bits - 1):
@@ -464,23 +475,17 @@
         latest = [near, hop(answer, "ctx", functools.partial(around, (1, 3, 2)))]
     else:
         latest = [swap(msg, "ctx", ctx_count - 1)]
-    base, scale, slots, weight_late, q_near = call(
-        inside_kernel,
+    base, scale, weight_late = call(
+        functools.partial(late_kernel, heads),
         (
             shape((length, heads * dh), f32),
             shape((length, LANES), f32),
-            shape((tokens, LANES), jnp.int32),
             shape((heads * dh, width - cuts[1]), bf16),
-            shape(q.shape, bf16),
         ),
-        q, k, v, decay, ids, weight, *got,
-        specs=[HBM] * 6 + [VMEM] * len(got),
-        scratch=[
-            pltpu.VMEM((length, heads * dh), f32),
-            pltpu.VMEM((length, LANES), f32),
-            part, part, small, pltpu.VMEM(ids.shape, jnp.int32), dma((6,)),
-        ],
-        moved=weight.size * 2,
+        weight, q_near, inside, growth, *got,
+        specs=[HBM] + [VMEM] * (3 + len(got)),
+        scratch=[dma],
+        moved=weight.size,
     )
     order = [sum(((i >> b) & 1) << (exp_bits - 1 - b) for b in range(exp_bits)) for i in range(exp_count)]
     sections = lax.axis_size("section")

time: 34.9 us -> 34.9 us (level)
  the two profiles are of different devices: /device:TPU:25 before, /device:TPU:29 now
where the time goes in v8:
time: 34.9 us; the launch traced here: 34.7 us
  waiting for transfers between devices  12.6 us (36%)
  starting transfers between devices  11.5 us (33%)
  Pallas kernels  9.82 us (28%)
  between operations  0.75 us (2%)
    pallas_call x14, Pallas kernels, call(): pl.pallas_call(kernel, out_shape=out, in_specs=specs, out_specs=out_specs...  9.82 us
    ppermute x6, starting transfers between devices, swap(): lax.ppermute(block, axis, [(i, i ^ mask) for i in range(lax.axis_size(axi...  5.15 us
    ppermute x6, waiting for transfers between devices, swap(): lax.ppermute(block, axis, [(i, i ^ mask) for i in range(lax.axis_size(axi...  5.05 us
    ppermute x3, starting transfers between devices, hop(): return lax.ppermute(block, (axis, 'exp'), pairs)  3.72 us
    ppermute x2, waiting for transfers between devices, relay(): lax.ppermute(block, 'section', [(i, (i + 1) % sections) for i in range(se...  3.57 us
    ppermute x3, waiting for transfers between devices, hop(): return lax.ppermute(block, (axis, 'exp'), pairs)  2.99 us
    ppermute x2, starting transfers between devices, relay(): lax.ppermute(block, 'section', [(i, (i + 1) % sections) for i in range(se...  2.55 us
    ppermute x1, waiting for transfers between devices, on_device(): lax.ppermute(msg, 'ctx', [(c, (c + 1) % ctx_count) for c in range(ctx_cou...  1 us
  transfers between devices with their start and end apart: 12, of which 6 were waited for; matrix products, arithmetic and copies ran while one was open for 0% of the time, Pallas kernels for 19%

profile of v8, /device:TPU:29, one launch (start us, length us, event | category | flops | bytes accessed | tf_op | source)
XLA Modules:
  0.0 34.7 jit_solution(5037110003066589378)
XLA Ops:
  0.6 1.2 %shard_map.104.own_ref = bf16[528,128]{1,0:T(8,128)(2,1)S(1)} custom-call(bf16[64,512]{1,0:T(8,128)(2,1)} %bitcast.21, bf16[64,512]{1,0:T(8,128)(2,1)} %bitcast.23, f32[4,64]{1,0:T(4,128)} %bitcast.27), custom_call_target="tpu_custom_call" | custom-call | tf_op jit(solution)/shard_map/pallas_call | solution.py:415
  1.9 0.1 collective-permute-start
  1.9 1.3 %collective-permute-start.2 = (bf16[64,512]{1,0:T(8,128)(2,1)}, bf16[64,512]{1,0:T(8,128)(2,1)S(1)}, u32[]{:S(2)}, u32[]{:S(2)}) collective-permute-start(bf16[64,512]{1,0:T(8,128)(2,1)} %bitcast.25), channel_id=1, source_target_pairs={{0,1},{1,0},{2,3},{3,2},{4,8},{5,9},{6,10},{7,11},{8,12},{9,13},{1... | collective-permute-start | bytes 196616 | tf_op jit(solution)/shard_map/ppermute | solution.py:400
  3.3 2.1 %shard_map.105 = (f32[64,512]{1,0:T(8,128)S(1)}, f32[64,128]{1,0:T(8,128)S(1)}, s32[16,128]{1,0:T(8,128)S(1)}, bf16[512,3072]{1,0:T(8,128)(2,1)S(1)}, bf16[64,512]{1,0:T(8,128)(2,1)S(1)}) custom-call(bf16[64,512]{1,0:T(8,128)(2,1)} %bitcast.26, bf16[64,512]{1,0:T(8,128)(2,1)} %bitcast.22, bf16[64,512]{1,0:T(8,128)(2,1)} %bitcast.24, f32[4,64]{1,0:T(4,128)} %bitcast.28, ...), custom_call_target="tpu_custom_call" | custom-call | bytes 3145728 | tf_op jit(solution)/shard_map/pallas_call | solution.py:415
  5.4 1.0 %collective-permute-done.refs_3_.got_ref = bf16[528,128]{1,0:T(8,128)(2,1)S(1)} collective-permute-done((bf16[528,128]{1,0:T(8,128)(2,1)S(1)}, bf16[528,128]{1,0:T(8,128)(2,1)S(1)}, u32[]{:S(2)}, u32[]{:S(2)}) %collective-permute-start) | collective-permute-done | bytes 135200 | tf_op jit(solution)/shard_map/ppermute | solution.py:464
  6.4 0.1 shard_map.107.state_ref
  6.4 2.3 %collective-permute-start.1 = (bf16[512,128]{1,0:T(8,128)(2,1)S(1)}, bf16[512,128]{1,0:T(8,128)(2,1)S(1)}, u32[]{:S(2)}, u32[]{:S(2)}) collective-permute-start(bf16[512,128]{1,0:T(8,128)(2,1)S(1)} %shard_map.107.state_ref), channel_id=1, source_target_pairs={{0,1},{1,0},{2,3},{3,2},{4,8},{5,9},{6,10},{7,11},{8,4},{9,5},{10,... | collective-permute-start | bytes 393224 | tf_op jit(solution)/shard_map/ppermute | solution.py:400
  8.8 0.0 collective-permute-done.2.asked_ref
  8.8 0.1 shard_map.108
  8.9 0.1 collective-permute-start.3
  9.0 2.0 %shard_map.106 = (f32[64,512]{1,0:T(8,128)S(1)}, f32[64,128]{1,0:T(8,128)S(1)}, bf16[512,3072]{1,0:T(8,128)(2,1)S(1)}) custom-call(bf16[512,6144]{1,0:T(8,128)(2,1)} %bitcast.19, bf16[64,512]{1,0:T(8,128)(2,1)S(1)} %get-tuple-element.31.refs_0_.q_ref, f32[64,512]{1,0:T(8,128)S(1)} %get-tuple-element.32.refs_1_, f32[64,128]{1,0:T(8,128)S(1)} %get-tuple-element.33.refs_2_, ...), custom_call_target="tpu_custom_call" | custom-call | bytes 3145728 | tf_op jit(solution)/shard_map/pallas_call | solution.py:415
  11.0 3.0 %collective-permute-done.3.rest_0_ = bf16[64,512]{1,0:T(8,128)(2,1)S(1)} collective-permute-done((bf16[64,512]{1,0:T(8,128)(2,1)S(1)}, bf16[64,512]{1,0:T(8,128)(2,1)S(1)}, u32[]{:S(2)}, u32[]{:S(2)}) %collective-permute-start.3) | collective-permute-done | bytes 65568 | tf_op jit(solution)/shard_map/ppermute | solution.py:400
  13.9 0.0 collective-permute-done.1.state_ref
  14.0 0.0 copy-start.1
  14.0 0.8 %shard_map.109 = (bf16[64,512]{1,0:T(8,128)(2,1)S(1)}, bf16[32,3072]{1,0:T(8,128)(2,1)S(1)}, bf16[32,3200]{1,0:T(8,128)(2,1)S(1)}) custom-call(bf16[64,512]{1,0:T(8,128)(2,1)S(1)} %get-tuple-element.31.refs_0_.q_ref, f32[64,512]{1,0:T(8,128)S(1)} %get-tuple-element.35.base_ref, f32[64,128]{1,0:T(8,128)S(1)} %get-tuple-element.36.scale_ref, ...), custom_call_target="tpu_custom_call" | custom-call | flops 201326592 | tf_op jit(solution)/shard_map/pallas_call | solution.py:415
  14.7 1.1 %collective-permute-start.4 = (bf16[32,3200]{1,0:T(8,128)(2,1)S(1)}, bf16[32,3200]{1,0:T(8,128)(2,1)S(1)}, u32[]{:S(2)}, u32[]{:S(2)}) collective-permute-start(bf16[32,3200]{1,0:T(8,128)(2,1)S(1)} %get-tuple-element.42.sent_ref), channel_id=1, source_target_pairs={{0,1},{1,0},{2,3},{3,2},{4,5},{5,4},{6,7},{7,6},{8,9},{9,8},{10,11... | collective-permute-start | bytes 614408 | tf_op jit(solution)/shard_map/ppermute | solution.py:394
  15.9 0.0 copy-start
  15.9 0.0 copy-start.2
  15.9 0.7 %shard_map.112 = (bf16[32,3072]{1,0:T(8,128)(2,1)S(1)}, bf16[32,3072]{1,0:T(8,128)(2,1)S(1)}) custom-call(bf16[64,512]{1,0:T(8,128)(2,1)S(1)} %get-tuple-element.43.mixed_ref, bf16[512,3072]{1,0:T(8,128)(2,1)S(1)} %get-tuple-element.44.weight_ref), custom_call_target="tpu_custom_call" | custom-call | flops 201326592 | tf_op jit(solution)/shard_map/pallas_call | solution.py:415
  16.6 0.1 collective-permute-start.8
  16.7 0.3 collective-permute-done.4.got_ref
  17.0 0.0 copy-done.1
  17.0 0.1 shard_map.110.own_ref
  17.1 0.3 collective-permute-start.5
  17.4 0.7 %collective-permute-done.8.got_ref = bf16[32,3072]{1,0:T(8,128)(2,1)S(1)} collective-permute-done((bf16[32,3072]{1,0:T(8,128)(2,1)S(1)}, bf16[32,3072]{1,0:T(8,128)(2,1)S(1)}, u32[]{:S(2)}, u32[]{:S(2)}) %collective-permute-start.8) | collective-permute-done | bytes 196640 | tf_op jit(solution)/shard_map/ppermute | solution.py:394
  18.1 0.1 shard_map.113
  18.1 1.3 %collective-permute-start.9 = (bf16[32,3072]{1,0:T(8,128)(2,1)S(1)}, bf16[32,3072]{1,0:T(8,128)(2,1)S(1)}, u32[]{:S(2)}, u32[]{:S(2)}) collective-permute-start(bf16[32,3072]{1,0:T(8,128)(2,1)S(1)} %shard_map.113), channel_id=1, source_target_pairs={{0,16},{16,0},{1,17},{17,1},{2,18},{18,2},{3,19},{19,3},{4,20},{20... | collective-permute-start | bytes 589832 | tf_op jit(solution)/shard_map/ppermute | solution.py:495
  19.4 4.0 %collective-permute-done.5.got_ref = bf16[32,3200]{1,0:T(8,128)(2,1)S(1)} collective-permute-done((bf16[32,3200]{1,0:T(8,128)(2,1)S(1)}, bf16[32,3200]{1,0:T(8,128)(2,1)S(1)}, u32[]{:S(2)}, u32[]{:S(2)}) %collective-permute-start.5) | collective-permute-done | bytes 204832 | tf_op jit(solution)/shard_map/ppermute | solution.py:394
  23.4 0.1 shard_map.111
  23.5 1.3 %collective-permute-start.6 = (bf16[32,3072]{1,0:T(8,128)(2,1)S(1)}, bf16[32,3072]{1,0:T(8,128)(2,1)S(1)}, u32[]{:S(2)}, u32[]{:S(2)}) collective-permute-start(bf16[32,3072]{1,0:T(8,128)(2,1)S(1)} %shard_map.111), channel_id=1, source_target_pairs={{0,16},{16,0},{1,17},{17,1},{2,18},{18,2},{3,19},{19,3},{4,20},{20... | collective-permute-start | bytes 589832 | tf_op jit(solution)/shard_map/ppermute | solution.py:495
  24.8 0.0 collective-permute-done.9.own_ref
  24.8 0.2 collective-permute-start.10
  25.0 0.2 shard_map.114
  25.2 3.6 %collective-permute-done.6.refs_0_ = bf16[32,3072]{1,0:T(8,128)(2,1)S(1)} collective-permute-done((bf16[32,3072]{1,0:T(8,128)(2,1)S(1)}, bf16[32,3072]{1,0:T(8,128)(2,1)S(1)}, u32[]{:S(2)}, u32[]{:S(2)}) %collective-permute-start.6) | collective-permute-done | bytes 196640 | tf_op jit(solution)/shard_map/ppermute | solution.py:495
  28.7 2.1 %collective-permute-start.7 = (bf16[32,3072]{1,0:T(8,128)(2,1)S(1)}, bf16[32,3072]{1,0:T(8,128)(2,1)S(1)}, u32[]{:S(2)}, u32[]{:S(2)}) collective-permute-start(bf16[32,3072]{1,0:T(8,128)(2,1)S(1)} %collective-permute-done.6.refs_0_), channel_id=1, source_target_pairs={{0,1},{1,0},{2,3},{3,2},{4,5},{5,4},{6,7},{7,6},{8,9},{9,8},{10,11... | collective-permute-start | bytes 589832 | tf_op jit(solution)/shard_map/ppermute | solution.py:394
  30.9 0.0 collective-permute-done.10.got_ref
  30.9 1.3 %collective-permute-start.11 = (bf16[32,3072]{1,0:T(8,128)(2,1)S(1)}, bf16[32,3072]{1,0:T(8,128)(2,1)S(1)}, u32[]{:S(2)}, u32[]{:S(2)}) collective-permute-start(bf16[32,3072]{1,0:T(8,128)(2,1)S(1)} %shard_map.115.refs_1_), channel_id=1, source_target_pairs={{0,1},{1,0},{2,3},{3,2},{4,5},{5,4},{6,7},{7,6},{8,9},{9,8},{10,11... | collective-permute-start | bytes 589832 | tf_op jit(solution)/shard_map/ppermute | solution.py:394
  32.2 0.0 collective-permute-done.7.refs_2_.refs_0_
  32.2 0.0 copy-done
  32.2 0.0 copy-done.2
  32.2 1.2 %shard_map.116 = (bf16[4,4,4,6144]{3,2,1,0:T(4,128)(2,1)}, f32[16,128]{1,0:T(8,128)S(1)}, f32[32,128]{1,0:T(8,128)S(1)}, f32[32,16]{1,0:T(8,128)S(1)}) custom-call(bf16[32,3072]{1,0:T(8,128)(2,1)S(1)} %collective-permute-done.6.refs_0_, bf16[32,3072]{1,0:T(8,128)(2,1)S(1)} %shard_map.115.refs_1_, ...), custom_call_target="tpu_custom_call" | custom-call | tf_op jit(solution)/shard_map/pallas_call | solution.py:415
  33.4 0.0 collective-permute-done.11.refs_1_
  33.4 1.2 %shard_map.117 = (bf16[4,4,4,6144]{3,2,1,0:T(4,128)(2,1)}, bf16[4,4,4]{2,1,0:T(4,128)(2,1)}) custom-call(bf16[32,3072]{1,0:T(8,128)(2,1)S(1)} %collective-permute-done.7.refs_2_.refs_0_, bf16[32,3072]{1,0:T(8,128)(2,1)S(1)} %collective-permute-done.11.refs_1_, bf16[64,32]{1,0:T(8,128)(2,1)S(1)} %get-tuple-element.50.refs_3_.refs_2_, ...), custom_call_target="tpu_custom_call", output_to_operand_aliasing={{0}: (9, {})} | custom-call | tf_op jit(solution)/shard_map/pallas_call | solution.py:415
  (1 shorter events, 0.0 us)
Async XLA Ops:
  1.9 4.5 %collective-permute-start = (bf16[528,128]{1,0:T(8,128)(2,1)S(1)}, bf16[528,128]{1,0:T(8,128)(2,1)S(1)}, u32[]{:S(2)}, u32[]{:S(2)}) collective-permute-start(bf16[528,128]{1,0:T(8,128)(2,1)S(1)} %shard_map.104.own_ref), channel_id=1, source_target_pairs={{0,4},{4,8},{8,12},{12,0},{1,5},{5,9},{9,13},{13,1},{2,6},{6,10},{... | collective-permute-start | bytes 405512 | tf_op jit(solution)/shard_map/ppermute | solution.py:464
  1.9 6.8 %collective-permute-start.2 = (bf16[64,512]{1,0:T(8,128)(2,1)}, bf16[64,512]{1,0:T(8,128)(2,1)S(1)}, u32[]{:S(2)}, u32[]{:S(2)}) collective-permute-start(bf16[64,512]{1,0:T(8,128)(2,1)} %bitcast.25), channel_id=1, source_target_pairs={{0,1},{1,0},{2,3},{3,2},{4,8},{5,9},{6,10},{7,11},{8,12},{9,13},{1... | collective-permute-start | bytes 196616 | tf_op jit(solution)/shard_map/ppermute | solution.py:400
  6.4 7.5 %collective-permute-start.1 = (bf16[512,128]{1,0:T(8,128)(2,1)S(1)}, bf16[512,128]{1,0:T(8,128)(2,1)S(1)}, u32[]{:S(2)}, u32[]{:S(2)}) collective-permute-start(bf16[512,128]{1,0:T(8,128)(2,1)S(1)} %shard_map.107.state_ref), channel_id=1, source_target_pairs={{0,1},{1,0},{2,3},{3,2},{4,8},{5,9},{6,10},{7,11},{8,4},{9,5},{10,... | collective-permute-start | bytes 393224 | tf_op jit(solution)/shard_map/ppermute | solution.py:400
  8.9 5.0 %collective-permute-start.3 = (bf16[64,512]{1,0:T(8,128)(2,1)S(1)}, bf16[64,512]{1,0:T(8,128)(2,1)S(1)}, u32[]{:S(2)}, u32[]{:S(2)}) collective-permute-start(bf16[64,512]{1,0:T(8,128)(2,1)S(1)} %shard_map.108), channel_id=1, source_target_pairs={{0,1},{1,0},{2,3},{3,2},{4,12},{5,13},{6,14},{7,15},{8,4},{9,5},{1... | collective-permute-start | bytes 196616 | tf_op jit(solution)/shard_map/ppermute | solution.py:400
  14.0 3.0 %copy-start.1 = (bf16[1,16,6144]{2,1,0:T(8,128)(2,1)S(1)}, bf16[1,16,6144]{2,1,0:T(8,128)(2,1)}, u32[]{:S(2)}) copy-start(bf16[1,16,6144]{2,1,0:T(8,128)(2,1)} %param.14) | copy-start | bytes 589828
  14.7 2.2 %collective-permute-start.4 = (bf16[32,3200]{1,0:T(8,128)(2,1)S(1)}, bf16[32,3200]{1,0:T(8,128)(2,1)S(1)}, u32[]{:S(2)}, u32[]{:S(2)}) collective-permute-start(bf16[32,3200]{1,0:T(8,128)(2,1)S(1)} %get-tuple-element.42.sent_ref), channel_id=1, source_target_pairs={{0,1},{1,0},{2,3},{3,2},{4,5},{5,4},{6,7},{7,6},{8,9},{9,8},{10,11... | collective-permute-start | bytes 614408 | tf_op jit(solution)/shard_map/ppermute | solution.py:394
  15.9 16.3 %copy-start = (bf16[1,6144,16]{1,2,0:T(8,128)(2,1)S(1)}, bf16[1,6144,16]{1,2,0:T(8,128)(2,1)}, u32[]{:S(2)}) copy-start(bf16[1,6144,16]{1,2,0:T(8,128)(2,1)} %param.16) | copy-start | bytes 589828
  15.9 16.3 %copy-start.2 = (f32[1,6144]{1,0:T(1,128)S(1)}, f32[1,6144]{1,0:T(1,128)}, u32[]{:S(2)}) copy-start(f32[1,6144]{1,0:T(1,128)} %refs_4_.1) | copy-start | bytes 73732
  16.6 1.5 %collective-permute-start.8 = (bf16[32,3072]{1,0:T(8,128)(2,1)S(1)}, bf16[32,3072]{1,0:T(8,128)(2,1)S(1)}, u32[]{:S(2)}, u32[]{:S(2)}) collective-permute-start(bf16[32,3072]{1,0:T(8,128)(2,1)S(1)} %get-tuple-element.46.sent_ref), channel_id=1, source_target_pairs={{0,1},{1,0},{2,3},{3,2},{4,5},{5,4},{6,7},{7,6},{8,9},{9,8},{10,11... | collective-permute-start | bytes 589832 | tf_op jit(solution)/shard_map/ppermute | solution.py:394
  17.1 6.4 %collective-permute-start.5 = (bf16[32,3200]{1,0:T(8,128)(2,1)S(1)}, bf16[32,3200]{1,0:T(8,128)(2,1)S(1)}, u32[]{:S(2)}, u32[]{:S(2)}) collective-permute-start(bf16[32,3200]{1,0:T(8,128)(2,1)S(1)} %shard_map.110.own_ref), channel_id=1, source_target_pairs={{0,2},{1,3},{2,0},{3,1},{4,6},{5,7},{6,4},{7,5},{8,10},{9,11},{10,... | collective-permute-start | bytes 614408 | tf_op jit(solution)/shard_map/ppermute | solution.py:394
  18.1 6.6 %collective-permute-start.9 = (bf16[32,3072]{1,0:T(8,128)(2,1)S(1)}, bf16[32,3072]{1,0:T(8,128)(2,1)S(1)}, u32[]{:S(2)}, u32[]{:S(2)}) collective-permute-start(bf16[32,3072]{1,0:T(8,128)(2,1)S(1)} %shard_map.113), channel_id=1, source_target_pairs={{0,16},{16,0},{1,17},{17,1},{2,18},{18,2},{3,19},{19,3},{4,20},{20... | collective-permute-start | bytes 589832 | tf_op jit(solution)/shard_map/ppermute | solution.py:495
  23.5 5.3 %collective-permute-start.6 = (bf16[32,3072]{1,0:T(8,128)(2,1)S(1)}, bf16[32,3072]{1,0:T(8,128)(2,1)S(1)}, u32[]{:S(2)}, u32[]{:S(2)}) collective-permute-start(bf16[32,3072]{1,0:T(8,128)(2,1)S(1)} %shard_map.111), channel_id=1, source_target_pairs={{0,16},{16,0},{1,17},{17,1},{2,18},{18,2},{3,19},{19,3},{4,20},{20... | collective-permute-start | bytes 589832 | tf_op jit(solution)/shard_map/ppermute | solution.py:495
  24.8 6.1 %collective-permute-start.10 = (bf16[32,3072]{1,0:T(8,128)(2,1)S(1)}, bf16[32,3072]{1,0:T(8,128)(2,1)S(1)}, u32[]{:S(2)}, u32[]{:S(2)}) collective-permute-start(bf16[32,3072]{1,0:T(8,128)(2,1)S(1)} %collective-permute-done.9.own_ref), channel_id=1, source_target_pairs={{0,2},{1,3},{2,0},{3,1},{4,6},{5,7},{6,4},{7,5},{8,10},{9,11},{10,... | collective-permute-start | bytes 589832 | tf_op jit(solution)/shard_map/ppermute | solution.py:394
  28.7 3.5 %collective-permute-start.7 = (bf16[32,3072]{1,0:T(8,128)(2,1)S(1)}, bf16[32,3072]{1,0:T(8,128)(2,1)S(1)}, u32[]{:S(2)}, u32[]{:S(2)}) collective-permute-start(bf16[32,3072]{1,0:T(8,128)(2,1)S(1)} %collective-permute-done.6.refs_0_), channel_id=1, source_target_pairs={{0,1},{1,0},{2,3},{3,2},{4,5},{5,4},{6,7},{7,6},{8,9},{9,8},{10,11... | collective-permute-start | bytes 589832 | tf_op jit(solution)/shard_map/ppermute | solution.py:394
  30.9 2.5 %collective-permute-start.11 = (bf16[32,3072]{1,0:T(8,128)(2,1)S(1)}, bf16[32,3072]{1,0:T(8,128)(2,1)S(1)}, u32[]{:S(2)}, u32[]{:S(2)}) collective-permute-start(bf16[32,3072]{1,0:T(8,128)(2,1)S(1)} %shard_map.115.refs_1_), channel_id=1, source_target_pairs={{0,1},{1,0},{2,3},{3,2},{4,5},{5,4},{6,7},{7,6},{8,9},{9,8},{10,11... | collective-permute-start | bytes 589832 | tf_op jit(solution)/shard_map/ppermute | solution.py:394

commit v9 on v7

--- a/solution.py
+++ b/solution.py
@@ -87,10 +87,10 @@
         lasts.append(jnp.broadcast_to(last, (1, dh)))
     msg_ref[base:, :] = log_rows(lasts)
     copies[1].wait()
+    keyed = [(k_ref[:, h * dh : (h + 1) * dh].astype(f32) * tails[h]).astype(bf16) for h in range(heads)]
     copies[2].wait()
     for h in range(heads):
-        keyed = (k_ref[:, h * dh : (h + 1) * dh].astype(f32) * tails[h]).astype(bf16)
-        msg_ref[h * dh : (h + 1) * dh, :] = mm(keyed, v_ref[:, h * dh : (h + 1) * dh], TN).astype(bf16)
+        msg_ref[h * dh : (h + 1) * dh, :] = mm(keyed[h], v_ref[:, h * dh : (h + 1) * dh], TN).astype(bf16)
 
 
 def joined(heads, bit, own_ref, got_ref):

time: 34.9 us -> 34.9 us (level)
  the two profiles are of different devices: /device:TPU:25 before, /device:TPU:29 now
where the time goes in v9:
time: 34.9 us; the launch traced here: 34.7 us
  waiting for transfers between devices  12.7 us (36%)
  starting transfers between devices  11.5 us (33%)
  Pallas kernels  9.76 us (28%)
  between operations  0.75 us (2%)
    pallas_call x14, Pallas kernels, call(): pl.pallas_call(kernel, out_shape=out, in_specs=specs, out_specs=out_specs...  9.76 us
    ppermute x6, starting transfers between devices, swap(): lax.ppermute(block, axis, [(i, i ^ mask) for i in range(lax.axis_size(axi...  5.15 us
    ppermute x6, waiting for transfers between devices, swap(): lax.ppermute(block, axis, [(i, i ^ mask) for i in range(lax.axis_size(axi...  5.05 us
    ppermute x3, starting transfers between devices, hop(): return lax.ppermute(block, (axis, 'exp'), pairs)  3.72 us
    ppermute x2, waiting for transfers between devices, relay(): lax.ppermute(block, 'section', [(i, (i + 1) % sections) for i in range(se...  3.57 us
    ppermute x3, waiting for transfers between devices, hop(): return lax.ppermute(block, (axis, 'exp'), pairs)  2.87 us
    ppermute x2, starting transfers between devices, relay(): lax.ppermute(block, 'section', [(i, (i + 1) % sections) for i in range(se...  2.55 us
    ppermute x1, waiting for transfers between devices, on_device(): lax.ppermute(msg, 'ctx', [(c, (c + 1) % ctx_count) for c in range(ctx_cou...  1.2 us
  transfers between devices with their start and end apart: 12, of which 6 were waited for; matrix products, arithmetic and copies ran while one was open for 0% of the time, Pallas kernels for 19%

profile of v9, /device:TPU:29, one launch (start us, length us, event | category | flops | bytes accessed | tf_op | source)
XLA Modules:
  0.0 34.7 jit_solution(15071599167568344352)
XLA Ops:
  0.6 1.3 %shard_map.104.own_ref = bf16[528,128]{1,0:T(8,128)(2,1)S(1)} custom-call(bf16[64,512]{1,0:T(8,128)(2,1)} %bitcast.21, bf16[64,512]{1,0:T(8,128)(2,1)} %bitcast.23, f32[4,64]{1,0:T(4,128)} %bitcast.27), custom_call_target="tpu_custom_call" | custom-call | tf_op jit(solution)/shard_map/pallas_call | solution.py:415
  1.9 0.1 collective-permute-start
  2.0 1.3 %collective-permute-start.2 = (bf16[64,512]{1,0:T(8,128)(2,1)}, bf16[64,512]{1,0:T(8,128)(2,1)S(1)}, u32[]{:S(2)}, u32[]{:S(2)}) collective-permute-start(bf16[64,512]{1,0:T(8,128)(2,1)} %bitcast.25), channel_id=1, source_target_pairs={{0,1},{1,0},{2,3},{3,2},{4,8},{5,9},{6,10},{7,11},{8,12},{9,13},{1... | collective-permute-start | bytes 196616 | tf_op jit(solution)/shard_map/ppermute | solution.py:400
  3.3 1.9 %shard_map.106.rest_1_ = bf16[512,3072]{1,0:T(8,128)(2,1)S(1)} custom-call(bf16[512,6144]{1,0:T(8,128)(2,1)} %bitcast.18), custom_call_target="tpu_custom_call" | custom-call | bytes 3145728 | tf_op jit(solution)/shard_map/pallas_call | solution.py:415
  5.2 1.2 %collective-permute-done.refs_0_.got_ref = bf16[528,128]{1,0:T(8,128)(2,1)S(1)} collective-permute-done((bf16[528,128]{1,0:T(8,128)(2,1)S(1)}, bf16[528,128]{1,0:T(8,128)(2,1)S(1)}, u32[]{:S(2)}, u32[]{:S(2)}) %collective-permute-start) | collective-permute-done | bytes 135200 | tf_op jit(solution)/shard_map/ppermute | solution.py:453
  6.4 0.1 shard_map.107.state_ref
  6.5 2.3 %collective-permute-start.1 = (bf16[512,128]{1,0:T(8,128)(2,1)S(1)}, bf16[512,128]{1,0:T(8,128)(2,1)S(1)}, u32[]{:S(2)}, u32[]{:S(2)}) collective-permute-start(bf16[512,128]{1,0:T(8,128)(2,1)S(1)} %shard_map.107.state_ref), channel_id=1, source_target_pairs={{0,1},{1,0},{2,3},{3,2},{4,8},{5,9},{6,10},{7,11},{8,4},{9,5},{10,... | collective-permute-start | bytes 393224 | tf_op jit(solution)/shard_map/ppermute | solution.py:400
  8.8 0.0 collective-permute-done.2.asked_ref
  8.8 0.1 shard_map.108
  8.9 0.1 collective-permute-start.3
  9.0 2.1 %shard_map.105 = (f32[64,512]{1,0:T(8,128)S(1)}, f32[64,128]{1,0:T(8,128)S(1)}, s32[16,128]{1,0:T(8,128)S(1)}, bf16[512,3072]{1,0:T(8,128)(2,1)S(1)}, bf16[64,512]{1,0:T(8,128)(2,1)S(1)}) custom-call(bf16[64,512]{1,0:T(8,128)(2,1)} %bitcast.26, bf16[64,512]{1,0:T(8,128)(2,1)} %bitcast.22, bf16[64,512]{1,0:T(8,128)(2,1)} %bitcast.24, f32[4,64]{1,0:T(4,128)} %bitcast.28, ...), custom_call_target="tpu_custom_call" | custom-call | bytes 6291456 | tf_op jit(solution)/shard_map/pallas_call | solution.py:415
  11.1 2.9 %collective-permute-done.3.rest_0_ = bf16[64,512]{1,0:T(8,128)(2,1)S(1)} collective-permute-done((bf16[64,512]{1,0:T(8,128)(2,1)S(1)}, bf16[64,512]{1,0:T(8,128)(2,1)S(1)}, u32[]{:S(2)}, u32[]{:S(2)}) %collective-permute-start.3) | collective-permute-done | bytes 65568 | tf_op jit(solution)/shard_map/ppermute | solution.py:400
  14.0 0.0 collective-permute-done.1.state_ref
  14.0 0.0 copy-start.1
  14.0 0.8 %shard_map.109 = (bf16[64,512]{1,0:T(8,128)(2,1)S(1)}, bf16[32,3072]{1,0:T(8,128)(2,1)S(1)}, bf16[32,3200]{1,0:T(8,128)(2,1)S(1)}) custom-call(bf16[64,512]{1,0:T(8,128)(2,1)S(1)} %get-tuple-element.28.q_ref, f32[64,512]{1,0:T(8,128)S(1)} %get-tuple-element.29.base_ref, f32[64,128]{1,0:T(8,128)S(1)} %get-tuple-element.30.scale_ref, ...), custom_call_target="tpu_custom_call" | custom-call | flops 201326592 | tf_op jit(solution)/shard_map/pallas_call | solution.py:415
  14.8 1.1 %collective-permute-start.4 = (bf16[32,3200]{1,0:T(8,128)(2,1)S(1)}, bf16[32,3200]{1,0:T(8,128)(2,1)S(1)}, u32[]{:S(2)}, u32[]{:S(2)}) collective-permute-start(bf16[32,3200]{1,0:T(8,128)(2,1)S(1)} %get-tuple-element.36.sent_ref), channel_id=1, source_target_pairs={{0,1},{1,0},{2,3},{3,2},{4,5},{5,4},{6,7},{7,6},{8,9},{9,8},{10,11... | collective-permute-start | bytes 614408 | tf_op jit(solution)/shard_map/ppermute | solution.py:394
  15.9 0.0 copy-start
  15.9 0.0 copy-start.2
  15.9 0.7 %shard_map.112 = (bf16[32,3072]{1,0:T(8,128)(2,1)S(1)}, bf16[32,3072]{1,0:T(8,128)(2,1)S(1)}) custom-call(bf16[64,512]{1,0:T(8,128)(2,1)S(1)} %get-tuple-element.37.mixed_ref, bf16[512,3072]{1,0:T(8,128)(2,1)S(1)} %get-tuple-element.38.weight_ref), custom_call_target="tpu_custom_call" | custom-call | flops 201326592 | tf_op jit(solution)/shard_map/pallas_call | solution.py:415
  16.6 0.1 collective-permute-start.8
  16.7 0.3 collective-permute-done.4.got_ref
  17.0 0.0 copy-done.1
  17.0 0.1 shard_map.110.own_ref
  17.1 0.3 collective-permute-start.5
  17.4 0.7 %collective-permute-done.8.got_ref = bf16[32,3072]{1,0:T(8,128)(2,1)S(1)} collective-permute-done((bf16[32,3072]{1,0:T(8,128)(2,1)S(1)}, bf16[32,3072]{1,0:T(8,128)(2,1)S(1)}, u32[]{:S(2)}, u32[]{:S(2)}) %collective-permute-start.8) | collective-permute-done | bytes 196640 | tf_op jit(solution)/shard_map/ppermute | solution.py:394
  18.1 0.1 shard_map.113
  18.1 1.3 %collective-permute-start.9 = (bf16[32,3072]{1,0:T(8,128)(2,1)S(1)}, bf16[32,3072]{1,0:T(8,128)(2,1)S(1)}, u32[]{:S(2)}, u32[]{:S(2)}) collective-permute-start(bf16[32,3072]{1,0:T(8,128)(2,1)S(1)} %shard_map.113), channel_id=1, source_target_pairs={{0,16},{16,0},{1,17},{17,1},{2,18},{18,2},{3,19},{19,3},{4,20},{20... | collective-permute-start | bytes 589832 | tf_op jit(solution)/shard_map/ppermute | solution.py:490
  19.4 4.0 %collective-permute-done.5.got_ref = bf16[32,3200]{1,0:T(8,128)(2,1)S(1)} collective-permute-done((bf16[32,3200]{1,0:T(8,128)(2,1)S(1)}, bf16[32,3200]{1,0:T(8,128)(2,1)S(1)}, u32[]{:S(2)}, u32[]{:S(2)}) %collective-permute-start.5) | collective-permute-done | bytes 204832 | tf_op jit(solution)/shard_map/ppermute | solution.py:394
  23.4 0.1 shard_map.111
  23.5 1.3 %collective-permute-start.6 = (bf16[32,3072]{1,0:T(8,128)(2,1)S(1)}, bf16[32,3072]{1,0:T(8,128)(2,1)S(1)}, u32[]{:S(2)}, u32[]{:S(2)}) collective-permute-start(bf16[32,3072]{1,0:T(8,128)(2,1)S(1)} %shard_map.111), channel_id=1, source_target_pairs={{0,16},{16,0},{1,17},{17,1},{2,18},{18,2},{3,19},{19,3},{4,20},{20... | collective-permute-start | bytes 589832 | tf_op jit(solution)/shard_map/ppermute | solution.py:490
  24.8 0.0 collective-permute-done.9.own_ref
  24.8 0.2 collective-permute-start.10
  25.0 0.2 shard_map.114
  25.2 3.6 %collective-permute-done.6.refs_0_ = bf16[32,3072]{1,0:T(8,128)(2,1)S(1)} collective-permute-done((bf16[32,3072]{1,0:T(8,128)(2,1)S(1)}, bf16[32,3072]{1,0:T(8,128)(2,1)S(1)}, u32[]{:S(2)}, u32[]{:S(2)}) %collective-permute-start.6) | collective-permute-done | bytes 196640 | tf_op jit(solution)/shard_map/ppermute | solution.py:490
  28.8 2.1 %collective-permute-start.7 = (bf16[32,3072]{1,0:T(8,128)(2,1)S(1)}, bf16[32,3072]{1,0:T(8,128)(2,1)S(1)}, u32[]{:S(2)}, u32[]{:S(2)}) collective-permute-start(bf16[32,3072]{1,0:T(8,128)(2,1)S(1)} %collective-permute-done.6.refs_0_), channel_id=1, source_target_pairs={{0,1},{1,0},{2,3},{3,2},{4,5},{5,4},{6,7},{7,6},{8,9},{9,8},{10,11... | collective-permute-start | bytes 589832 | tf_op jit(solution)/shard_map/ppermute | solution.py:394
  30.9 0.0 collective-permute-done.10.got_ref
  30.9 1.3 %collective-permute-start.11 = (bf16[32,3072]{1,0:T(8,128)(2,1)S(1)}, bf16[32,3072]{1,0:T(8,128)(2,1)S(1)}, u32[]{:S(2)}, u32[]{:S(2)}) collective-permute-start(bf16[32,3072]{1,0:T(8,128)(2,1)S(1)} %shard_map.115.refs_1_), channel_id=1, source_target_pairs={{0,1},{1,0},{2,3},{3,2},{4,5},{5,4},{6,7},{7,6},{8,9},{9,8},{10,11... | collective-permute-start | bytes 589832 | tf_op jit(solution)/shard_map/ppermute | solution.py:394
  32.2 0.0 collective-permute-done.7.refs_2_.refs_0_
  32.2 0.0 copy-done
  32.2 0.0 copy-done.2
  32.2 1.2 %shard_map.116 = (bf16[4,4,4,6144]{3,2,1,0:T(4,128)(2,1)}, f32[16,128]{1,0:T(8,128)S(1)}, f32[32,128]{1,0:T(8,128)S(1)}, f32[32,16]{1,0:T(8,128)S(1)}) custom-call(bf16[32,3072]{1,0:T(8,128)(2,1)S(1)} %collective-permute-done.6.refs_0_, bf16[32,3072]{1,0:T(8,128)(2,1)S(1)} %shard_map.115.refs_1_, ...), custom_call_target="tpu_custom_call" | custom-call | tf_op jit(solution)/shard_map/pallas_call | solution.py:415
  33.4 0.0 collective-permute-done.11.refs_1_
  33.4 1.2 %shard_map.117 = (bf16[4,4,4,6144]{3,2,1,0:T(4,128)(2,1)}, bf16[4,4,4]{2,1,0:T(4,128)(2,1)}) custom-call(bf16[32,3072]{1,0:T(8,128)(2,1)S(1)} %collective-permute-done.7.refs_2_.refs_0_, bf16[32,3072]{1,0:T(8,128)(2,1)S(1)} %collective-permute-done.11.refs_1_, bf16[64,32]{1,0:T(8,128)(2,1)S(1)} %get-tuple-element.44.refs_3_.refs_2_, ...), custom_call_target="tpu_custom_call", output_to_operand_aliasing={{0}: (9, {})} | custom-call | tf_op jit(solution)/shard_map/pallas_call | solution.py:415
  (1 shorter events, 0.0 us)
Async XLA Ops:
  1.9 4.5 %collective-permute-start = (bf16[528,128]{1,0:T(8,128)(2,1)S(1)}, bf16[528,128]{1,0:T(8,128)(2,1)S(1)}, u32[]{:S(2)}, u32[]{:S(2)}) collective-permute-start(bf16[528,128]{1,0:T(8,128)(2,1)S(1)} %shard_map.104.own_ref), channel_id=1, source_target_pairs={{0,4},{4,8},{8,12},{12,0},{1,5},{5,9},{9,13},{13,1},{2,6},{6,10},{... | collective-permute-start | bytes 405512 | tf_op jit(solution)/shard_map/ppermute | solution.py:453
  2.0 6.8 %collective-permute-start.2 = (bf16[64,512]{1,0:T(8,128)(2,1)}, bf16[64,512]{1,0:T(8,128)(2,1)S(1)}, u32[]{:S(2)}, u32[]{:S(2)}) collective-permute-start(bf16[64,512]{1,0:T(8,128)(2,1)} %bitcast.25), channel_id=1, source_target_pairs={{0,1},{1,0},{2,3},{3,2},{4,8},{5,9},{6,10},{7,11},{8,12},{9,13},{1... | collective-permute-start | bytes 196616 | tf_op jit(solution)/shard_map/ppermute | solution.py:400
  6.5 7.5 %collective-permute-start.1 = (bf16[512,128]{1,0:T(8,128)(2,1)S(1)}, bf16[512,128]{1,0:T(8,128)(2,1)S(1)}, u32[]{:S(2)}, u32[]{:S(2)}) collective-permute-start(bf16[512,128]{1,0:T(8,128)(2,1)S(1)} %shard_map.107.state_ref), channel_id=1, source_target_pairs={{0,1},{1,0},{2,3},{3,2},{4,8},{5,9},{6,10},{7,11},{8,4},{9,5},{10,... | collective-permute-start | bytes 393224 | tf_op jit(solution)/shard_map/ppermute | solution.py:400
  8.9 5.0 %collective-permute-start.3 = (bf16[64,512]{1,0:T(8,128)(2,1)S(1)}, bf16[64,512]{1,0:T(8,128)(2,1)S(1)}, u32[]{:S(2)}, u32[]{:S(2)}) collective-permute-start(bf16[64,512]{1,0:T(8,128)(2,1)S(1)} %shard_map.108), channel_id=1, source_target_pairs={{0,1},{1,0},{2,3},{3,2},{4,12},{5,13},{6,14},{7,15},{8,4},{9,5},{1... | collective-permute-start | bytes 196616 | tf_op jit(solution)/shard_map/ppermute | solution.py:400
  14.0 3.0 %copy-start.1 = (bf16[1,16,6144]{2,1,0:T(8,128)(2,1)S(1)}, bf16[1,16,6144]{2,1,0:T(8,128)(2,1)}, u32[]{:S(2)}) copy-start(bf16[1,16,6144]{2,1,0:T(8,128)(2,1)} %param.14) | copy-start | bytes 589828
  14.8 2.2 %collective-permute-start.4 = (bf16[32,3200]{1,0:T(8,128)(2,1)S(1)}, bf16[32,3200]{1,0:T(8,128)(2,1)S(1)}, u32[]{:S(2)}, u32[]{:S(2)}) collective-permute-start(bf16[32,3200]{1,0:T(8,128)(2,1)S(1)} %get-tuple-element.36.sent_ref), channel_id=1, source_target_pairs={{0,1},{1,0},{2,3},{3,2},{4,5},{5,4},{6,7},{7,6},{8,9},{9,8},{10,11... | collective-permute-start | bytes 614408 | tf_op jit(solution)/shard_map/ppermute | solution.py:394
  15.9 16.3 %copy-start = (bf16[1,6144,16]{1,2,0:T(8,128)(2,1)S(1)}, bf16[1,6144,16]{1,2,0:T(8,128)(2,1)}, u32[]{:S(2)}) copy-start(bf16[1,6144,16]{1,2,0:T(8,128)(2,1)} %param.16) | copy-start | bytes 589828
  15.9 16.3 %copy-start.2 = (f32[1,6144]{1,0:T(1,128)S(1)}, f32[1,6144]{1,0:T(1,128)}, u32[]{:S(2)}) copy-start(f32[1,6144]{1,0:T(1,128)} %refs_4_.1) | copy-start | bytes 73732
  16.6 1.5 %collective-permute-start.8 = (bf16[32,3072]{1,0:T(8,128)(2,1)S(1)}, bf16[32,3072]{1,0:T(8,128)(2,1)S(1)}, u32[]{:S(2)}, u32[]{:S(2)}) collective-permute-start(bf16[32,3072]{1,0:T(8,128)(2,1)S(1)} %get-tuple-element.40.sent_ref), channel_id=1, source_target_pairs={{0,1},{1,0},{2,3},{3,2},{4,5},{5,4},{6,7},{7,6},{8,9},{9,8},{10,11... | collective-permute-start | bytes 589832 | tf_op jit(solution)/shard_map/ppermute | solution.py:394
  17.1 6.4 %collective-permute-start.5 = (bf16[32,3200]{1,0:T(8,128)(2,1)S(1)}, bf16[32,3200]{1,0:T(8,128)(2,1)S(1)}, u32[]{:S(2)}, u32[]{:S(2)}) collective-permute-start(bf16[32,3200]{1,0:T(8,128)(2,1)S(1)} %shard_map.110.own_ref), channel_id=1, source_target_pairs={{0,2},{1,3},{2,0},{3,1},{4,6},{5,7},{6,4},{7,5},{8,10},{9,11},{10,... | collective-permute-start | bytes 614408 | tf_op jit(solution)/shard_map/ppermute | solution.py:394
  18.1 6.6 %collective-permute-start.9 = (bf16[32,3072]{1,0:T(8,128)(2,1)S(1)}, bf16[32,3072]{1,0:T(8,128)(2,1)S(1)}, u32[]{:S(2)}, u32[]{:S(2)}) collective-permute-start(bf16[32,3072]{1,0:T(8,128)(2,1)S(1)} %shard_map.113), channel_id=1, source_target_pairs={{0,16},{16,0},{1,17},{17,1},{2,18},{18,2},{3,19},{19,3},{4,20},{20... | collective-permute-start | bytes 589832 | tf_op jit(solution)/shard_map/ppermute | solution.py:490
  23.5 5.3 %collective-permute-start.6 = (bf16[32,3072]{1,0:T(8,128)(2,1)S(1)}, bf16[32,3072]{1,0:T(8,128)(2,1)S(1)}, u32[]{:S(2)}, u32[]{:S(2)}) collective-permute-start(bf16[32,3072]{1,0:T(8,128)(2,1)S(1)} %shard_map.111), channel_id=1, source_target_pairs={{0,16},{16,0},{1,17},{17,1},{2,18},{18,2},{3,19},{19,3},{4,20},{20... | collective-permute-start | bytes 589832 | tf_op jit(solution)/shard_map/ppermute | solution.py:490
  24.8 6.1 %collective-permute-start.10 = (bf16[32,3072]{1,0:T(8,128)(2,1)S(1)}, bf16[32,3072]{1,0:T(8,128)(2,1)S(1)}, u32[]{:S(2)}, u32[]{:S(2)}) collective-permute-start(bf16[32,3072]{1,0:T(8,128)(2,1)S(1)} %collective-permute-done.9.own_ref), channel_id=1, source_target_pairs={{0,2},{1,3},{2,0},{3,1},{4,6},{5,7},{6,4},{7,5},{8,10},{9,11},{10,... | collective-permute-start | bytes 589832 | tf_op jit(solution)/shard_map/ppermute | solution.py:394
  28.8 3.5 %collective-permute-start.7 = (bf16[32,3072]{1,0:T(8,128)(2,1)S(1)}, bf16[32,3072]{1,0:T(8,128)(2,1)S(1)}, u32[]{:S(2)}, u32[]{:S(2)}) collective-permute-start(bf16[32,3072]{1,0:T(8,128)(2,1)S(1)} %collective-permute-done.6.refs_0_), channel_id=1, source_target_pairs={{0,1},{1,0},{2,3},{3,2},{4,5},{5,4},{6,7},{7,6},{8,9},{9,8},{10,11... | collective-permute-start | bytes 589832 | tf_op jit(solution)/shard_map/ppermute | solution.py:394
  30.9 2.5 %collective-permute-start.11 = (bf16[32,3072]{1,0:T(8,128)(2,1)S(1)}, bf16[32,3072]{1,0:T(8,128)(2,1)S(1)}, u32[]{:S(2)}, u32[]{:S(2)}) collective-permute-start(bf16[32,3072]{1,0:T(8,128)(2,1)S(1)} %shard_map.115.refs_1_), channel_id=1, source_target_pairs={{0,1},{1,0},{2,3},{3,2},{4,5},{5,4},{6,7},{7,6},{8,9},{9,8},{10,11... | collective-permute-start | bytes 589832 | tf_op jit(solution)/shard_map/ppermute | solution.py:394
